TPU v7x, 512 devices: a whole 4x8x8 slice. The times are simulated.
512 devices in a mesh: geo: 16 (over z, core), freq: 32 (over y, x).
Axes of the slice: x: 4, y: 8, z: 8, core: 2. Of those that a mesh axis runs over, the one named last changes fastest.
Arguments:
- adjoint_final: bfloat16 [32, 36, 64, 2048], P('freq', None, None, 'geo'), may hold values from 0.099609375 to 1
- trajectory: bfloat16 [2, 1152, 131072], P(None, None, ('geo', 'freq')), may hold values from 0.099609375 to 2
- interaction: bfloat16 [1152, 1152], replicated, may hold values from -0.1875 to 0.1875
- friction_factor: float32 [32, 131072], P(None, ('geo', 'freq')), may hold values from 0.2 to 1.6
- friction_coeff: float32 [64], replicated, may hold values from 0.25 to 2
- courant_lon: float32 [32, 36], replicated, may hold values from -0.45 to 0.45
- courant_lat: float32 [32, 36], replicated, may hold values from -0.45 to 0.45
- sea_mask: int32 [64, 2048], P(None, 'geo'), may hold values 0 or 1
- sediment: int32 [131072], P(('geo', 'freq')), may hold values from 0 to 63, as said below
Outputs:
- adjoint_initial: bfloat16 [1152, 131072], P(None, ('geo', 'freq'))
- sensitivity: float32 [64], replicated
Inputs may be any that keep to these rules, and one draw needn't show every extreme that they name: `sediment`: every group 0 .. 63 occurs.
All inputs are finite; a program needn't handle non-finite values. No bound on the sum of `sea_mask` on one device may be relied on, other than what follows from the above.
Results may differ from a plain program's by a relative error of at most 0.0057.
Values may be sent and summed in bfloat16 or wider, within the bound.
No kernel may reach another device: no remote copies, remote signals or barrier semaphores. Data moves between devices by JAX's collectives and lax.ppermute only.
A program may use at most 64 MiB of HBM per device.

v0:
```python
import jax
import jax.numpy as jnp
from jax import lax
from jax.sharding import PartitionSpec as P

SUBSTEPS = 2


step_weight = 0.25


def with_halo(shard, sides, width):
    for axis, dim in sides:
        size, length = (lax.axis_size(axis), shard.shape[dim])
        up = [(i, (i + 1) % size) for i in range(size)]
        down = [(j, i) for i, j in up]
        last = lax.slice_in_dim(shard, length - width, length, axis=dim)
        first = lax.slice_in_dim(shard, 0, width, axis=dim)
        before = lax.ppermute(last, axis, up)
        after = lax.ppermute(first, axis, down)
        shard = jnp.concatenate([before, shard, after], axis=dim)
    return shard


def stencil(center, east_side, west_side, north_row, south_row, lon_rate, lat_rate):
    lon_abs = jnp.abs(lon_rate)[:, :, None, None]
    lat_abs = jnp.abs(lat_rate)[:, :, None, None]
    lon_term = jnp.where((lon_rate > 0)[:, :, None, None], east_side, west_side)
    lat_term = jnp.where((lat_rate > 0)[:, :, None, None], north_row, south_row)
    result = (1.0 - lon_abs - lat_abs) * center + lon_abs * lon_term + lat_abs * lat_term
    return result.astype(jnp.bfloat16)


def grid_adjoint(masked, lon_rate, lat_rate):
    padded = with_halo(masked, (("geo", 3),), 1).astype(jnp.float32)
    center = padded[:, :, :, 1:-1]
    zero_row = jnp.zeros_like(center[:, :, :1, :])
    north_row = jnp.concatenate([center[:, :, 1:, :], zero_row], axis=2)
    south_row = jnp.concatenate([zero_row, center[:, :, :-1, :]], axis=2)
    return stencil(
        center, padded[:, :, :, 2:], padded[:, :, :, :-2], north_row, south_row, lon_rate, lat_rate
    )


def into_points(field):
    freq_local, directions, lat_cells, lon_cells = field.shape
    flat = field.reshape(freq_local, directions, lat_cells * lon_cells)
    moved = lax.all_to_all(flat, "freq", split_axis=2, concat_axis=0, tiled=True)
    return moved.reshape(moved.shape[0] * directions, moved.shape[2])


def into_grid(values, directions, lat_cells, lon_cells):
    split = values.reshape(values.shape[0] // directions, directions, values.shape[1])
    moved = lax.all_to_all(split, "freq", split_axis=0, concat_axis=2, tiled=True)
    return moved.reshape(moved.shape[0], directions, lat_cells, lon_cells)


def source_adjoint(adjoint, start_state, kappa_rows, coeff_point, interaction):
    freq_count = kappa_rows.shape[0]
    components, columns = adjoint.shape
    factor = jnp.broadcast_to(
        kappa_rows[:, None, :], (freq_count, components // freq_count, columns)
    ).reshape(components, columns)
    friction = factor * coeff_point[None, :]
    states = [start_state]
    substep = 0
    current = states[-1]
    squares = (current * current).astype(jnp.bfloat16)
    forced = jnp.dot(interaction, squares, preferred_element_type=jnp.float32)
    states.append(current + step_weight * (forced - friction * current))
    weights = jnp.zeros((columns,), jnp.float32)
    for substep in range(SUBSTEPS - 1, -1, -1):
        current = states[substep]
        weights = weights + jnp.sum(adjoint * factor * current, axis=0)
        pulled = lax.dot_general(
            interaction,
            adjoint.astype(jnp.bfloat16),
            (((0,), (0,)), ((), ())),
            preferred_element_type=jnp.float32,
        )
        adjoint = adjoint + step_weight * (2.0 * current * pulled - friction * adjoint)
    return (adjoint, weights)


def add_groups(total, local_sums):
    return total + lax.psum(local_sums, ("geo", "freq"))


def shards(
    adjoint_final,
    trajectory,
    interaction,
    friction_factor,
    friction_coeff,
    courant_lon,
    courant_lat,
    sea_mask,
    sediment,
):
    freq_local, directions, lat_cells, lon_cells = adjoint_final.shape
    components = interaction.shape[0]
    steps_count = trajectory.shape[0]
    columns = trajectory.shape[2]
    groups = friction_coeff.shape[0]
    freq_start = lax.axis_index("freq") * freq_local
    lon_local = lax.dynamic_slice_in_dim(courant_lon, freq_start, freq_local, 0)
    lat_local = lax.dynamic_slice_in_dim(courant_lat, freq_start, freq_local, 0)
    mask_grid = sea_mask.astype(jnp.bfloat16)[None, None]
    onehot = (sediment[:, None] == jnp.arange(groups, dtype=jnp.int32)[None, :]).astype(jnp.float32)
    coeff_point = jnp.dot(
        onehot, friction_coeff, precision=lax.Precision.HIGHEST, preferred_element_type=jnp.float32
    )
    total = jnp.zeros((groups,), jnp.float32)
    point_now = None
    grid_now = adjoint_final
    for step_index in range(steps_count - 1, -1, -1):
        if step_index < steps_count - 1:
            grid_now = into_grid(point_now, directions, lat_cells, lon_cells)
        moved = into_points(grid_adjoint(grid_now * mask_grid, lon_local, lat_local))
        adjoint_new, weights = source_adjoint(
            moved.astype(jnp.float32),
            trajectory[step_index].astype(jnp.float32),
            friction_factor,
            coeff_point,
            interaction,
        )
        local_sums = jnp.dot(
            weights, onehot, precision=lax.Precision.HIGHEST, preferred_element_type=jnp.float32
        )
        point_now, local_sums = (adjoint_new.astype(jnp.bfloat16), local_sums)
        total = add_groups(total, local_sums)
    point_total = columns * lax.axis_size("geo") * lax.axis_size("freq")
    sensitivity = total * (-step_weight * groups / (point_total * components))
    return (point_now, sensitivity)


def solution(mesh):
    in_specs = (
        P("freq", None, None, "geo"),
        P(None, None, ("geo", "freq")),
        P(),
        P(None, ("geo", "freq")),
        P(),
        P(),
        P(),
        P(None, "geo"),
        P(("geo", "freq")),
    )
    out_specs = (P(None, ("geo", "freq")), P())
    return jax.shard_map(shards, mesh=mesh, in_specs=in_specs, out_specs=out_specs, check_vma=False)
```

profile of v0, /device:TPU:1, one launch (start us, length us, event | category | flops | bytes accessed | tf_op | source)
XLA Modules:
  0.0 418.8 jit_solution(9454002583855576393)
XLA Ops:
  3.9 1.4 copy.45
  5.3 3.5 collective-permute-start
  8.8 1.4 copy.46
  10.1 3.4 collective-permute-start.1
  17.2 1.9 maximum_convert_fusion
  19.8 1.8 fusion.39
  21.6 1.6 reshape.164
  23.3 6.8 %copy.49 = bf16[1,36,8192]{1,0,2:T(2,128)(2,1)} copy(bf16[1,36,8192]{2,1,0:T(8,128)(2,1)S(1)} %reshape.164) | data formatting | bytes 1179648 | tf_op jit(solution)/shard_map/reshape | solution.py:47
  30.6 46.5 %reduce = bf16[8192,36]{1,0:T(8,128)(2,1)} reduce(bf16[8192,1,36]{2,1,0:T(2,128)(2,1)} %bitcast.145, bf16[]{:T(256)} %broadcast.68), dimensions={1}, to_apply=%bitcast.129.reduce_sub_computation | reduce | bytes 1179650
  77.2 6.9 %reshape.180 = bf16[32,2,4608]{2,1,0:T(2,128)(2,1)} reshape(bf16[8192,36]{1,0:T(8,128)(2,1)} %reduce) | data formatting | bytes 1179648
  84.1 7.6 %all-to-all-start = ((bf16[32,2,4608]{2,1,0:T(2,128)(2,1)}), bf16[32,2,4608]{2,1,0:T(2,128)(2,1)}, u32[]{:S(2)}, u32[]{:S(2)}) async-start(bf16[32,2,4608]{2,1,0:T(2,128)(2,1)} %reshape.180), calls=%async_computation | async-start | bytes 1179648 | tf_op jit(solution)/shard_map/all_to_all | solution.py:48
  92.8 2.4 reshape.166
  95.2 2.7 copy.54
  97.9 2.3 fusion.54
  100.3 1.4 copy.72
  101.9 3.5 fusion.21
  105.3 11.1 %reshape.181 = bf16[8192,1,36]{2,1,0:T(2,128)(2,1)} reshape(bf16[32,2,4608]{2,1,0:T(2,128)(2,1)} %all-to-all-done) | data formatting | bytes 1179648
  116.4 9.0 %copy.50 = bf16[1,36,8192]{2,1,0:T(8,128)(2,1)} copy(bf16[1,36,8192]{1,0,2:T(2,128)(2,1)} %bitcast.147) | data formatting | bytes 1179648 | tf_op jit(solution)/shard_map/all_to_all | solution.py:48
  127.8 2.0 reshape.165
  129.8 2.1 copy.52
  131.9 3.3 fusion.18
  136.3 2.0 fusion.22
  138.3 2.1 copy.55
  140.4 2.0 reshape.167
  142.4 23.4 %all_to_all.45 = bf16[32,36,256]{2,1,0:T(8,128)(2,1)S(1)} all-to-all(bf16[32,36,256]{2,1,0:T(8,128)(2,1)} %reshape.167), channel_id=1, replica_groups=mesh['geo'=16,'freq'=32] {'freq'}, dimensions={0} | all-to-all | bytes 1179648 | tf_op jit(solution)/shard_map/all_to_all | solution.py:54
  166.8 2.0 reshape.168
  168.8 2.0 reshape.169
  173.2 1.4 copy.57
  174.6 10.0 %collective-permute-start.2 = (bf16[1,36,64,1]{2,1,3,0:T(8,128)(2,1)S(1)}, bf16[1,36,64,1]{2,1,3,0:T(8,128)(2,1)S(1)}, u32[]{:S(2)}, u32[]{:S(2)}) collective-permute-start(bf16[1,36,64,1]{2,1,3,0:T(8,128)(2,1)S(1)} %copy.57), channel_id=1, source_target_pairs={{0,32},{32,64},{64,96},{96,128},{128,160},{160,192},{192,224},{224... | collective-permute-start | bytes 13832 | tf_op jit(solution)/shard_map/ppermute | solution.py:19
  184.6 1.4 copy.59
  186.0 1.9 multiply_bitcast_fusion
  190.2 2.1 maximum_convert_fusion.1
  193.0 1.8 fusion.35
  194.8 2.1 reshape.170
  196.9 8.8 %copy.62 = bf16[1,36,8192]{1,0,2:T(2,128)(2,1)} copy(bf16[1,36,8192]{2,1,0:T(8,128)(2,1)} %reshape.170) | data formatting | bytes 1179648 | tf_op jit(solution)/shard_map/reshape | solution.py:47
  205.7 46.5 %reduce.1 = bf16[8192,36]{1,0:T(8,128)(2,1)} reduce(bf16[8192,1,36]{2,1,0:T(2,128)(2,1)} %bitcast.146, bf16[]{:T(256)} %broadcast.68), dimensions={1}, to_apply=%bitcast.131.reduce_sub_computation | reduce | bytes 1179650
  252.2 7.1 %reshape.182 = bf16[32,2,4608]{2,1,0:T(2,128)(2,1)} reshape(bf16[8192,36]{1,0:T(8,128)(2,1)} %reduce.1) | data formatting | bytes 1179648
  259.3 4.8 %all-to-all-start.2 = ((bf16[32,2,4608]{2,1,0:T(2,128)(2,1)}), bf16[32,2,4608]{2,1,0:T(2,128)(2,1)}, u32[]{:S(2)}, u32[]{:S(2)}) async-start(bf16[32,2,4608]{2,1,0:T(2,128)(2,1)} %reshape.182), calls=%async_computation.2 | async-start | bytes 1179648 | tf_op jit(solution)/shard_map/all_to_all | solution.py:48
  264.1 2.1 copy.73
  266.2 3.7 fusion.10
  269.9 8.8 %all-to-all-done.2 = bf16[32,2,4608]{2,1,0:T(2,128)(2,1)} async-done(((bf16[32,2,4608]{2,1,0:T(2,128)(2,1)}), bf16[32,2,4608]{2,1,0:T(2,128)(2,1)}, u32[]{:S(2)}, u32[]{:S(2)}) %all-to-all-start.2) | async-done | bytes 589856 | tf_op jit(solution)/shard_map/all_to_all | solution.py:48
  278.6 11.1 %reshape.183 = bf16[8192,1,36]{2,1,0:T(2,128)(2,1)} reshape(bf16[32,2,4608]{2,1,0:T(2,128)(2,1)} %all-to-all-done.2) | data formatting | bytes 1179648
  289.7 9.0 %copy.63 = bf16[1,36,8192]{2,1,0:T(8,128)(2,1)} copy(bf16[1,36,8192]{1,0,2:T(2,128)(2,1)} %bitcast.148) | data formatting | bytes 1179648 | tf_op jit(solution)/shard_map/all_to_all | solution.py:48
  301.2 2.0 reshape.171
  303.2 2.2 copy.65
  305.3 5.6 %fusion.29 = (f32[256]{0:T(256)S(1)}, f32[256]{0:T(256)S(1)}, f32[256]{0:T(256)S(1)}, f32[256]{0:T(256)S(1)}, f32[1152,256]{0,1:T(8,128)}) fusion(f32[1152,256]{0,1:T(8,128)} %copy-done.2, f32[1152,256]{0,1:T(8,128)} %copy.54, bf16[1,1152,256]{1,2,0:T(8,128)(2,1)S(1)} %copy.72, bf16[1,1152,256]{1,2,0:T(8,128)(2,1)} %copy.73, f32[1152,256]{0,1:T(8,128)} %fusion.10, ...), kind=kOutput, calls=%fused_computation.47 | convolution fusion | flops 686259200 | bytes 11506688 | tf_op jit(solution)/shard_map/dot_general | solution.py:75
  311.4 102.4 %psum.16 = f32[64]{0:T(128)S(1)} all-reduce(f32[64]{0:T(128)S(1)} %fusion.40), channel_id=1, replica_groups=mesh['geo'=16,'freq'=32] {'geo','freq'}, use_global_device_ids=true, to_apply=%region_2.3 | all-reduce | flops 64 | bytes 512 | tf_op jit(solution)/shard_map/psum | solution.py:86
  414.3 3.2 fusion.23
  (47 shorter events, 23.9 us)
Async XLA Ops:
  0.6 101.2 %copy-start = (bf16[1152,1152]{1,0:T(8,128)(2,1)S(1)}, bf16[1152,1152]{1,0:T(8,128)(2,1)}, u32[]{:S(2)}) copy-start(bf16[1152,1152]{1,0:T(8,128)(2,1)} %param.11) | copy-start | bytes 7962628
  5.3 9.7 %collective-permute-start = (bf16[1,36,64,1]{2,1,3,0:T(8,128)(2,1)S(1)}, bf16[1,36,64,1]{2,1,3,0:T(8,128)(2,1)S(1)}, u32[]{:S(2)}, u32[]{:S(2)}) collective-permute-start(bf16[1,36,64,1]{2,1,3,0:T(8,128)(2,1)S(1)} %copy.45), channel_id=1, source_target_pairs={{0,32},{32,64},{64,96},{96,128},{128,160},{160,192},{192,224},{224... | collective-permute-start | bytes 13832 | tf_op jit(solution)/shard_map/ppermute | solution.py:19
  10.1 6.0 %collective-permute-start.1 = (bf16[1,36,64,1]{2,1,3,0:T(8,128)(2,1)S(1)}, bf16[1,36,64,1]{2,1,3,0:T(8,128)(2,1)S(1)}, u32[]{:S(2)}, u32[]{:S(2)}) collective-permute-start(bf16[1,36,64,1]{2,1,3,0:T(8,128)(2,1)S(1)} %copy.46), channel_id=1, source_target_pairs={{32,0},{64,32},{96,64},{128,96},{160,128},{192,160},{224,192},{256... | collective-permute-start | bytes 13832 | tf_op jit(solution)/shard_map/ppermute | solution.py:20
  84.1 7.6 %copy-start.3 = (f32[32,256]{1,0:T(8,128)S(1)}, f32[32,256]{1,0:T(8,128)}, u32[]{:S(2)}) copy-start(f32[32,256]{1,0:T(8,128)} %param.12) | copy-start | bytes 98308
  84.1 21.3 %all-to-all-start = ((bf16[32,2,4608]{2,1,0:T(2,128)(2,1)}), bf16[32,2,4608]{2,1,0:T(2,128)(2,1)}, u32[]{:S(2)}, u32[]{:S(2)}) async-start(bf16[32,2,4608]{2,1,0:T(2,128)(2,1)} %reshape.180), calls=%async_computation | async-start | bytes 1179648 | tf_op jit(solution)/shard_map/all_to_all | solution.py:48
  100.2 1.4 copy-start.4
  100.3 1.4 copy-start.5
  131.9 4.4 %copy-start.1 = (f32[1152,256]{0,1:T(8,128)S(1)}, f32[1152,256]{0,1:T(8,128)}, u32[]{:S(2)}) copy-start(f32[1152,256]{0,1:T(8,128)} %copy.54) | copy-start | bytes 3538948
  135.2 1.1 copy-start.2
  174.6 13.3 %collective-permute-start.2 = (bf16[1,36,64,1]{2,1,3,0:T(8,128)(2,1)S(1)}, bf16[1,36,64,1]{2,1,3,0:T(8,128)(2,1)S(1)}, u32[]{:S(2)}, u32[]{:S(2)}) collective-permute-start(bf16[1,36,64,1]{2,1,3,0:T(8,128)(2,1)S(1)} %copy.57), channel_id=1, source_target_pairs={{0,32},{32,64},{64,96},{96,128},{128,160},{160,192},{192,224},{224... | collective-permute-start | bytes 13832 | tf_op jit(solution)/shard_map/ppermute | solution.py:19
  186.0 3.1 collective-permute-start.3
  259.3 19.3 %all-to-all-start.2 = ((bf16[32,2,4608]{2,1,0:T(2,128)(2,1)}), bf16[32,2,4608]{2,1,0:T(2,128)(2,1)}, u32[]{:S(2)}, u32[]{:S(2)}) async-start(bf16[32,2,4608]{2,1,0:T(2,128)(2,1)} %reshape.182), calls=%async_computation.2 | async-start | bytes 1179648 | tf_op jit(solution)/shard_map/all_to_all | solution.py:48
where the time goes:
time: 427 us; the launch traced here: 419 us
  blocking collectives  126 us (30%)
  local copies, waits for them, and re-layouts  124 us (29%)
  other arithmetic  108 us (25%)
  starting transfers between devices  29.3 us (7%)
  matrix products  21.8 us (5%)
  waiting for transfers between devices  8.81 us (2%)
    psum x1, blocking collectives, add_groups(): return total + lax.psum(local_sums, ('geo', 'freq'))  102 us
    unnamed x2, other arithmetic  93.1 us
    unnamed x22, local copies, waits for them, and re-layouts  44.8 us
    all_to_all x1, blocking collectives, into_grid(): lax.all_to_all(split, 'freq', split_axis=0, concat_axis=2, tiled=True)  23.4 us
    all_to_all x6, local copies, waits for them, and re-layouts, into_points(): lax.all_to_all(flat, 'freq', split_axis=2, concat_axis=0, tiled=True)  20.5 us
    reshape x4, local copies, waits for them, and re-layouts, into_points(): flat = field.reshape(freq_local, directions, lat_cells * lon_cells)  19.4 us
    dot_general x4, matrix products, source_adjoint(): lax.dot_general(interaction, adjoint.astype(jnp.bfloat16), (((0,), (0,)),...  14 us
    ppermute x2, starting transfers between devices, with_halo(): before = lax.ppermute(last, axis, up)  13.5 us
  transfers between devices with their start and end apart: 6, of which 2 were waited for; matrix products, arithmetic and copies ran while one was open for 7% of the time, Pallas kernels for 0%

commit v1 on v0

v1 whole, which is shorter than its diff:
```python
import functools

import jax
import jax.numpy as jnp
from jax import lax
from jax.experimental import pallas as pl
from jax.experimental.pallas import tpu as pltpu
from jax.sharding import PartitionSpec as P

F32 = jnp.float32
BF16 = jnp.bfloat16
step_weight = 0.25
PAD = 40
MIB = 1 << 20
WHOLE = pl.BlockSpec(memory_space=pltpu.VMEM)


def call(kernel, outs, args, scratch=(), flops=0, limit=32):
    size = sum(a.size * a.dtype.itemsize for a in (*args, *outs))
    return pl.pallas_call(
        kernel,
        out_shape=outs,
        in_specs=[WHOLE] * len(args),
        out_specs=[WHOLE] * len(outs),
        scratch_shapes=list(scratch),
        compiler_params=pltpu.CompilerParams(vmem_limit_bytes=limit * MIB),
        cost_estimate=pl.CostEstimate(flops=flops, bytes_accessed=size, transcendentals=0),
    )(*args)


def shape(dims, kind):
    return jax.ShapeDtypeStruct(dims, kind)


def edge_picks(width, lon):
    row = lax.broadcasted_iota(jnp.int32, (16, width), 0)
    lane = lax.broadcasted_iota(jnp.int32, (16, width), 1)
    picks = jnp.zeros((16, width), F32)
    for half in range(width // lon):
        picks = jnp.where((row == half) & (lane == half * lon), 1.0, picks)
        picks = jnp.where((row == 8 + half) & (lane == half * lon + lon - 1), 1.0, picks)
    return picks.astype(BF16)


def take_edges(values, picks):
    return lax.dot_general(picks, values, (((1,), (1,)), ((), ())), preferred_element_type=F32)


def put_edges(from_west, from_east, width, lon):
    both = jnp.concatenate([from_west.astype(F32), from_east.astype(F32)], axis=0).astype(BF16)
    return lax.dot_general(
        both, edge_picks(width, lon), (((0,), (0,)), ((), ())), preferred_element_type=F32
    )


def split_rates(lon_rate, lat_rate):
    lon_abs, lat_abs = jnp.abs(lon_rate), jnp.abs(lat_rate)
    east = jnp.where(lon_rate > 0, lon_abs, 0.0)
    north = jnp.where(lat_rate > 0, lat_abs, 0.0)
    return 1.0 - lon_abs - lat_abs, east, lon_abs - east, north, lat_abs - north


def regroup_kernel(field_ref, mask_ref, rows_ref, west_ref, east_ref):
    directions, lat, lon = field_ref.shape
    rows = directions * lat
    mask = mask_ref[...].astype(F32)
    rows_ref[0:PAD, :] = jnp.zeros((PAD, lon), F32)
    rows_ref[PAD + rows :, :] = jnp.zeros((PAD, lon), F32)
    for d in range(directions):
        rows_ref[pl.ds(PAD + d, lat, stride=directions), :] = field_ref[d].astype(F32) * mask
    edges = take_edges(rows_ref[PAD : PAD + rows, :].astype(BF16), edge_picks(lon, lon))
    west_ref[...] = edges[0:8].astype(BF16)
    east_ref[...] = edges[8:16].astype(BF16)


def interior_kernel(rows_ref, lon_ref, lat_ref, part_ref, rate_ref, lon_scr, lat_scr):
    freqs, directions = lon_ref.shape
    peers, height, lon = part_ref.shape
    own = lax.broadcasted_iota(jnp.int32, (freqs, lon), 0) == lax.axis_index("freq")
    own = own.astype(F32)
    for ref, scr in ((lon_ref, lon_scr), (lat_ref, lat_scr)):
        rate = lax.dot_general(
            ref[...], own, (((0,), (0,)), ((), ())),
            precision=lax.Precision.HIGHEST, preferred_element_type=F32,
        )
        for at in range(0, height, directions):
            scr[at : at + directions, :] = rate
    center, east, west, north, south = split_rates(lon_scr[...], lat_scr[...])
    lane = lax.broadcasted_iota(jnp.int32, (height, lon), 1)
    rate_ref[...] = jnp.where(lane == 0, west, east)
    east = jnp.where(lane == lon - 1, 0.0, east)
    west = jnp.where(lane == 0, 0.0, west)
    for r in range(peers):
        at = PAD + r * height
        here = rows_ref[at : at + height, :]
        part_ref[r] = (
            center * here
            + east * pltpu.roll(here, lon - 1, 1)
            + west * pltpu.roll(here, 1, 1)
            + north * rows_ref[at + directions : at + directions + height, :]
            + south * rows_ref[at - directions : at - directions + height, :]
        )


def edges_kernel(part_ref, rate_ref, west_ref, east_ref, out_ref):
    peers, height, lon = part_ref.shape
    cols = put_edges(west_ref[...], east_ref[...], lon, lon)
    rate = rate_ref[...]
    for r in range(peers):
        out_ref[r] = (part_ref[r] + rate * cols[r * height : (r + 1) * height]).astype(BF16)


def rates_kernel(lon_ref, lat_ref, center_ref, east_ref, west_ref, north_ref, south_ref, scr):
    freqs, directions = lon_ref.shape
    lanes = center_ref.shape[1]
    turned = []
    for ref in (lon_ref, lat_ref):
        scr[...] = jnp.zeros_like(scr)
        scr[0:freqs, 0:directions] = ref[...]
        turned.append(scr[...].T)
    refs = (center_ref, east_ref, west_ref, north_ref, south_ref)
    for f in range(freqs):
        cols = [jnp.broadcast_to(t[0:directions, f : f + 1], (directions, lanes)) for t in turned]
        for ref, rate in zip(refs, split_rates(*cols)):
            ref[f * directions : (f + 1) * directions, :] = rate


def group_hits(sediment, groups):
    points = sediment.shape[1]
    return (lax.broadcasted_iota(jnp.int32, (groups, points), 0) == sediment).astype(F32)


def states_kernel(
    traj_ref, inter_ref, kappa_ref, coeff_ref, sed_ref, turned_ref, decay_ref, factor_ref, next_ref
):
    steps, components, points = traj_ref.shape
    freqs = kappa_ref.shape[0]
    directions = components // freqs
    groups = coeff_ref.shape[1]
    hits = group_hits(sed_ref[...], groups)
    coeff = jnp.dot(
        jnp.broadcast_to(coeff_ref[...], (8, groups)), hits,
        precision=lax.Precision.HIGHEST, preferred_element_type=F32,
    )[0:1]
    for f in range(freqs):
        factor_ref[f * directions : (f + 1) * directions, :] = jnp.broadcast_to(
            kappa_ref[f : f + 1, :], (directions, points)
        )
    decay_ref[...] = 1.0 - step_weight * (factor_ref[...] * coeff)
    turned_ref[...] = inter_ref[...].T
    chunk = components // 4
    for n in range(steps):
        state = traj_ref[n]
        squares = state * state
        for at in range(0, components, chunk):
            forced = jnp.dot(inter_ref[at : at + chunk, :], squares, preferred_element_type=F32)
            here = traj_ref[n, at : at + chunk, :].astype(F32)
            next_ref[n, at : at + chunk, :] = (
                decay_ref[at : at + chunk, :] * here + step_weight * forced
            )


def two_substeps(m_scr, r_scr, turned_ref, decay_ref, factor_ref, next_ref, traj_ref, n, write):
    components, points = m_scr.shape
    chunk = components // 4
    weights = jnp.zeros((8, points), F32)
    moved = r_scr[...]
    for at in range(0, components, chunk):
        rows = slice(at, at + chunk)
        pulled = jnp.dot(turned_ref[rows, :], moved, preferred_element_type=F32)
        after, state = next_ref[n, rows, :], traj_ref[n, rows, :].astype(F32)
        old = m_scr[rows, :]
        new = decay_ref[rows, :] * old + 0.5 * (after * pulled)
        terms = factor_ref[rows, :] * (old * after + new * state)
        weights = weights + terms.reshape(chunk // 8, 8, points).sum(axis=0)
        m_scr[rows, :] = new
        r_scr[rows, :] = new.astype(BF16)
    moved = r_scr[...]
    for at in range(0, components, chunk):
        rows = slice(at, at + chunk)
        pulled = jnp.dot(turned_ref[rows, :], moved, preferred_element_type=F32)
        state = traj_ref[n, rows, :].astype(F32)
        write(rows, decay_ref[rows, :] * m_scr[rows, :] + 0.5 * (state * pulled))
    return weights


def first_kernel(
    n, moved_ref, turned_ref, decay_ref, factor_ref, next_ref, traj_ref, mask_ref,
    low_ref, high_ref, west_ref, east_ref, weights_ref, m_scr, r_scr,
):
    freqs, height, lon = moved_ref.shape
    directions = height // 2
    for f in range(freqs):
        block = moved_ref[f].astype(F32)
        rows = slice(f * directions, (f + 1) * directions)
        m_scr[rows, 0:lon] = block[0:directions]
        m_scr[rows, lon : 2 * lon] = block[directions:height]
    r_scr[...] = m_scr[...].astype(BF16)
    mask = mask_ref[...]
    picks = edge_picks(2 * lon, lon)

    def write(rows, values):
        masked = (values * mask).astype(BF16)
        low_ref[rows, :] = masked[:, 0:lon]
        high_ref[rows, :] = masked[:, lon : 2 * lon]
        r_scr[rows, :] = masked

    weights_ref[...] = two_substeps(
        m_scr, r_scr, turned_ref, decay_ref, factor_ref, next_ref, traj_ref, n, write
    )
    edges = take_edges(r_scr[...], picks)
    west_ref[...] = edges[0:8].astype(BF16)
    east_ref[...] = edges[8:16].astype(BF16)


def second_kernel(
    n, low_ref, high_ref, north_ref, south_ref, west_ref, east_ref,
    center_rate, east_rate, west_rate, north_rate, south_rate,
    turned_ref, decay_ref, factor_ref, next_ref, traj_ref, sed_ref, weights_ref,
    out_ref, sums_ref, m_scr, r_scr,
):
    components, lon = low_ref.shape
    cols = put_edges(west_ref[...], east_ref[...], 2 * lon, lon)
    chunk = components // 8
    lane = lax.broadcasted_iota(jnp.int32, (chunk, lon), 1)
    for at in range(0, components, chunk):
        rows = slice(at, at + chunk)
        low, high = low_ref[rows, :].astype(F32), high_ref[rows, :].astype(F32)
        above, below = north_ref[rows, :].astype(F32), south_ref[rows, :].astype(F32)
        for half, (here, up, down) in enumerate(((low, high, below), (high, above, low))):
            lanes = slice(half * lon, (half + 1) * lon)
            edge = cols[rows, lanes]
            east = jnp.where(lane == lon - 1, edge, pltpu.roll(here, lon - 1, 1))
            west = jnp.where(lane == 0, edge, pltpu.roll(here, 1, 1))
            value = (
                center_rate[rows, :] * here
                + east_rate[rows, :] * east
                + west_rate[rows, :] * west
                + north_rate[rows, :] * up
                + south_rate[rows, :] * down
            ).astype(BF16)
            r_scr[rows, lanes] = value
            m_scr[rows, lanes] = value.astype(F32)

    def write(rows, values):
        out_ref[rows, :] = values.astype(BF16)

    weights = weights_ref[...] + two_substeps(
        m_scr, r_scr, turned_ref, decay_ref, factor_ref, next_ref, traj_ref, n, write
    )
    hits = group_hits(sed_ref[...], sums_ref.shape[2])
    sums = lax.dot_general(
        weights, hits, (((1,), (1,)), ((), ())),
        precision=lax.Precision.HIGHEST, preferred_element_type=F32,
    )
    sums_ref[...] = jnp.broadcast_to(sums[None], sums_ref.shape)


def add_kernel(parts_ref, out_ref):
    out_ref[...] = jnp.broadcast_to(parts_ref[...].sum(axis=0)[None], out_ref.shape)


def final_kernel(scale, parts_ref, out_ref):
    total = parts_ref[...].sum(axis=0).sum(axis=0, keepdims=True)
    out_ref[...] = total[:, 0 : out_ref.shape[1]] * scale


def shards(
    adjoint_final, trajectory, interaction, friction_factor, friction_coeff,
    courant_lon, courant_lat, sea_mask, sediment,
):
    freq_local, directions, lat, lon = adjoint_final.shape
    steps, components, points = trajectory.shape
    groups = friction_coeff.shape[0]
    peers, regions = lax.axis_size("freq"), lax.axis_size("geo")
    me = lax.axis_index("freq")
    rows = directions * lat
    height = rows // peers
    eastward = [(i, (i + 1) % regions) for i in range(regions)]
    westward = [(j, i) for i, j in eastward]
    northward = [(i, i + 1) for i in range(peers - 1)]
    southward = [(j, i) for i, j in northward]

    field = adjoint_final.reshape(directions, lat, lon)
    grouped, west, east = call(
        regroup_kernel,
        [shape((rows + 2 * PAD, lon), F32), shape((8, rows), BF16), shape((8, rows), BF16)],
        [field, sea_mask],
    )
    from_west = lax.ppermute(east, "geo", eastward)
    from_east = lax.ppermute(west, "geo", westward)
    part, rate = call(
        interior_kernel,
        [shape((peers, height, lon), F32), shape((height, lon), F32)],
        [grouped, courant_lon, courant_lat],
        [pltpu.VMEM((height, lon), F32), pltpu.VMEM((height, lon), F32)],
    )
    (sent,) = call(
        edges_kernel, [shape((peers, height, lon), BF16)], [part, rate, from_west, from_east]
    )
    sent, trajectory, courant_lon, courant_lat = lax.optimization_barrier(
        (sent, trajectory, courant_lon, courant_lat)
    )
    moved = lax.all_to_all(sent, "freq", split_axis=0, concat_axis=0, tiled=True)

    sediment_row = sediment.reshape(1, points)
    mask_row = lax.dynamic_slice_in_dim(sea_mask, me * (points // lon), points // lon, 0)
    mask_row = mask_row.astype(F32).reshape(1, points)
    turned, decay, factor, following = call(
        states_kernel,
        [
            shape((components, components), BF16),
            shape((components, points), F32),
            shape((components, points), F32),
            shape((steps, components, points), F32),
        ],
        [trajectory, interaction, friction_factor, friction_coeff.reshape(1, groups), sediment_row],
        flops=4 * components * components * points,
    )
    rates = call(
        rates_kernel,
        [shape((components, lon), F32)] * 5,
        [courant_lon, courant_lat],
        [pltpu.VMEM((128, 128), F32)],
    )
    carried = [pltpu.VMEM((components, points), F32), pltpu.VMEM((components, points), BF16)]
    low, high, west, east, weights = call(
        functools.partial(first_kernel, 1),
        [
            shape((components, lon), BF16),
            shape((components, lon), BF16),
            shape((8, components), BF16),
            shape((8, components), BF16),
            shape((8, points), F32),
        ],
        [moved, turned, decay, factor, following, trajectory, mask_row],
        carried,
        flops=4 * components * components * points,
    )
    above = lax.ppermute(low, "freq", southward)
    below = lax.ppermute(high, "freq", northward)
    from_west = lax.ppermute(east, "geo", eastward)
    from_east = lax.ppermute(west, "geo", westward)
    result, sums = call(
        functools.partial(second_kernel, 0),
        [shape((components, points), BF16), shape((peers, 8, 128), F32)],
        [
            low, high, above, below, from_west, from_east, *rates,
            turned, decay, factor, following, trajectory, sediment_row, weights,
        ],
        carried,
        flops=4 * components * components * points,
    )
    sums = lax.all_to_all(sums, "freq", split_axis=0, concat_axis=0, tiled=True)
    (sums,) = call(add_kernel, [shape((regions, 8, 128), F32)], [sums])
    sums = lax.all_to_all(sums, "geo", split_axis=0, concat_axis=0, tiled=True)
    point_total = points * peers * regions
    scale = -step_weight * groups / (point_total * components)
    (total,) = call(functools.partial(final_kernel, scale), [shape((1, groups), F32)], [sums])
    return result, total.reshape(groups)


def solution(mesh):
    in_specs = (
        P("freq", None, None, "geo"),
        P(None, None, ("geo", "freq")),
        P(),
        P(None, ("geo", "freq")),
        P(),
        P(),
        P(),
        P(None, "geo"),
        P(("geo", "freq")),
    )
    out_specs = (P(None, ("geo", "freq")), P())
    return jax.shard_map(shards, mesh=mesh, in_specs=in_specs, out_specs=out_specs, check_vma=False)
```

time: 427 us -> 102 us (0.24); the launches traced: 419 us -> 102 us
  local copies, waits for them, and re-layouts: 124 us -> 15.2 us
  other arithmetic: 108 us -> 0.7 us
  blocking collectives: 126 us -> 39.9 us
  matrix products: 21.8 us -> 0 us
  Pallas kernels: 0 us -> 11 us
    psum x1 -> x0, blocking collectives: 102 us -> none  [add_groups(): return total + lax.psum(local_sums, ('geo', 'freq'))]
    unnamed x2 -> x0, other arithmetic: 93.1 us -> none
    reshape x13 -> x0, local copies, waits for them, and re-layouts: 38.7 us -> none  [the longest x4 19.4 us: into_points(): flat = field.reshape(freq_local, directions, lat_cells * lon_cells)]
    unnamed x22 -> x42, local copies, waits for them, and re-layouts: 44.8 us -> 15.2 us
    dot_general x9 -> x0, matrix products: 21.8 us -> none  [the longest x4 14 us: source_adjoint(): lax.dot_general(interaction, adjoint.astype(jnp.bfloat16), (((0,), (0,)),...]
    all_to_all x7 -> x0, local copies, waits for them, and re-layouts: 21.4 us -> none  [the longest x6 20.5 us: into_points(): lax.all_to_all(flat, 'freq', split_axis=2, concat_axis=0, tiled=True)]
    all_to_all x1 -> x2, blocking collectives: 23.4 us -> 39.9 us  [the longest x1 23.3 us: shards(): sums = lax.all_to_all(sums, 'geo', split_axis=0, concat_axis=0, tiled=True)]
    slice x9 -> x0, local copies, waits for them, and re-layouts: 11.7 us -> none  [the longest x4 5.23 us: with_halo(): last = lax.slice_in_dim(shard, length - width, length, axis=dim)]
  transfers between devices with their start and end apart: 6 -> 7, of which waited for: 2 -> 3; matrix products, arithmetic and copies ran while one was open for 7% -> 1% of each run, Pallas kernels for 0% -> 3%
where the time goes in v1:
time: 102 us
  blocking collectives  39.9 us (39%)
  starting transfers between devices  27 us (26%)
  local copies, waits for them, and re-layouts  15.2 us (15%)
  Pallas kernels  11 us (11%)
  waiting for transfers between devices  7.03 us (7%)
    all_to_all x1, blocking collectives, shards(): sums = lax.all_to_all(sums, 'geo', split_axis=0, concat_axis=0, tiled=True)  23.3 us
    all_to_all x1, blocking collectives, shards(): sums = lax.all_to_all(sums, 'freq', split_axis=0, concat_axis=0, tiled=True)  16.6 us
    unnamed x42, local copies, waits for them, and re-layouts  15.2 us
    ppermute x2, starting transfers between devices, shards(): from_west = lax.ppermute(east, 'geo', eastward)  11 us
    pallas_call x9, Pallas kernels, call(): pl.pallas_call(kernel, out_shape=outs, in_specs=[WHOLE] * len(args), out_...  11 us
    all_to_all x1, starting transfers between devices, shards(): lax.all_to_all(sent, 'freq', split_axis=0, concat_axis=0, tiled=True)  7.27 us
    all_to_all x1, waiting for transfers between devices, shards(): lax.all_to_all(sent, 'freq', split_axis=0, concat_axis=0, tiled=True)  4.39 us
    ppermute x1, starting transfers between devices, shards(): below = lax.ppermute(high, 'freq', northward)  4 us
  transfers between devices with their start and end apart: 7, of which 3 were waited for; matrix products, arithmetic and copies ran while one was open for 1% of the time, Pallas kernels for 3%

profile of v1, /device:TPU:1, one launch (start us, length us, event | category | flops | bytes accessed | tf_op | source)
XLA Modules:
  0.0 101.6 jit_solution(13052298242388379596)
XLA Ops:
  0.6 0.0 copy-start.11
  0.6 1.1 %copy-done.11 = bf16[1,36,64,128]{3,2,1,0:T(8,128)(2,1)S(1)} copy-done((bf16[1,36,64,128]{3,2,1,0:T(8,128)(2,1)S(1)}, bf16[1,36,64,128]{3,2,1,0:T(8,128)(2,1)}, u32[]{:S(2)}) %copy-start.11) | copy-done | bytes 589848
  1.7 0.8 copy-done.16
  2.5 0.3 shard_map.104
  2.8 3.5 %collective-permute-start = (bf16[8,2304]{1,0:T(8,128)(2,1)S(1)}, bf16[8,2304]{1,0:T(8,128)(2,1)S(1)}, u32[]{:S(2)}, u32[]{:S(2)}) collective-permute-start(bf16[8,2304]{1,0:T(8,128)(2,1)S(1)} %get-tuple-element.30), channel_id=1, source_target_pairs={{0,32},{32,64},{64,96},{96,128},{128,160},{160,192},{192,224},{224... | collective-permute-start | bytes 110600 | tf_op jit(solution)/shard_map/ppermute | solution.py:290
  6.3 3.4 %collective-permute-start.1 = (bf16[8,2304]{1,0:T(8,128)(2,1)S(1)}, bf16[8,2304]{1,0:T(8,128)(2,1)S(1)}, u32[]{:S(2)}, u32[]{:S(2)}) collective-permute-start(bf16[8,2304]{1,0:T(8,128)(2,1)S(1)} %get-tuple-element.31), channel_id=1, source_target_pairs={{32,0},{64,32},{96,64},{128,96},{160,128},{192,160},{224,192},{256... | collective-permute-start | bytes 110600 | tf_op jit(solution)/shard_map/ppermute | solution.py:291
  9.7 0.7 copy-done.12
  10.4 0.7 copy-done.14
  11.1 0.9 shard_map.105
  12.0 0.0 collective-permute-done.west_ref
  12.0 0.0 collective-permute-done.1.east_ref
  12.0 0.0 copy-start.17
  12.0 0.0 copy-start.19
  12.1 0.0 copy-start.20
  12.1 1.2 %shard_map.106 = bf16[32,72,128]{2,1,0:T(8,128)(2,1)} custom-call(f32[32,72,128]{2,1,0:T(8,128)S(1)} %get-tuple-element.28.part_ref, f32[72,128]{1,0:T(8,128)S(1)} %get-tuple-element.29.rate_ref, bf16[8,2304]{1,0:T(8,128)(2,1)S(1)} %collective-permute-done.west_ref, bf16[8,2304]{1,0:T(8,128)(2,1)S(1)} %collective-permute-done.1.east_ref), custom_call_target="tpu_custom_call" | custom-call | bytes 1880064 | tf_op jit(solution)/shard_map/pallas_call | solution.py:20
  13.2 7.3 %all-to-all-start = ((bf16[32,72,128]{2,1,0:T(8,128)(2,1)}), bf16[32,72,128]{2,1,0:T(8,128)(2,1)S(1)}, u32[]{:S(2)}, u32[]{:S(2)}) async-start(bf16[32,72,128]{2,1,0:T(8,128)(2,1)} %shard_map.106), calls=%async_computation | async-start | bytes 1179648 | tf_op jit(solution)/shard_map/all_to_all | solution.py:304
  20.5 0.7 dynamic-slice_convert_fusion
  21.2 0.0 copy-done.17
  21.2 0.0 copy-done.19
  21.2 0.0 copy-start.3
  21.3 1.3 %copy-done.3 = bf16[2,1152,256]{2,1,0:T(8,128)(2,1)S(1)} copy-done((bf16[2,1152,256]{2,1,0:T(8,128)(2,1)S(1)}, bf16[2,1152,256]{2,1,0:T(8,128)(2,1)}, u32[]{:S(2)}) %copy-start.3) | copy-done | bytes 1179672
  22.5 1.7 %copy-done.18 = bf16[1152,1152]{1,0:T(8,128)(2,1)S(1)} copy-done((bf16[1152,1152]{1,0:T(8,128)(2,1)S(1)}, bf16[1152,1152]{1,0:T(8,128)(2,1)}, u32[]{:S(2)}) %copy-start.18) | copy-done | bytes 2654232
  24.3 1.8 %shard_map.107 = (bf16[1152,1152]{1,0:T(8,128)(2,1)S(1)}, f32[1152,256]{1,0:T(8,128)S(1)}, f32[1152,256]{1,0:T(8,128)S(1)}, f32[2,1152,256]{2,1,0:T(8,128)S(1)}) custom-call(bf16[2,1152,256]{2,1,0:T(8,128)(2,1)S(1)} %copy-done.3, bf16[1152,1152]{1,0:T(8,128)(2,1)S(1)} %copy-done.18, f32[32,256]{1,0:T(8,128)S(1)} %copy-done.19, f32[1,64]{1,0:T(1,128)S(1)} %bitcast.9, ...), custom_call_target="tpu_custom_call" | custom-call | flops 1358954496 | bytes 11240704 | tf_op jit(solution)/shard_map/pallas_call | solution.py:20
  26.1 1.4 %copy-done = f32[2,1152,256]{2,1,0:T(8,128)} copy-done((f32[2,1152,256]{2,1,0:T(8,128)}, f32[2,1152,256]{2,1,0:T(8,128)S(1)}, u32[]{:S(2)}) %copy-start) | copy-done | bytes 2359320
  27.5 1.0 copy-done.6
  28.5 1.0 copy-done.9
  29.5 4.4 %all-to-all-done.moved_ref = bf16[32,72,128]{2,1,0:T(8,128)(2,1)S(1)} async-done(((bf16[32,72,128]{2,1,0:T(8,128)(2,1)}), bf16[32,72,128]{2,1,0:T(8,128)(2,1)S(1)}, u32[]{:S(2)}, u32[]{:S(2)}) %all-to-all-start) | async-done | bytes 589856 | tf_op jit(solution)/shard_map/all_to_all | solution.py:304
  33.9 1.7 %copy-done.1 = f32[2,1152,256]{2,1,0:T(8,128)S(1)} copy-done((f32[2,1152,256]{2,1,0:T(8,128)S(1)}, f32[2,1152,256]{2,1,0:T(8,128)}, u32[]{:S(2)}) %copy-start.1) | copy-done | bytes 2359320
  35.6 1.3 %copy-done.4 = bf16[2,1152,256]{2,1,0:T(8,128)(2,1)S(1)} copy-done((bf16[2,1152,256]{2,1,0:T(8,128)(2,1)S(1)}, bf16[2,1152,256]{2,1,0:T(8,128)(2,1)}, u32[]{:S(2)}) %copy-start.4) | copy-done | bytes 1179672
  36.9 1.3 %copy-done.7 = f32[1152,256]{1,0:T(8,128)S(1)} copy-done((f32[1152,256]{1,0:T(8,128)S(1)}, f32[1152,256]{1,0:T(8,128)}, u32[]{:S(2)}) %copy-start.7) | copy-done | bytes 1179672
  38.1 1.3 %copy-done.10 = f32[1152,256]{1,0:T(8,128)S(1)} copy-done((f32[1152,256]{1,0:T(8,128)S(1)}, f32[1152,256]{1,0:T(8,128)}, u32[]{:S(2)}) %copy-start.10) | copy-done | bytes 1179672
  39.4 2.0 %shard_map.108 = (bf16[1152,128]{1,0:T(8,128)(2,1)S(1)}, bf16[1152,128]{1,0:T(8,128)(2,1)S(1)}, bf16[8,1152]{1,0:T(8,128)(2,1)S(1)}, bf16[8,1152]{1,0:T(8,128)(2,1)S(1)}, f32[8,256]{1,0:T(8,128)S(1)}) custom-call(bf16[32,72,128]{2,1,0:T(8,128)(2,1)S(1)} %all-to-all-done.moved_ref, bf16[1152,1152]{1,0:T(8,128)(2,1)S(1)} %get-tuple-element.34.turned_ref, ...), custom_call_target="tpu_custom_call" | custom-call | flops 1358954496 | bytes 9778176 | tf_op jit(solution)/shard_map/pallas_call | solution.py:20
  41.5 1.3 %collective-permute-start.2 = (bf16[1152,128]{1,0:T(8,128)(2,1)S(1)}, bf16[1152,128]{1,0:T(8,128)(2,1)S(1)}, u32[]{:S(2)}, u32[]{:S(2)}) collective-permute-start(bf16[1152,128]{1,0:T(8,128)(2,1)S(1)} %get-tuple-element.38.low_ref), channel_id=1, source_target_pairs={{1,0},{2,1},{3,2},{4,3},{5,4},{6,5},{7,6},{8,7},{9,8},{10,9},{11,1... | collective-permute-start | bytes 884744 | tf_op jit(solution)/shard_map/ppermute | solution.py:340
  42.8 4.0 %collective-permute-start.3 = (bf16[1152,128]{1,0:T(8,128)(2,1)S(1)}, bf16[1152,128]{1,0:T(8,128)(2,1)S(1)}, u32[]{:S(2)}, u32[]{:S(2)}) collective-permute-start(bf16[1152,128]{1,0:T(8,128)(2,1)S(1)} %get-tuple-element.39.high_ref), channel_id=1, source_target_pairs={{0,1},{1,2},{2,3},{3,4},{4,5},{5,6},{6,7},{7,8},{8,9},{9,10},{10,1... | collective-permute-start | bytes 884744 | tf_op jit(solution)/shard_map/ppermute | solution.py:341
  46.8 7.5 %collective-permute-start.4 = (bf16[8,1152]{1,0:T(8,128)(2,1)S(1)}, bf16[8,1152]{1,0:T(8,128)(2,1)S(1)}, u32[]{:S(2)}, u32[]{:S(2)}) collective-permute-start(bf16[8,1152]{1,0:T(8,128)(2,1)S(1)} %get-tuple-element.40), channel_id=1, source_target_pairs={{0,32},{32,64},{64,96},{96,128},{128,160},{160,192},{192,224},{224... | collective-permute-start | bytes 55304 | tf_op jit(solution)/shard_map/ppermute | solution.py:342
  54.3 0.0 collective-permute-start.5
  54.3 0.0 copy-done.15
  54.3 0.5 shard_map.109
  54.8 0.3 collective-permute-done.4.west_ref
  55.2 2.3 %collective-permute-done.5.east_ref = bf16[8,1152]{1,0:T(8,128)(2,1)S(1)} collective-permute-done((bf16[8,1152]{1,0:T(8,128)(2,1)S(1)}, bf16[8,1152]{1,0:T(8,128)(2,1)S(1)}, u32[]{:S(2)}, u32[]{:S(2)}) %collective-permute-start.5) | collective-permute-done | bytes 18464 | tf_op jit(solution)/shard_map/ppermute | solution.py:343
  57.5 0.0 collective-permute-done.2.north_ref
  57.5 0.0 collective-permute-done.3.south_ref
  57.5 0.0 copy-done.5
  57.5 0.0 copy-done.8
  57.5 3.6 %shard_map.110 = (bf16[1152,256]{1,0:T(8,128)(2,1)}, f32[32,8,128]{2,1,0:T(8,128)S(1)}) custom-call(bf16[1152,128]{1,0:T(8,128)(2,1)S(1)} %get-tuple-element.38.low_ref, bf16[1152,128]{1,0:T(8,128)(2,1)S(1)} %get-tuple-element.39.high_ref, bf16[1152,128]{1,0:T(8,128)(2,1)S(1)} %collective-permute-done.2.north_ref, ...), custom_call_target="tpu_custom_call" | custom-call | flops 1358954496 | bytes 13448192 | tf_op jit(solution)/shard_map/pallas_call | solution.py:20
  61.1 16.6 %all_to_all.15.parts_ref = f32[32,8,128]{2,1,0:T(8,128)S(1)} all-to-all(f32[32,8,128]{2,1,0:T(8,128)S(1)} %get-tuple-element.51), channel_id=1, replica_groups=mesh['geo'=16,'freq'=32] {'freq'}, dimensions={0} | all-to-all | bytes 262144 | tf_op jit(solution)/shard_map/all_to_all | solution.py:354
  77.8 23.3 %all_to_all.16.parts_ref = f32[16,8,128]{2,1,0:T(8,128)S(1)} all-to-all(f32[16,8,128]{2,1,0:T(8,128)S(1)} %shard_map.111), channel_id=1, replica_groups=mesh['geo'=16,'freq'=32] {'geo'}, dimensions={0} | all-to-all | bytes 131072 | tf_op jit(solution)/shard_map/all_to_all | solution.py:356
  101.0 0.5 shard_map.112
  (20 shorter events, 0.1 us)
Async XLA Ops:
  0.6 1.1 %copy-start.11 = (bf16[1,36,64,128]{3,2,1,0:T(8,128)(2,1)S(1)}, bf16[1,36,64,128]{3,2,1,0:T(8,128)(2,1)}, u32[]{:S(2)}) copy-start(bf16[1,36,64,128]{3,2,1,0:T(8,128)(2,1)} %param.9) | copy-start | bytes 1769476
  1.7 0.8 copy-start.16
  2.8 9.2 %collective-permute-start = (bf16[8,2304]{1,0:T(8,128)(2,1)S(1)}, bf16[8,2304]{1,0:T(8,128)(2,1)S(1)}, u32[]{:S(2)}, u32[]{:S(2)}) collective-permute-start(bf16[8,2304]{1,0:T(8,128)(2,1)S(1)} %get-tuple-element.30), channel_id=1, source_target_pairs={{0,32},{32,64},{64,96},{96,128},{128,160},{160,192},{192,224},{224... | collective-permute-start | bytes 110600 | tf_op jit(solution)/shard_map/ppermute | solution.py:290
  6.3 5.7 %collective-permute-start.1 = (bf16[8,2304]{1,0:T(8,128)(2,1)S(1)}, bf16[8,2304]{1,0:T(8,128)(2,1)S(1)}, u32[]{:S(2)}, u32[]{:S(2)}) collective-permute-start(bf16[8,2304]{1,0:T(8,128)(2,1)S(1)} %get-tuple-element.31), channel_id=1, source_target_pairs={{32,0},{64,32},{96,64},{128,96},{160,128},{192,160},{224,192},{256... | collective-permute-start | bytes 110600 | tf_op jit(solution)/shard_map/ppermute | solution.py:291
  9.7 0.7 copy-start.12
  10.4 0.7 copy-start.14
  12.0 9.2 %copy-start.17 = (s32[256]{0:T(256)S(1)}, s32[256]{0:T(256)}, u32[]{:S(2)}) copy-start(s32[256]{0:T(256)} %param.17) | copy-start | bytes 3076
  12.0 9.2 %copy-start.19 = (f32[32,256]{1,0:T(8,128)S(1)}, f32[32,256]{1,0:T(8,128)}, u32[]{:S(2)}) copy-start(f32[32,256]{1,0:T(8,128)} %kappa_ref.1) | copy-start | bytes 98308
  12.1 9.2 %copy-start.20 = (f32[64]{0:T(128)S(1)}, f32[64]{0:T(128)}, u32[]{:S(2)}) copy-start(f32[64]{0:T(128)} %param.13) | copy-start | bytes 772
  13.2 20.7 %all-to-all-start = ((bf16[32,72,128]{2,1,0:T(8,128)(2,1)}), bf16[32,72,128]{2,1,0:T(8,128)(2,1)S(1)}, u32[]{:S(2)}, u32[]{:S(2)}) async-start(bf16[32,72,128]{2,1,0:T(8,128)(2,1)} %shard_map.106), calls=%async_computation | async-start | bytes 1179648 | tf_op jit(solution)/shard_map/all_to_all | solution.py:304
  21.2 1.3 %copy-start.3 = (bf16[2,1152,256]{2,1,0:T(8,128)(2,1)S(1)}, bf16[2,1152,256]{2,1,0:T(8,128)(2,1)}, u32[]{:S(2)}) copy-start(bf16[2,1152,256]{2,1,0:T(8,128)(2,1)} %traj_ref.2) | copy-start | bytes 3538948
  22.5 1.7 %copy-start.18 = (bf16[1152,1152]{1,0:T(8,128)(2,1)S(1)}, bf16[1152,1152]{1,0:T(8,128)(2,1)}, u32[]{:S(2)}) copy-start(bf16[1152,1152]{1,0:T(8,128)(2,1)} %inter_ref.1) | copy-start | bytes 7962628
  26.1 1.4 %copy-start = (f32[2,1152,256]{2,1,0:T(8,128)}, f32[2,1152,256]{2,1,0:T(8,128)S(1)}, u32[]{:S(2)}) copy-start(f32[2,1152,256]{2,1,0:T(8,128)S(1)} %get-tuple-element.37.next_ref) | copy-start | bytes 7077892
  27.5 1.0 %copy-start.6 = (f32[1152,256]{1,0:T(8,128)}, f32[1152,256]{1,0:T(8,128)S(1)}, u32[]{:S(2)}) copy-start(f32[1152,256]{1,0:T(8,128)S(1)} %get-tuple-element.35.decay_ref) | copy-start | bytes 3538948
  28.5 1.0 %copy-start.9 = (f32[1152,256]{1,0:T(8,128)}, f32[1152,256]{1,0:T(8,128)S(1)}, u32[]{:S(2)}) copy-start(f32[1152,256]{1,0:T(8,128)S(1)} %get-tuple-element.36.factor_ref) | copy-start | bytes 3538948
  33.9 1.7 %copy-start.1 = (f32[2,1152,256]{2,1,0:T(8,128)S(1)}, f32[2,1152,256]{2,1,0:T(8,128)}, u32[]{:S(2)}) copy-start(f32[2,1152,256]{2,1,0:T(8,128)} %copy-done) | copy-start | bytes 7077892
  35.6 1.3 %copy-start.4 = (bf16[2,1152,256]{2,1,0:T(8,128)(2,1)S(1)}, bf16[2,1152,256]{2,1,0:T(8,128)(2,1)}, u32[]{:S(2)}) copy-start(bf16[2,1152,256]{2,1,0:T(8,128)(2,1)} %traj_ref.2) | copy-start | bytes 3538948
  36.9 1.3 %copy-start.7 = (f32[1152,256]{1,0:T(8,128)S(1)}, f32[1152,256]{1,0:T(8,128)}, u32[]{:S(2)}) copy-start(f32[1152,256]{1,0:T(8,128)} %copy-done.6) | copy-start | bytes 3538948
  38.1 1.3 %copy-start.10 = (f32[1152,256]{1,0:T(8,128)S(1)}, f32[1152,256]{1,0:T(8,128)}, u32[]{:S(2)}) copy-start(f32[1152,256]{1,0:T(8,128)} %copy-done.9) | copy-start | bytes 3538948
  39.4 14.9 %copy-start.13 = (f32[32,36]{1,0:T(8,128)S(1)}, f32[32,36]{1,0:T(8,128)}, u32[]{:S(2)}) copy-start(f32[32,36]{1,0:T(8,128)} %lon_ref.2) | copy-start | bytes 13828
  39.4 14.9 %copy-start.15 = (f32[32,36]{1,0:T(8,128)S(1)}, f32[32,36]{1,0:T(8,128)}, u32[]{:S(2)}) copy-start(f32[32,36]{1,0:T(8,128)} %lat_ref.2) | copy-start | bytes 13828
  39.4 18.1 %copy-start.2 = (f32[2,1152,256]{2,1,0:T(8,128)S(1)}, f32[2,1152,256]{2,1,0:T(8,128)}, u32[]{:S(2)}) copy-start(f32[2,1152,256]{2,1,0:T(8,128)} %copy-done) | copy-start | bytes 7077892
  39.4 18.1 %copy-start.5 = (bf16[2,1152,256]{2,1,0:T(8,128)(2,1)S(1)}, bf16[2,1152,256]{2,1,0:T(8,128)(2,1)}, u32[]{:S(2)}) copy-start(bf16[2,1152,256]{2,1,0:T(8,128)(2,1)} %traj_ref.2) | copy-start | bytes 3538948
  39.4 18.1 %copy-start.8 = (f32[1152,256]{1,0:T(8,128)S(1)}, f32[1152,256]{1,0:T(8,128)}, u32[]{:S(2)}) copy-start(f32[1152,256]{1,0:T(8,128)} %copy-done.6) | copy-start | bytes 3538948
  41.5 16.0 %collective-permute-start.2 = (bf16[1152,128]{1,0:T(8,128)(2,1)S(1)}, bf16[1152,128]{1,0:T(8,128)(2,1)S(1)}, u32[]{:S(2)}, u32[]{:S(2)}) collective-permute-start(bf16[1152,128]{1,0:T(8,128)(2,1)S(1)} %get-tuple-element.38.low_ref), channel_id=1, source_target_pairs={{1,0},{2,1},{3,2},{4,3},{5,4},{6,5},{7,6},{8,7},{9,8},{10,9},{11,1... | collective-permute-start | bytes 884744 | tf_op jit(solution)/shard_map/ppermute | solution.py:340
  42.8 14.7 %collective-permute-start.3 = (bf16[1152,128]{1,0:T(8,128)(2,1)S(1)}, bf16[1152,128]{1,0:T(8,128)(2,1)S(1)}, u32[]{:S(2)}, u32[]{:S(2)}) collective-permute-start(bf16[1152,128]{1,0:T(8,128)(2,1)S(1)} %get-tuple-element.39.high_ref), channel_id=1, source_target_pairs={{0,1},{1,2},{2,3},{3,4},{4,5},{5,6},{6,7},{7,8},{8,9},{9,10},{10,1... | collective-permute-start | bytes 884744 | tf_op jit(solution)/shard_map/ppermute | solution.py:341
  46.8 8.4 %collective-permute-start.4 = (bf16[8,1152]{1,0:T(8,128)(2,1)S(1)}, bf16[8,1152]{1,0:T(8,128)(2,1)S(1)}, u32[]{:S(2)}, u32[]{:S(2)}) collective-permute-start(bf16[8,1152]{1,0:T(8,128)(2,1)S(1)} %get-tuple-element.40), channel_id=1, source_target_pairs={{0,32},{32,64},{64,96},{96,128},{128,160},{160,192},{192,224},{224... | collective-permute-start | bytes 55304 | tf_op jit(solution)/shard_map/ppermute | solution.py:342
  54.3 3.2 %collective-permute-start.5 = (bf16[8,1152]{1,0:T(8,128)(2,1)S(1)}, bf16[8,1152]{1,0:T(8,128)(2,1)S(1)}, u32[]{:S(2)}, u32[]{:S(2)}) collective-permute-start(bf16[8,1152]{1,0:T(8,128)(2,1)S(1)} %get-tuple-element.41), channel_id=1, source_target_pairs={{32,0},{64,32},{96,64},{128,96},{160,128},{192,160},{224,192},{256... | collective-permute-start | bytes 55304 | tf_op jit(solution)/shard_map/ppermute | solution.py:343

commit v2 on v1

v2 whole, which is shorter than its diff:
```python
import functools

import jax
import jax.numpy as jnp
from jax import lax
from jax.experimental import pallas as pl
from jax.experimental.pallas import tpu as pltpu
from jax.sharding import PartitionSpec as P

F32 = jnp.float32
BF16 = jnp.bfloat16
step_weight = 0.25
PAD = 40
MIB = 1 << 20
WHOLE = pl.BlockSpec(memory_space=pltpu.VMEM)
OUTSIDE = pl.BlockSpec(memory_space=pl.ANY)


def call(kernel, outs, args, scratch=(), flops=0, late=None, limit=32):
    late = {} if late is None else late
    places = sorted(late)
    size = sum(a.size * a.dtype.itemsize for a in (*args, *outs))
    args = [
        pltpu.with_memory_space_constraint(a, pltpu.HBM) if i in late else a
        for i, a in enumerate(args)
    ]
    n = len(args) + len(outs) + len(scratch)

    def body(*refs):
        given, kept, buffers = list(refs[: len(args)]), refs[len(args) : n], refs[n:]
        copies = {}
        for k, i in enumerate(places):
            source = given[i] if late[i] is None else given[i].at[late[i]]
            copies[i] = pltpu.make_async_copy(source, buffers[k], buffers[-1].at[k])
            copies[i].start()
            given[i] = buffers[k]
        if places:
            kernel(*given, *kept, wait=lambda *which: [copies[i].wait() for i in which])
        else:
            kernel(*given, *kept)

    buffers = [
        pltpu.VMEM(args[i].shape if late[i] is None else args[i].shape[1:], args[i].dtype)
        for i in places
    ]
    if places:
        buffers.append(pltpu.SemaphoreType.DMA((len(places),)))
    return pl.pallas_call(
        body,
        out_shape=outs,
        in_specs=[OUTSIDE if i in late else WHOLE for i in range(len(args))],
        out_specs=[WHOLE] * len(outs),
        scratch_shapes=[*scratch, *buffers],
        compiler_params=pltpu.CompilerParams(vmem_limit_bytes=limit * MIB),
        cost_estimate=pl.CostEstimate(flops=flops, bytes_accessed=size, transcendentals=0),
    )(*args)


def shape(dims, kind):
    return jax.ShapeDtypeStruct(dims, kind)


def edge_picks(width, lon):
    row = lax.broadcasted_iota(jnp.int32, (16, width), 0)
    lane = lax.broadcasted_iota(jnp.int32, (16, width), 1)
    picks = jnp.zeros((16, width), F32)
    for half in range(width // lon):
        picks = jnp.where((row == half) & (lane == half * lon), 1.0, picks)
        picks = jnp.where((row == 8 + half) & (lane == half * lon + lon - 1), 1.0, picks)
    return picks.astype(BF16)


def take_edges(values, picks):
    return lax.dot_general(picks, values, (((1,), (1,)), ((), ())), preferred_element_type=F32)


def put_edges(from_west, from_east, width, lon):
    both = jnp.concatenate([from_west.astype(F32), from_east.astype(F32)], axis=0).astype(BF16)
    return lax.dot_general(
        both, edge_picks(width, lon), (((0,), (0,)), ((), ())), preferred_element_type=F32
    )


def split_rates(lon_rate, lat_rate):
    lon_abs, lat_abs = jnp.abs(lon_rate), jnp.abs(lat_rate)
    east = jnp.where(lon_rate > 0, lon_abs, 0.0)
    north = jnp.where(lat_rate > 0, lat_abs, 0.0)
    return 1.0 - lon_abs - lat_abs, east, lon_abs - east, north, lat_abs - north


def regroup_kernel(
    field_ref, mask_ref, lon_ref, lat_ref, rows_ref, west_ref, east_ref, rates_ref, wait
):
    directions, lat, lon = field_ref.shape
    freqs = lon_ref.shape[0]
    rows = directions * lat
    height = rates_ref.shape[1]
    rows_ref[0:PAD, :] = jnp.zeros((PAD, lon), F32)
    rows_ref[PAD + rows :, :] = jnp.zeros((PAD, lon), F32)
    own = lax.broadcasted_iota(jnp.int32, (freqs, lon), 0) == lax.axis_index("freq")
    own = own.astype(F32)
    wait(2, 3)
    for at in range(0, height, directions):
        for slot, ref in enumerate((lon_ref, lat_ref)):
            rates_ref[slot, at : at + directions, :] = lax.dot_general(
                ref[...], own, (((0,), (0,)), ((), ())),
                precision=lax.Precision.HIGHEST, preferred_element_type=F32,
            )
    wait(0, 1)
    mask = mask_ref[...].astype(F32)
    for d in range(directions):
        rows_ref[pl.ds(PAD + d, lat, stride=directions), :] = field_ref[d].astype(F32) * mask
    edges = take_edges(rows_ref[PAD : PAD + rows, :].astype(BF16), edge_picks(lon, lon))
    west_ref[...] = edges[0:8].astype(BF16)
    east_ref[...] = edges[8:16].astype(BF16)


def interior_kernel(rows_ref, rates_ref, part_ref, rate_ref, *, directions):
    peers, height, lon = part_ref.shape
    center, east, west, north, south = split_rates(rates_ref[0], rates_ref[1])
    lane = lax.broadcasted_iota(jnp.int32, (height, lon), 1)
    rate_ref[...] = jnp.where(lane == 0, west, east)
    east = jnp.where(lane == lon - 1, 0.0, east)
    west = jnp.where(lane == 0, 0.0, west)
    for r in range(peers):
        at = PAD + r * height
        here = rows_ref[at : at + height, :]
        part_ref[r] = (
            center * here
            + east * pltpu.roll(here, lon - 1, 1)
            + west * pltpu.roll(here, 1, 1)
            + north * rows_ref[at + directions : at + directions + height, :]
            + south * rows_ref[at - directions : at - directions + height, :]
        )


def edges_kernel(part_ref, rate_ref, west_ref, east_ref, out_ref):
    peers, height, lon = part_ref.shape
    cols = put_edges(west_ref[...], east_ref[...], lon, lon)
    rate = rate_ref[...]
    for r in range(peers):
        out_ref[r] = (part_ref[r] + rate * cols[r * height : (r + 1) * height]).astype(BF16)


def spread_rates(courant_refs, turn_scr, rates_scr):
    freqs, directions = courant_refs[0].shape
    for slot, ref in enumerate(courant_refs):
        turn_scr[...] = jnp.zeros_like(turn_scr)
        turn_scr[0:freqs, 0:directions] = ref[...]
        turned = turn_scr[...].T
        for f in range(freqs):
            rates_scr[slot, f * directions : (f + 1) * directions, :] = jnp.broadcast_to(
                turned[0:directions, f : f + 1], (directions, rates_scr.shape[2])
            )


def spread_factor(kappa_ref, factor_scr):
    freqs, points = kappa_ref.shape
    directions = factor_scr.shape[0] // freqs
    for f in range(freqs):
        factor_scr[f * directions : (f + 1) * directions, :] = jnp.broadcast_to(
            kappa_ref[f : f + 1, :], (directions, points)
        )


def decay_of(factor, coeff):
    return 1.0 - step_weight * (factor * coeff)


def states_kernel(
    traj_ref, inter_ref, kappa_ref, coeff_ref, sed_ref,
    turned_ref, point_coeff_ref, next1_ref, next0_ref, low_ref, high_ref, west_ref, east_ref,
    factor_scr, product_scr, pull_scr, wait,
):
    steps, components, points = traj_ref.shape
    groups = coeff_ref.shape[1]
    lon = low_ref.shape[1]
    wait(2, 3, 4)
    sediment = sed_ref[...]
    hits = (lax.broadcasted_iota(jnp.int32, (groups, points), 0) == sediment).astype(F32)
    coeff = jnp.dot(
        jnp.broadcast_to(coeff_ref[...], (8, groups)), hits,
        precision=lax.Precision.HIGHEST, preferred_element_type=F32,
    )[0:1]
    point_coeff_ref[...] = coeff
    spread_factor(kappa_ref, factor_scr)
    wait(0, 1)
    turned_ref[...] = inter_ref[...].T
    chunk = components // 4
    for n, next_ref in ((0, next0_ref), (1, next1_ref)):
        state = traj_ref[n]
        squares = state * state
        for at in range(0, components, chunk):
            rows = slice(at, at + chunk)
            forced = jnp.dot(inter_ref[rows, :], squares, preferred_element_type=F32)
            here = traj_ref[n, rows, :].astype(F32)
            factor = factor_scr[rows, :]
            after = decay_of(factor, coeff) * here + step_weight * forced
            next_ref[rows, :] = after
            if n == 0:
                product_scr[rows, :] = (0.5 * factor * here * after).astype(BF16)
    product = product_scr[...]
    for at in range(0, components, chunk):
        rows = slice(at, at + chunk)
        pushed = jnp.dot(inter_ref[rows, :], product, preferred_element_type=F32)
        factor, here = factor_scr[rows, :], traj_ref[0, rows, :].astype(F32)
        pull = factor * (next0_ref[rows, :] + decay_of(factor, coeff) * here) + pushed
        pull_scr[rows, :] = pull.astype(BF16)
    extra = pull_scr.shape[0] - components
    first_row = lax.broadcasted_iota(jnp.int32, (extra, points), 0) == 0
    pull_scr[components:, :] = jnp.where(first_row, sediment.astype(F32), 0.0).astype(BF16)
    low_ref[...] = pull_scr[:, 0:lon]
    high_ref[...] = pull_scr[:, lon : 2 * lon]
    edges = take_edges(pull_scr[...], edge_picks(2 * lon, lon))
    west_ref[...] = edges[0:8].astype(BF16)
    east_ref[...] = edges[8:16].astype(BF16)


def fields_kernel(
    low_ref, high_ref, above_ref, below_ref, west_ref, east_ref, courant_lon_ref, courant_lat_ref,
    fields_ref, near_ref, turn_scr, rates_scr, wait,
):
    total, lon = low_ref.shape
    components = rates_scr.shape[1]
    cols = put_edges(west_ref[...], east_ref[...], 2 * lon, lon)
    wait(6, 7)
    spread_rates((courant_lon_ref, courant_lat_ref), turn_scr, rates_scr)
    near_ref[...] = jnp.zeros_like(near_ref)
    chunk = components // 8
    for at, size in [(i, chunk) for i in range(0, components, chunk)] + [(components, total - components)]:
        rows = slice(at, at + size)
        lane = lax.broadcasted_iota(jnp.int32, (size, lon), 1)
        low, high = low_ref[rows, :].astype(F32), high_ref[rows, :].astype(F32)
        above, below = above_ref[rows, :].astype(F32), below_ref[rows, :].astype(F32)
        if at < components:
            rates = split_rates(rates_scr[0, rows, :], rates_scr[1, rows, :])
        for half, (here, up, down) in enumerate(((low, high, below), (high, above, low))):
            lanes = slice(half * lon, (half + 1) * lon)
            edge = cols[rows, lanes]
            west = jnp.where(lane == 0, edge, pltpu.roll(here, 1, 1))
            east = jnp.where(lane == lon - 1, edge, pltpu.roll(here, lon - 1, 1))
            for slot, value in enumerate((here, west, east, down, up)):
                if at < components:
                    fields_ref[slot, rows, lanes] = (rates[slot] * value).astype(BF16)
                else:
                    near_ref[slot : slot + 1, lanes] = value[0:1]


def two_substeps(m_scr, r_scr, turned_ref, factor_scr, coeff, ready, write, weigh):
    components, points = m_scr.shape
    chunk = components // 4
    weights = jnp.zeros((8, points), F32)
    moved = r_scr[...]
    for at in range(0, components, chunk):
        rows = slice(at, at + chunk)
        pulled = jnp.dot(turned_ref[rows, :], moved, preferred_element_type=F32)
        after, state = ready(rows)
        factor, old = factor_scr[rows, :], m_scr[rows, :]
        new = decay_of(factor, coeff) * old + 0.5 * (after * pulled)
        if weigh:
            terms = factor * (old * after + new * state)
            weights = weights + terms.reshape(chunk // 8, 8, points).sum(axis=0)
        m_scr[rows, :] = new
        r_scr[rows, :] = new.astype(BF16)
    moved = r_scr[...]
    for at in range(0, components, chunk):
        rows = slice(at, at + chunk)
        pulled = jnp.dot(turned_ref[rows, :], moved, preferred_element_type=F32)
        state = ready(rows)[1]
        new = decay_of(factor_scr[rows, :], coeff) * m_scr[rows, :] + 0.5 * (state * pulled)
        write(rows, new)
    return weights


def first_kernel(
    moved_ref, turned_ref, kappa_ref, coeff_ref, mask_ref, near_ref, next_ref, traj_ref, fields_ref,
    low_ref, high_ref, west_ref, east_ref, sums_ref, m_scr, r_scr, factor_scr, wait,
):
    freqs, height, lon = moved_ref.shape
    points = 2 * lon
    directions = height // 2
    for f in range(freqs):
        block = moved_ref[f].astype(F32)
        rows = slice(f * directions, (f + 1) * directions)
        m_scr[rows, 0:lon] = block[0:directions]
        m_scr[rows, lon:points] = block[directions:height]
    r_scr[...] = m_scr[...].astype(BF16)
    wait(2)
    spread_factor(kappa_ref, factor_scr)
    wait(3, 4, 5, 6, 7, 8)
    mask = mask_ref[pl.ds(2 * lax.axis_index("freq"), 2), :].astype(F32)
    picks = edge_picks(points, lon)
    slots = fields_ref.shape[0]
    weights = [jnp.zeros((8, points), F32)] * slots

    def ready(rows):
        return next_ref[rows, :], traj_ref[rows, :].astype(F32)

    def write(rows, values):
        low = (values[:, 0:lon] * mask[0:1]).astype(BF16)
        high = (values[:, lon:points] * mask[1:2]).astype(BF16)
        low_ref[rows, :] = low
        high_ref[rows, :] = high
        next_ref[rows, 0:lon] = low.astype(F32)
        next_ref[rows, lon:points] = high.astype(F32)

    own = two_substeps(m_scr, r_scr, turned_ref, factor_scr, coeff_ref[...], ready, write, True)
    components = m_scr.shape[0]
    edges = take_edges(next_ref[...].astype(BF16), picks)
    west_ref[...] = edges[0:8].astype(BF16)
    east_ref[...] = edges[8:16].astype(BF16)
    chunk = components // 4
    for at in range(0, components, chunk):
        rows = slice(at, at + chunk)
        value = next_ref[rows, :]
        for slot in range(slots):
            terms = fields_ref[slot, rows, :].astype(F32) * value
            weights[slot] = weights[slot] + terms.reshape(chunk // 8, 8, points).sum(axis=0)
    weights[0] = weights[0] + own
    sums = jnp.zeros(sums_ref.shape[1:], F32)
    group = lax.broadcasted_iota(jnp.int32, (sums.shape[1], points), 0).astype(F32)
    for slot in range(slots):
        hits = (group == near_ref[slot : slot + 1, :]).astype(F32)
        sums = sums + lax.dot_general(
            weights[slot], hits, (((1,), (1,)), ((), ())),
            precision=lax.Precision.HIGHEST, preferred_element_type=F32,
        )
    sums_ref[...] = jnp.broadcast_to(sums[None], sums_ref.shape)


def second_kernel(
    low_ref, high_ref, north_ref, south_ref, west_ref, east_ref,
    turned_ref, kappa_ref, coeff_ref, next_ref, traj_ref, courant_lon_ref, courant_lat_ref,
    out_ref, m_scr, r_scr, factor_scr, turn_scr, rates_scr, wait,
):
    components, lon = low_ref.shape
    wait(11, 12)
    spread_rates((courant_lon_ref, courant_lat_ref), turn_scr, rates_scr)
    wait(7)
    spread_factor(kappa_ref, factor_scr)
    cols = put_edges(west_ref[...], east_ref[...], 2 * lon, lon)
    chunk = components // 8
    lane = lax.broadcasted_iota(jnp.int32, (chunk, lon), 1)
    for at in range(0, components, chunk):
        rows = slice(at, at + chunk)
        low, high = low_ref[rows, :].astype(F32), high_ref[rows, :].astype(F32)
        above, below = north_ref[rows, :].astype(F32), south_ref[rows, :].astype(F32)
        rates = split_rates(rates_scr[0, rows, :], rates_scr[1, rows, :])
        for half, (here, up, down) in enumerate(((low, high, below), (high, above, low))):
            lanes = slice(half * lon, (half + 1) * lon)
            edge = cols[rows, lanes]
            east = jnp.where(lane == lon - 1, edge, pltpu.roll(here, lon - 1, 1))
            west = jnp.where(lane == 0, edge, pltpu.roll(here, 1, 1))
            value = (
                rates[0] * here
                + rates[1] * east
                + rates[2] * west
                + rates[3] * up
                + rates[4] * down
            ).astype(BF16)
            r_scr[rows, lanes] = value
            m_scr[rows, lanes] = value.astype(F32)

    wait(8, 9, 10)

    def ready(rows):
        return next_ref[rows, :], traj_ref[rows, :].astype(F32)

    def write(rows, values):
        out_ref[rows, :] = values.astype(BF16)

    two_substeps(m_scr, r_scr, turned_ref, factor_scr, coeff_ref[...], ready, write, False)


def add_kernel(parts_ref, out_ref):
    out_ref[...] = jnp.broadcast_to(parts_ref[...].sum(axis=0)[None], out_ref.shape)


def final_kernel(scale, parts_ref, out_ref):
    total = parts_ref[...].sum(axis=0).sum(axis=0, keepdims=True)
    out_ref[...] = total[:, 0 : out_ref.shape[1]] * scale


def shards(
    adjoint_final, trajectory, interaction, friction_factor, friction_coeff,
    courant_lon, courant_lat, sea_mask, sediment,
):
    freq_local, directions, lat, lon = adjoint_final.shape
    steps, components, points = trajectory.shape
    groups = friction_coeff.shape[0]
    peers, regions = lax.axis_size("freq"), lax.axis_size("geo")
    rows = directions * lat
    height = rows // peers
    eastward = [(i, (i + 1) % regions) for i in range(regions)]
    westward = [(j, i) for i, j in eastward]
    northward = [(i, i + 1) for i in range(peers - 1)]
    southward = [(j, i) for i, j in northward]

    def swap(low, high, west, east):
        return (
            lax.ppermute(low, "freq", southward),
            lax.ppermute(high, "freq", northward),
            lax.ppermute(east, "geo", eastward),
            lax.ppermute(west, "geo", westward),
        )

    field = adjoint_final.reshape(directions, lat, lon)
    grouped, west, east, own_rates = call(
        regroup_kernel,
        [
            shape((rows + 2 * PAD, lon), F32),
            shape((8, rows), BF16),
            shape((8, rows), BF16),
            shape((2, height, lon), F32),
        ],
        [field, sea_mask, courant_lon, courant_lat],
        late={0: None, 1: None, 2: None, 3: None},
    )
    from_west = lax.ppermute(east, "geo", eastward)
    from_east = lax.ppermute(west, "geo", westward)
    part, rate = call(
        functools.partial(interior_kernel, directions=directions),
        [shape((peers, height, lon), F32), shape((height, lon), F32)],
        [grouped, own_rates],
    )
    (sent,) = call(
        edges_kernel, [shape((peers, height, lon), BF16)], [part, rate, from_west, from_east]
    )
    sent, trajectory, courant_lon, courant_lat = lax.optimization_barrier(
        (sent, trajectory, courant_lon, courant_lat)
    )
    moved = lax.all_to_all(sent, "freq", split_axis=0, concat_axis=0, tiled=True)

    product = 2 * components * components * points
    full, half_full = (components, points), (components, lon)
    tall = components + 16
    turned, coeff, next1, next0, *pulls = call(
        states_kernel,
        [
            shape((components, components), BF16),
            shape((1, points), F32),
            shape(full, F32),
            shape(full, F32),
            shape((tall, lon), BF16),
            shape((tall, lon), BF16),
            shape((8, tall), BF16),
            shape((8, tall), BF16),
        ],
        [
            trajectory, interaction, friction_factor, friction_coeff.reshape(1, groups),
            sediment.reshape(1, points),
        ],
        [pltpu.VMEM(full, F32), pltpu.VMEM(full, BF16), pltpu.VMEM((tall, points), BF16)],
        flops=3 * product,
        late={0: None, 1: None, 2: None, 3: None, 4: None},
    )

    spread = [pltpu.VMEM((128, 128), F32), pltpu.VMEM((2, *half_full), F32)]
    fields, near = call(
        fields_kernel,
        [shape((5, *full), BF16), shape((8, points), F32)],
        [pulls[0], pulls[1], *swap(*pulls), courant_lon, courant_lat],
        spread,
        late={6: None, 7: None},
    )
    carried = [pltpu.VMEM(full, F32), pltpu.VMEM(full, BF16), pltpu.VMEM(full, F32)]
    low, high, west, east, sums = call(
        first_kernel,
        [
            shape(half_full, BF16),
            shape(half_full, BF16),
            shape((8, components), BF16),
            shape((8, components), BF16),
            shape((peers, 8, 128), F32),
        ],
        [moved, turned, friction_factor, coeff, sea_mask, near, next1, trajectory, fields],
        carried,
        flops=2 * product,
        late={2: None, 3: None, 4: None, 5: None, 6: None, 7: 1, 8: None},
    )
    (result,) = call(
        second_kernel,
        [shape(full, BF16)],
        [
            low, high, *swap(low, high, west, east),
            turned, friction_factor, coeff, next0, trajectory, courant_lon, courant_lat,
        ],
        carried + spread,
        flops=2 * product,
        late={7: None, 8: None, 9: None, 10: 0, 11: None, 12: None},
    )
    sums = lax.all_to_all(sums, "freq", split_axis=0, concat_axis=0, tiled=True)
    (sums,) = call(add_kernel, [shape((regions, 8, 128), F32)], [sums])
    sums = lax.all_to_all(sums, "geo", split_axis=0, concat_axis=0, tiled=True)
    point_total = points * peers * regions
    scale = -step_weight * groups / (point_total * components)
    (total,) = call(functools.partial(final_kernel, scale), [shape((1, groups), F32)], [sums])
    return result, total.reshape(groups)


def solution(mesh):
    in_specs = (
        P("freq", None, None, "geo"),
        P(None, None, ("geo", "freq")),
        P(),
        P(None, ("geo", "freq")),
        P(),
        P(),
        P(),
        P(None, "geo"),
        P(("geo", "freq")),
    )
    out_specs = (P(None, ("geo", "freq")), P())
    return jax.shard_map(shards, mesh=mesh, in_specs=in_specs, out_specs=out_specs, check_vma=False)
```

time: 102 us -> 102 us (level)
  blocking collectives: 39.9 us -> 0 us
  starting transfers between devices: 27 us -> 63.1 us
  Pallas kernels: 11 us -> 24.5 us
  local copies, waits for them, and re-layouts: 15.2 us -> 6.12 us
    all_to_all x2 -> x0, blocking collectives: 39.9 us -> none  [the longest x1 23.3 us: shards(): sums = lax.all_to_all(sums, 'geo', split_axis=0, concat_axis=0, tiled=True)]
    all_to_all x0 -> x2, starting transfers between devices: none -> 25.7 us  [the longest x1 13 us: shards(): sums = lax.all_to_all(sums, 'freq', split_axis=0, concat_axis=0, tiled=True)]
    ppermute x2 -> x8, starting transfers between devices: 5.3 us -> 21.7 us  [the longest x2 8.77 us: swap(): lax.ppermute(high, 'freq', northward)]
    pallas_call x9, Pallas kernels: 11 us -> 24.5 us  [call(): pl.pallas_call(body, out_shape=outs, in_specs=[OUTSIDE if i in late else...]
    unnamed x42 -> x16, local copies, waits for them, and re-layouts: 15.2 us -> 6.12 us
    ppermute x2 -> x1, starting transfers between devices: 11 us -> 3.5 us  [shards(): from_west = lax.ppermute(east, 'geo', eastward)]
    all_to_all x0 -> x2, waiting for transfers between devices: none -> 5.54 us  [the longest x1 4.38 us: shards(): sums = lax.all_to_all(sums, 'freq', split_axis=0, concat_axis=0, tiled=True)]
    all_to_all x1, waiting for transfers between devices: 4.39 us -> 0.01 us  [shards(): lax.all_to_all(sent, 'freq', split_axis=0, concat_axis=0, tiled=True)]
  transfers between devices with their start and end apart: 7 -> 13, of which waited for: 3 -> 5; matrix products, arithmetic and copies ran while one was open for 1% -> 0% of each run, Pallas kernels for 3% -> 15%
where the time goes in v2:
time: 102 us; the launch traced here: 101 us
  starting transfers between devices  63.1 us (62%)
  Pallas kernels  24.5 us (24%)
  waiting for transfers between devices  6.57 us (6%)
  local copies, waits for them, and re-layouts  6.12 us (6%)
    pallas_call x9, Pallas kernels, call(): pl.pallas_call(body, out_shape=outs, in_specs=[OUTSIDE if i in late else...  24.5 us
    all_to_all x1, starting transfers between devices, shards(): sums = lax.all_to_all(sums, 'freq', split_axis=0, concat_axis=0, tiled=True)  13 us
    all_to_all x1, starting transfers between devices, shards(): sums = lax.all_to_all(sums, 'geo', split_axis=0, concat_axis=0, tiled=True)  12.7 us
    all_to_all x1, starting transfers between devices, shards(): lax.all_to_all(sent, 'freq', split_axis=0, concat_axis=0, tiled=True)  8.77 us
    ppermute x2, starting transfers between devices, swap(): lax.ppermute(high, 'freq', northward)  8.77 us
    ppermute x2, starting transfers between devices, swap(): lax.ppermute(west, 'geo', westward)  7.02 us
    unnamed x16, local copies, waits for them, and re-layouts  6.12 us
    all_to_all x1, waiting for transfers between devices, shards(): sums = lax.all_to_all(sums, 'freq', split_axis=0, concat_axis=0, tiled=True)  4.38 us
  transfers between devices with their start and end apart: 13, of which 5 were waited for; matrix products, arithmetic and copies ran while one was open for 0% of the time, Pallas kernels for 15%

profile of v2, /device:TPU:1, one launch (start us, length us, event | category | flops | bytes accessed | tf_op | source)
XLA Modules:
  0.0 101.1 jit_solution(7278904613682767639)
XLA Ops:
  0.6 1.7 %shard_map.104 = (f32[2384,128]{1,0:T(8,128)S(1)}, bf16[8,2304]{1,0:T(8,128)(2,1)S(1)}, bf16[8,2304]{1,0:T(8,128)(2,1)S(1)}, f32[2,72,128]{2,1,0:T(8,128)S(1)}) custom-call(bf16[36,64,128]{2,1,0:T(8,128)(2,1)} %bitcast.4, s32[64,128]{1,0:T(8,128)} %refs_4_.1, f32[32,36]{1,0:T(8,128)} %refs_11_, f32[32,36]{1,0:T(8,128)} %refs_12_), custom_call_target="tpu_custom_call" | custom-call | bytes 1999872 | tf_op jit(solution)/shard_map/pallas_call | solution.py:48
  2.3 3.5 %collective-permute-start = (bf16[8,2304]{1,0:T(8,128)(2,1)S(1)}, bf16[8,2304]{1,0:T(8,128)(2,1)S(1)}, u32[]{:S(2)}, u32[]{:S(2)}) collective-permute-start(bf16[8,2304]{1,0:T(8,128)(2,1)S(1)} %get-tuple-element.31), channel_id=1, source_target_pairs={{0,32},{32,64},{64,96},{96,128},{128,160},{160,192},{192,224},{224... | collective-permute-start | bytes 110600 | tf_op jit(solution)/shard_map/ppermute | solution.py:419
  5.8 3.4 %collective-permute-start.1 = (bf16[8,2304]{1,0:T(8,128)(2,1)S(1)}, bf16[8,2304]{1,0:T(8,128)(2,1)S(1)}, u32[]{:S(2)}, u32[]{:S(2)}) collective-permute-start(bf16[8,2304]{1,0:T(8,128)(2,1)S(1)} %get-tuple-element.32), channel_id=1, source_target_pairs={{32,0},{64,32},{96,64},{128,96},{160,128},{192,160},{224,192},{256... | collective-permute-start | bytes 110600 | tf_op jit(solution)/shard_map/ppermute | solution.py:420
  9.2 0.7 shard_map.105
  9.9 0.0 collective-permute-done.refs_2_
  9.9 0.2 collective-permute-done.1.refs_3_
  10.1 1.2 %shard_map.106 = bf16[32,72,128]{2,1,0:T(8,128)(2,1)} custom-call(f32[32,72,128]{2,1,0:T(8,128)S(1)} %get-tuple-element.29.refs_0_, f32[72,128]{1,0:T(8,128)S(1)} %get-tuple-element.30.refs_1_, bf16[8,2304]{1,0:T(8,128)(2,1)S(1)} %collective-permute-done.refs_2_, bf16[8,2304]{1,0:T(8,128)(2,1)S(1)} %collective-permute-done.1.refs_3_), custom_call_target="tpu_custom_call" | custom-call | bytes 1880064 | tf_op jit(solution)/shard_map/pallas_call | solution.py:48
  11.3 8.8 %all-to-all-start = ((bf16[32,72,128]{2,1,0:T(8,128)(2,1)}), bf16[32,72,128]{2,1,0:T(8,128)(2,1)S(1)}, u32[]{:S(2)}, u32[]{:S(2)}) async-start(bf16[32,72,128]{2,1,0:T(8,128)(2,1)} %shard_map.106), calls=%async_computation | async-start | bytes 1179648 | tf_op jit(solution)/shard_map/all_to_all | solution.py:432
  20.0 5.1 %shard_map.107 = (bf16[1152,1152]{1,0:T(8,128)(2,1)S(1)}, f32[1,256]{1,0:T(1,128)S(1)}, f32[1152,256]{1,0:T(8,128)S(1)}, f32[1152,256]{1,0:T(8,128)S(1)}, bf16[1...) custom-call(bf16[2,1152,256]{2,1,0:T(8,128)(2,1)} %refs_10_, ...), custom_call_target="tpu_custom_call" | custom-call | flops 2038431744 | bytes 9517824 | tf_op jit(solution)/shard_map/pallas_call | solution.py:48
  25.1 0.0 copy-start.1
  25.1 1.0 %copy-done.1 = f32[1152,256]{1,0:T(8,128)} copy-done((f32[1152,256]{1,0:T(8,128)}, f32[1152,256]{1,0:T(8,128)S(1)}, u32[]{:S(2)}) %copy-start.1) | copy-done | bytes 1179672
  26.2 0.0 copy-start.2
  26.2 1.0 %copy-done.2 = f32[1152,256]{1,0:T(8,128)} copy-done((f32[1152,256]{1,0:T(8,128)}, f32[1152,256]{1,0:T(8,128)S(1)}, u32[]{:S(2)}) %copy-start.2) | copy-done | bytes 1179672
  27.2 0.0 copy-start.5
  27.2 1.3 %collective-permute-start.2 = (bf16[1168,128]{1,0:T(8,128)(2,1)S(1)}, bf16[1168,128]{1,0:T(8,128)(2,1)S(1)}, u32[]{:S(2)}, u32[]{:S(2)}) collective-permute-start(bf16[1168,128]{1,0:T(8,128)(2,1)S(1)} %get-tuple-element.37.refs_0_), channel_id=1, source_target_pairs={{1,0},{2,1},{3,2},{4,3},{5,4},{6,5},{7,6},{8,7},{9,8},{10,9},{11,1... | collective-permute-start | bytes 897032 | tf_op jit(solution)/shard_map/ppermute | solution.py:401
  28.5 4.0 %collective-permute-start.3 = (bf16[1168,128]{1,0:T(8,128)(2,1)S(1)}, bf16[1168,128]{1,0:T(8,128)(2,1)S(1)}, u32[]{:S(2)}, u32[]{:S(2)}) collective-permute-start(bf16[1168,128]{1,0:T(8,128)(2,1)S(1)} %get-tuple-element.38.refs_1_), channel_id=1, source_target_pairs={{0,1},{1,2},{2,3},{3,4},{4,5},{5,6},{6,7},{7,8},{8,9},{9,10},{10,1... | collective-permute-start | bytes 897032 | tf_op jit(solution)/shard_map/ppermute | solution.py:402
  32.5 0.9 collective-permute-start.4
  33.4 4.8 %collective-permute-start.5 = (bf16[8,1168]{1,0:T(8,128)(2,1)S(1)}, bf16[8,1168]{1,0:T(8,128)(2,1)S(1)}, u32[]{:S(2)}, u32[]{:S(2)}) collective-permute-start(bf16[8,1168]{1,0:T(8,128)(2,1)S(1)} %get-tuple-element.40), channel_id=1, source_target_pairs={{32,0},{64,32},{96,64},{128,96},{160,128},{192,160},{224,192},{256... | collective-permute-start | bytes 56072 | tf_op jit(solution)/shard_map/ppermute | solution.py:404
  38.2 0.7 collective-permute-done.4.refs_4_
  38.8 0.2 collective-permute-done.5.refs_5_
  39.0 0.0 collective-permute-done.2.refs_2_
  39.0 0.0 copy-done.5
  39.0 0.0 collective-permute-done.3.refs_3_
  39.0 2.0 %shard_map.108 = (bf16[5,1152,256]{2,1,0:T(8,128)(2,1)S(1)}, f32[8,256]{1,0:T(8,128)S(1)}) custom-call(bf16[1168,128]{1,0:T(8,128)(2,1)S(1)} %get-tuple-element.37.refs_0_, bf16[1168,128]{1,0:T(8,128)(2,1)S(1)} %get-tuple-element.38.refs_1_, bf16[1168,128]{1,0:T(8,128)(2,1)S(1)} %collective-permute-done.2.refs_2_, ...), custom_call_target="tpu_custom_call" | custom-call | bytes 4199936 | tf_op jit(solution)/shard_map/pallas_call | solution.py:48
  41.1 0.0 copy-start
  41.1 1.6 %copy-done = bf16[5,1152,256]{2,1,0:T(8,128)(2,1)} copy-done((bf16[5,1152,256]{2,1,0:T(8,128)(2,1)}, bf16[5,1152,256]{2,1,0:T(8,128)(2,1)S(1)}, u32[]{:S(2)}) %copy-start) | copy-done | bytes 2949144
  42.7 0.6 copy-done.4
  43.3 0.0 all-to-all-done.refs_0_
  43.3 6.1 %shard_map.109 = (bf16[1152,128]{1,0:T(8,128)(2,1)S(1)}, bf16[1152,128]{1,0:T(8,128)(2,1)}, bf16[8,1152]{1,0:T(8,128)(2,1)S(1)}, bf16[8,1152]{1,0:T(8,128)(2,1)S(1)}, f32[32,8,128]{2,1,0:T(8,128)S(1)}) custom-call(bf16[32,72,128]{2,1,0:T(8,128)(2,1)S(1)} %all-to-all-done.refs_0_, bf16[1152,1152]{1,0:T(8,128)(2,1)S(1)} %get-tuple-element.35.refs_1_.refs_6_, ...), custom_call_target="tpu_custom_call" | custom-call | flops 1358954496 | bytes 9384960 | tf_op jit(solution)/shard_map/pallas_call | solution.py:48
  49.3 0.0 copy-start.3
  49.4 0.6 copy-done.3
  50.0 0.6 copy-done.6
  50.6 0.6 copy-done.7
  51.2 1.3 %collective-permute-start.6 = (bf16[1152,128]{1,0:T(8,128)(2,1)S(1)}, bf16[1152,128]{1,0:T(8,128)(2,1)S(1)}, u32[]{:S(2)}, u32[]{:S(2)}) collective-permute-start(bf16[1152,128]{1,0:T(8,128)(2,1)S(1)} %get-tuple-element.46.refs_0_), channel_id=1, source_target_pairs={{1,0},{2,1},{3,2},{4,3},{5,4},{6,5},{7,6},{8,7},{9,8},{10,9},{11,1... | collective-permute-start | bytes 884744 | tf_op jit(solution)/shard_map/ppermute | solution.py:401
  52.5 4.8 %collective-permute-start.7 = (bf16[1152,128]{1,0:T(8,128)(2,1)}, bf16[1152,128]{1,0:T(8,128)(2,1)}, u32[]{:S(2)}, u32[]{:S(2)}) collective-permute-start(bf16[1152,128]{1,0:T(8,128)(2,1)} %get-tuple-element.47.refs_1_), channel_id=1, source_target_pairs={{0,1},{1,2},{2,3},{3,4},{4,5},{5,6},{6,7},{7,8},{8,9},{9,10},{10,1... | collective-permute-start | bytes 884744 | tf_op jit(solution)/shard_map/ppermute | solution.py:402
  57.3 13.0 %all-to-all-start.1 = ((f32[32,8,128]{2,1,0:T(8,128)}), f32[32,8,128]{2,1,0:T(8,128)S(1)}, u32[]{:S(2)}, u32[]{:S(2)}) async-start(f32[32,8,128]{2,1,0:T(8,128)} %copy-done.3), calls=%async_computation.1 | async-start | bytes 262144 | tf_op jit(solution)/shard_map/all_to_all | solution.py:492
  70.2 2.5 %collective-permute-start.8 = (bf16[8,1152]{1,0:T(8,128)(2,1)}, bf16[8,1152]{1,0:T(8,128)(2,1)S(1)}, u32[]{:S(2)}, u32[]{:S(2)}) collective-permute-start(bf16[8,1152]{1,0:T(8,128)(2,1)} %copy-done.7), channel_id=1, source_target_pairs={{0,32},{32,64},{64,96},{96,128},{128,160},{160,192},{192,224},{224... | collective-permute-start | bytes 55304 | tf_op jit(solution)/shard_map/ppermute | solution.py:403
  72.7 2.2 %collective-permute-start.9 = (bf16[8,1152]{1,0:T(8,128)(2,1)}, bf16[8,1152]{1,0:T(8,128)(2,1)S(1)}, u32[]{:S(2)}, u32[]{:S(2)}) collective-permute-start(bf16[8,1152]{1,0:T(8,128)(2,1)} %copy-done.6), channel_id=1, source_target_pairs={{32,0},{64,32},{96,64},{128,96},{160,128},{192,160},{224,192},{256... | collective-permute-start | bytes 55304 | tf_op jit(solution)/shard_map/ppermute | solution.py:404
  74.9 4.4 %all-to-all-done.1.refs_0_ = f32[32,8,128]{2,1,0:T(8,128)S(1)} async-done(((f32[32,8,128]{2,1,0:T(8,128)}), f32[32,8,128]{2,1,0:T(8,128)S(1)}, u32[]{:S(2)}, u32[]{:S(2)}) %all-to-all-start.1) | async-done | bytes 131104 | tf_op jit(solution)/shard_map/all_to_all | solution.py:492
  79.3 0.7 shard_map.111
  80.0 12.7 %all-to-all-start.2 = ((f32[16,8,128]{2,1,0:T(8,128)}), f32[16,8,128]{2,1,0:T(8,128)S(1)}, u32[]{:S(2)}, u32[]{:S(2)}) async-start(f32[16,8,128]{2,1,0:T(8,128)} %shard_map.111), calls=%async_computation.2 | async-start | bytes 131072 | tf_op jit(solution)/shard_map/all_to_all | solution.py:494
  92.7 0.0 collective-permute-done.8.refs_4_
  92.7 0.0 collective-permute-done.9.refs_5_
  92.7 0.0 collective-permute-done.6.refs_2_
  92.7 0.0 collective-permute-done.7.refs_3_
  92.8 6.6 %shard_map.110 = bf16[1152,256]{1,0:T(8,128)(2,1)} custom-call(bf16[1152,128]{1,0:T(8,128)(2,1)S(1)} %get-tuple-element.46.refs_0_, bf16[1152,128]{1,0:T(8,128)(2,1)} %get-tuple-element.47.refs_1_, bf16[1152,128]{1,0:T(8,128)(2,1)S(1)} %collective-permute-done.6.refs_2_, bf16[1152,128]{1,0:T(8,128)(2,1)} %collective-permute-done.7.refs_3_, ...), custom_call_target="tpu_custom_call" | custom-call | flops 1358954496 | bytes 6862848 | tf_op jit(solution)/shard_map/pallas_call | solution.py:48
  99.4 1.2 %all-to-all-done.2.refs_0_ = f32[16,8,128]{2,1,0:T(8,128)S(1)} async-done(((f32[16,8,128]{2,1,0:T(8,128)}), f32[16,8,128]{2,1,0:T(8,128)S(1)}, u32[]{:S(2)}, u32[]{:S(2)}) %all-to-all-start.2) | async-done | bytes 65568 | tf_op jit(solution)/shard_map/all_to_all | solution.py:494
  100.5 0.5 shard_map.112
  (3 shorter events, 0.0 us)
Async XLA Ops:
  2.3 7.6 %collective-permute-start = (bf16[8,2304]{1,0:T(8,128)(2,1)S(1)}, bf16[8,2304]{1,0:T(8,128)(2,1)S(1)}, u32[]{:S(2)}, u32[]{:S(2)}) collective-permute-start(bf16[8,2304]{1,0:T(8,128)(2,1)S(1)} %get-tuple-element.31), channel_id=1, source_target_pairs={{0,32},{32,64},{64,96},{96,128},{128,160},{160,192},{192,224},{224... | collective-permute-start | bytes 110600 | tf_op jit(solution)/shard_map/ppermute | solution.py:419
  5.8 4.3 %collective-permute-start.1 = (bf16[8,2304]{1,0:T(8,128)(2,1)S(1)}, bf16[8,2304]{1,0:T(8,128)(2,1)S(1)}, u32[]{:S(2)}, u32[]{:S(2)}) collective-permute-start(bf16[8,2304]{1,0:T(8,128)(2,1)S(1)} %get-tuple-element.32), channel_id=1, source_target_pairs={{32,0},{64,32},{96,64},{128,96},{160,128},{192,160},{224,192},{256... | collective-permute-start | bytes 110600 | tf_op jit(solution)/shard_map/ppermute | solution.py:420
  11.3 32.0 %all-to-all-start = ((bf16[32,72,128]{2,1,0:T(8,128)(2,1)}), bf16[32,72,128]{2,1,0:T(8,128)(2,1)S(1)}, u32[]{:S(2)}, u32[]{:S(2)}) async-start(bf16[32,72,128]{2,1,0:T(8,128)(2,1)} %shard_map.106), calls=%async_computation | async-start | bytes 1179648 | tf_op jit(solution)/shard_map/all_to_all | solution.py:432
  25.1 1.0 %copy-start.1 = (f32[1152,256]{1,0:T(8,128)}, f32[1152,256]{1,0:T(8,128)S(1)}, u32[]{:S(2)}) copy-start(f32[1152,256]{1,0:T(8,128)S(1)} %get-tuple-element.50.refs_9_) | copy-start | bytes 3538948
  26.2 1.1 %copy-start.2 = (f32[1152,256]{1,0:T(8,128)}, f32[1152,256]{1,0:T(8,128)S(1)}, u32[]{:S(2)}) copy-start(f32[1152,256]{1,0:T(8,128)S(1)} %get-tuple-element.44.refs_6_) | copy-start | bytes 3538948
  27.2 11.8 %copy-start.5 = (f32[1,256]{1,0:T(1,128)}, f32[1,256]{1,0:T(1,128)S(1)}, u32[]{:S(2)}) copy-start(f32[1,256]{1,0:T(1,128)S(1)} %get-tuple-element.36.refs_3_.refs_8_) | copy-start | bytes 3076
  27.2 11.8 %collective-permute-start.2 = (bf16[1168,128]{1,0:T(8,128)(2,1)S(1)}, bf16[1168,128]{1,0:T(8,128)(2,1)S(1)}, u32[]{:S(2)}, u32[]{:S(2)}) collective-permute-start(bf16[1168,128]{1,0:T(8,128)(2,1)S(1)} %get-tuple-element.37.refs_0_), channel_id=1, source_target_pairs={{1,0},{2,1},{3,2},{4,3},{5,4},{6,5},{7,6},{8,7},{9,8},{10,9},{11,1... | collective-permute-start | bytes 897032 | tf_op jit(solution)/shard_map/ppermute | solution.py:401
  28.5 10.5 %collective-permute-start.3 = (bf16[1168,128]{1,0:T(8,128)(2,1)S(1)}, bf16[1168,128]{1,0:T(8,128)(2,1)S(1)}, u32[]{:S(2)}, u32[]{:S(2)}) collective-permute-start(bf16[1168,128]{1,0:T(8,128)(2,1)S(1)} %get-tuple-element.38.refs_1_), channel_id=1, source_target_pairs={{0,1},{1,2},{2,3},{3,4},{4,5},{5,6},{6,7},{7,8},{8,9},{9,10},{10,1... | collective-permute-start | bytes 897032 | tf_op jit(solution)/shard_map/ppermute | solution.py:402
  32.5 6.3 %collective-permute-start.4 = (bf16[8,1168]{1,0:T(8,128)(2,1)S(1)}, bf16[8,1168]{1,0:T(8,128)(2,1)S(1)}, u32[]{:S(2)}, u32[]{:S(2)}) collective-permute-start(bf16[8,1168]{1,0:T(8,128)(2,1)S(1)} %get-tuple-element.39), channel_id=1, source_target_pairs={{0,32},{32,64},{64,96},{96,128},{128,160},{160,192},{192,224},{224... | collective-permute-start | bytes 56072 | tf_op jit(solution)/shard_map/ppermute | solution.py:403
  33.4 5.6 %collective-permute-start.5 = (bf16[8,1168]{1,0:T(8,128)(2,1)S(1)}, bf16[8,1168]{1,0:T(8,128)(2,1)S(1)}, u32[]{:S(2)}, u32[]{:S(2)}) collective-permute-start(bf16[8,1168]{1,0:T(8,128)(2,1)S(1)} %get-tuple-element.40), channel_id=1, source_target_pairs={{32,0},{64,32},{96,64},{128,96},{160,128},{192,160},{224,192},{256... | collective-permute-start | bytes 56072 | tf_op jit(solution)/shard_map/ppermute | solution.py:404
  41.1 1.6 %copy-start = (bf16[5,1152,256]{2,1,0:T(8,128)(2,1)}, bf16[5,1152,256]{2,1,0:T(8,128)(2,1)S(1)}, u32[]{:S(2)}) copy-start(bf16[5,1152,256]{2,1,0:T(8,128)(2,1)S(1)} %get-tuple-element.45.refs_8_) | copy-start | bytes 8847364
  42.7 0.6 copy-start.4
  49.3 0.7 copy-start.3
  50.0 0.6 copy-start.6
  50.6 0.6 copy-start.7
  51.2 41.5 %collective-permute-start.6 = (bf16[1152,128]{1,0:T(8,128)(2,1)S(1)}, bf16[1152,128]{1,0:T(8,128)(2,1)S(1)}, u32[]{:S(2)}, u32[]{:S(2)}) collective-permute-start(bf16[1152,128]{1,0:T(8,128)(2,1)S(1)} %get-tuple-element.46.refs_0_), channel_id=1, source_target_pairs={{1,0},{2,1},{3,2},{4,3},{5,4},{6,5},{7,6},{8,7},{9,8},{10,9},{11,1... | collective-permute-start | bytes 884744 | tf_op jit(solution)/shard_map/ppermute | solution.py:401
  52.5 40.2 %collective-permute-start.7 = (bf16[1152,128]{1,0:T(8,128)(2,1)}, bf16[1152,128]{1,0:T(8,128)(2,1)}, u32[]{:S(2)}, u32[]{:S(2)}) collective-permute-start(bf16[1152,128]{1,0:T(8,128)(2,1)} %get-tuple-element.47.refs_1_), channel_id=1, source_target_pairs={{0,1},{1,2},{2,3},{3,4},{4,5},{5,6},{6,7},{7,8},{8,9},{9,10},{10,1... | collective-permute-start | bytes 884744 | tf_op jit(solution)/shard_map/ppermute | solution.py:402
  57.3 22.1 %all-to-all-start.1 = ((f32[32,8,128]{2,1,0:T(8,128)}), f32[32,8,128]{2,1,0:T(8,128)S(1)}, u32[]{:S(2)}, u32[]{:S(2)}) async-start(f32[32,8,128]{2,1,0:T(8,128)} %copy-done.3), calls=%async_computation.1 | async-start | bytes 262144 | tf_op jit(solution)/shard_map/all_to_all | solution.py:492
  70.2 22.5 %collective-permute-start.8 = (bf16[8,1152]{1,0:T(8,128)(2,1)}, bf16[8,1152]{1,0:T(8,128)(2,1)S(1)}, u32[]{:S(2)}, u32[]{:S(2)}) collective-permute-start(bf16[8,1152]{1,0:T(8,128)(2,1)} %copy-done.7), channel_id=1, source_target_pairs={{0,32},{32,64},{64,96},{96,128},{128,160},{160,192},{192,224},{224... | collective-permute-start | bytes 55304 | tf_op jit(solution)/shard_map/ppermute | solution.py:403
  72.7 20.0 %collective-permute-start.9 = (bf16[8,1152]{1,0:T(8,128)(2,1)}, bf16[8,1152]{1,0:T(8,128)(2,1)S(1)}, u32[]{:S(2)}, u32[]{:S(2)}) collective-permute-start(bf16[8,1152]{1,0:T(8,128)(2,1)} %copy-done.6), channel_id=1, source_target_pairs={{32,0},{64,32},{96,64},{128,96},{160,128},{192,160},{224,192},{256... | collective-permute-start | bytes 55304 | tf_op jit(solution)/shard_map/ppermute | solution.py:404
  80.0 20.5 %all-to-all-start.2 = ((f32[16,8,128]{2,1,0:T(8,128)}), f32[16,8,128]{2,1,0:T(8,128)S(1)}, u32[]{:S(2)}, u32[]{:S(2)}) async-start(f32[16,8,128]{2,1,0:T(8,128)} %shard_map.111), calls=%async_computation.2 | async-start | bytes 131072 | tf_op jit(solution)/shard_map/all_to_all | solution.py:494

commit v3 on v2

--- a/solution.py
+++ b/solution.py
@@ -1,4 +1,5 @@
 import functools
+import math
 
 import jax
 import jax.numpy as jnp
@@ -16,7 +17,7 @@
 OUTSIDE = pl.BlockSpec(memory_space=pl.ANY)
 
 
-def call(kernel, outs, args, scratch=(), flops=0, late=None, limit=32):
+def call(kernel, outs, args, scratch=(), flops=0, late=None, outside=(), limit=32):
     late = {} if late is None else late
     places = sorted(late)
     size = sum(a.size * a.dtype.itemsize for a in (*args, *outs))
@@ -32,8 +33,9 @@
         for k, i in enumerate(places):
             source = given[i] if late[i] is None else given[i].at[late[i]]
             copies[i] = pltpu.make_async_copy(source, buffers[k], buffers[-1].at[k])
+            given[i] = buffers[k]
+        for i in sorted(places, key=lambda i: math.prod(given[i].shape)):
             copies[i].start()
-            given[i] = buffers[k]
         if places:
             kernel(*given, *kept, wait=lambda *which: [copies[i].wait() for i in which])
         else:
@@ -48,7 +50,7 @@
     return pl.pallas_call(
         body,
         out_shape=outs,
-        in_specs=[OUTSIDE if i in late else WHOLE for i in range(len(args))],
+        in_specs=[OUTSIDE if i in late or i in outside else WHOLE for i in range(len(args))],
         out_specs=[WHOLE] * len(outs),
         scratch_shapes=[*scratch, *buffers],
         compiler_params=pltpu.CompilerParams(vmem_limit_bytes=limit * MIB),
@@ -75,9 +77,10 @@
 
 
 def put_edges(from_west, from_east, width, lon):
-    both = jnp.concatenate([from_west.astype(F32), from_east.astype(F32)], axis=0).astype(BF16)
+    both = jnp.concatenate([from_west.astype(F32)[8:16], from_east.astype(F32)[0:8]], axis=0)
     return lax.dot_general(
-        both, edge_picks(width, lon), (((0,), (0,)), ((), ())), preferred_element_type=F32
+        both.astype(BF16), edge_picks(width, lon), (((0,), (0,)), ((), ())),
+        preferred_element_type=F32,
     )
 
 
@@ -89,7 +92,7 @@
 
 
 def regroup_kernel(
-    field_ref, mask_ref, lon_ref, lat_ref, rows_ref, west_ref, east_ref, rates_ref, wait
+    field_ref, mask_ref, lon_ref, lat_ref, rows_ref, edge_ref, rates_ref, wait
 ):
     directions, lat, lon = field_ref.shape
     freqs = lon_ref.shape[0]
@@ -111,8 +114,7 @@
     for d in range(directions):
         rows_ref[pl.ds(PAD + d, lat, stride=directions), :] = field_ref[d].astype(F32) * mask
     edges = take_edges(rows_ref[PAD : PAD + rows, :].astype(BF16), edge_picks(lon, lon))
-    west_ref[...] = edges[0:8].astype(BF16)
-    east_ref[...] = edges[8:16].astype(BF16)
+    edge_ref[...] = edges.astype(BF16)
 
 
 def interior_kernel(rows_ref, rates_ref, part_ref, rate_ref, *, directions):
@@ -167,14 +169,36 @@
     return 1.0 - step_weight * (factor * coeff)
 
 
-def states_kernel(
-    traj_ref, inter_ref, kappa_ref, coeff_ref, sed_ref,
-    turned_ref, point_coeff_ref, next1_ref, next0_ref, low_ref, high_ref, west_ref, east_ref,
-    factor_scr, product_scr, pull_scr, wait,
-):
-    steps, components, points = traj_ref.shape
+def forward(state_ref, inter_ref, factor_scr, coeff, rows):
+    forced = jnp.dot(inter_ref[rows, :], square_of(state_ref), preferred_element_type=F32)
+    here = state_ref[rows, :].astype(F32)
+    return here, decay_of(factor_scr[rows, :], coeff) * here + step_weight * forced
+
+
+def square_of(state_ref):
+    state = state_ref[...]
+    return state * state
+
+
+def blocks_of(size, count):
+    return [slice(at, at + size // count) for at in range(0, size, size // count)]
+
+
+def pull_kernel(
+    traj_ref, inter_any, kappa_ref, coeff_ref, sed_ref,
+    point_coeff_ref, next_ref, low_ref, high_ref, edge_ref,
+    factor_scr, product_scr, pull_scr, inter_ref, sems, wait,
+):
+    components, points = traj_ref.shape
     groups = coeff_ref.shape[1]
     lon = low_ref.shape[1]
+    blocks = blocks_of(components, 4)
+    copies = [
+        pltpu.make_async_copy(inter_any.at[rows, :], inter_ref.at[rows, :], sems.at[i])
+        for i, rows in enumerate(blocks)
+    ]
+    for copy in copies:
+        copy.start()
     wait(2, 3, 4)
     sediment = sed_ref[...]
     hits = (lax.broadcasted_iota(jnp.int32, (groups, points), 0) == sediment).astype(F32)
@@ -184,66 +208,84 @@
     )[0:1]
     point_coeff_ref[...] = coeff
     spread_factor(kappa_ref, factor_scr)
-    wait(0, 1)
-    turned_ref[...] = inter_ref[...].T
-    chunk = components // 4
-    for n, next_ref in ((0, next0_ref), (1, next1_ref)):
-        state = traj_ref[n]
-        squares = state * state
-        for at in range(0, components, chunk):
-            rows = slice(at, at + chunk)
-            forced = jnp.dot(inter_ref[rows, :], squares, preferred_element_type=F32)
-            here = traj_ref[n, rows, :].astype(F32)
-            factor = factor_scr[rows, :]
-            after = decay_of(factor, coeff) * here + step_weight * forced
-            next_ref[rows, :] = after
-            if n == 0:
-                product_scr[rows, :] = (0.5 * factor * here * after).astype(BF16)
+    wait(0)
+    for copy, rows in zip(copies, blocks):
+        copy.wait()
+        here, after = forward(traj_ref, inter_ref, factor_scr, coeff, rows)
+        next_ref[rows, :] = after
+        product_scr[rows, :] = (0.5 * factor_scr[rows, :] * here * after).astype(BF16)
     product = product_scr[...]
-    for at in range(0, components, chunk):
-        rows = slice(at, at + chunk)
+    for rows in blocks:
         pushed = jnp.dot(inter_ref[rows, :], product, preferred_element_type=F32)
-        factor, here = factor_scr[rows, :], traj_ref[0, rows, :].astype(F32)
-        pull = factor * (next0_ref[rows, :] + decay_of(factor, coeff) * here) + pushed
+        factor, here = factor_scr[rows, :], traj_ref[rows, :].astype(F32)
+        pull = factor * (next_ref[rows, :] + decay_of(factor, coeff) * here) + pushed
         pull_scr[rows, :] = pull.astype(BF16)
     extra = pull_scr.shape[0] - components
     first_row = lax.broadcasted_iota(jnp.int32, (extra, points), 0) == 0
     pull_scr[components:, :] = jnp.where(first_row, sediment.astype(F32), 0.0).astype(BF16)
     low_ref[...] = pull_scr[:, 0:lon]
     high_ref[...] = pull_scr[:, lon : 2 * lon]
-    edges = take_edges(pull_scr[...], edge_picks(2 * lon, lon))
-    west_ref[...] = edges[0:8].astype(BF16)
-    east_ref[...] = edges[8:16].astype(BF16)
-
-
-def fields_kernel(
-    low_ref, high_ref, above_ref, below_ref, west_ref, east_ref, courant_lon_ref, courant_lat_ref,
-    fields_ref, near_ref, turn_scr, rates_scr, wait,
-):
-    total, lon = low_ref.shape
-    components = rates_scr.shape[1]
+    edge_ref[...] = take_edges(pull_scr[...], edge_picks(2 * lon, lon)).astype(BF16)
+
+
+def states_kernel(
+    traj_ref, inter_ref, kappa_ref, coeff_ref, turned_ref, next_ref, factor_scr, wait
+):
+    components = traj_ref.shape[0]
+    wait(2, 3)
+    spread_factor(kappa_ref, factor_scr)
+    wait(0, 1)
+    coeff = coeff_ref[...]
+    turned_ref[...] = inter_ref[...].T
+    for rows in blocks_of(components, 4):
+        next_ref[rows, :] = forward(traj_ref, inter_ref, factor_scr, coeff, rows)[1]
+
+
+def sums_kernel(
+    low_ref, high_ref, pull_low_ref, pull_high_ref, above_ref, below_ref, west_ref, east_ref,
+    courant_lon_ref, courant_lat_ref, own_ref, sums_ref, turn_scr, rates_scr, wait,
+):
+    components, lon = low_ref.shape
+    total = components + 16
+    wait(8, 9)
+    spread_rates((courant_lon_ref, courant_lat_ref), turn_scr, rates_scr)
+    wait(6, 7)
     cols = put_edges(west_ref[...], east_ref[...], 2 * lon, lon)
-    wait(6, 7)
-    spread_rates((courant_lon_ref, courant_lat_ref), turn_scr, rates_scr)
-    near_ref[...] = jnp.zeros_like(near_ref)
-    chunk = components // 8
-    for at, size in [(i, chunk) for i in range(0, components, chunk)] + [(components, total - components)]:
-        rows = slice(at, at + size)
+    wait(2, 3, 4, 5)
+    weights = [[jnp.zeros((8, lon), F32)] * 5 for _ in range(2)]
+    weights[0][0], weights[1][0] = own_ref[:, 0:lon], own_ref[:, lon : 2 * lon]
+    near = [[None] * 5, [None] * 5]
+    for rows in [*blocks_of(components, components // 144), slice(components, total)]:
+        size = rows.stop - rows.start
         lane = lax.broadcasted_iota(jnp.int32, (size, lon), 1)
-        low, high = low_ref[rows, :].astype(F32), high_ref[rows, :].astype(F32)
+        low, high = pull_low_ref[rows, :].astype(F32), pull_high_ref[rows, :].astype(F32)
         above, below = above_ref[rows, :].astype(F32), below_ref[rows, :].astype(F32)
-        if at < components:
+        if rows.start < components:
             rates = split_rates(rates_scr[0, rows, :], rates_scr[1, rows, :])
-        for half, (here, up, down) in enumerate(((low, high, below), (high, above, low))):
-            lanes = slice(half * lon, (half + 1) * lon)
-            edge = cols[rows, lanes]
+        for half, (here, up, down, field) in enumerate(
+            ((low, high, below, low_ref), (high, above, low, high_ref))
+        ):
+            edge = cols[rows, half * lon : (half + 1) * lon]
             west = jnp.where(lane == 0, edge, pltpu.roll(here, 1, 1))
             east = jnp.where(lane == lon - 1, edge, pltpu.roll(here, lon - 1, 1))
-            for slot, value in enumerate((here, west, east, down, up)):
-                if at < components:
-                    fields_ref[slot, rows, lanes] = (rates[slot] * value).astype(BF16)
-                else:
-                    near_ref[slot : slot + 1, lanes] = value[0:1]
+            reached = (here, west, east, down, up)
+            if rows.start == components:
+                near[half] = [value[0:1] for value in reached]
+                continue
+            masked = field[rows, :].astype(F32)
+            for slot, value in enumerate(reached):
+                terms = (rates[slot] * value * masked).reshape(size // 8, 8, lon)
+                weights[half][slot] = weights[half][slot] + terms.sum(axis=0)
+    sums = jnp.zeros(sums_ref.shape[1:], F32)
+    group = lax.broadcasted_iota(jnp.int32, (sums.shape[1], lon), 0).astype(F32)
+    for half in range(2):
+        for slot in range(5):
+            hits = (group == near[half][slot]).astype(F32)
+            sums = sums + lax.dot_general(
+                weights[half][slot], hits, (((1,), (1,)), ((), ())),
+                precision=lax.Precision.HIGHEST, preferred_element_type=F32,
+            )
+    sums_ref[...] = jnp.broadcast_to(sums[None], sums_ref.shape)
 
 
 def two_substeps(m_scr, r_scr, turned_ref, factor_scr, coeff, ready, write, weigh):
@@ -273,8 +315,8 @@
 
 
 def first_kernel(
-    moved_ref, turned_ref, kappa_ref, coeff_ref, mask_ref, near_ref, next_ref, traj_ref, fields_ref,
-    low_ref, high_ref, west_ref, east_ref, sums_ref, m_scr, r_scr, factor_scr, wait,
+    moved_ref, turned_ref, kappa_ref, coeff_ref, mask_ref, next_ref, traj_ref,
+    low_ref, high_ref, edge_ref, weights_ref, m_scr, r_scr, factor_scr, wait,
 ):
     freqs, height, lon = moved_ref.shape
     points = 2 * lon
@@ -285,13 +327,10 @@
         m_scr[rows, 0:lon] = block[0:directions]
         m_scr[rows, lon:points] = block[directions:height]
     r_scr[...] = m_scr[...].astype(BF16)
-    wait(2)
+    wait(2, 3, 4)
     spread_factor(kappa_ref, factor_scr)
-    wait(3, 4, 5, 6, 7, 8)
     mask = mask_ref[pl.ds(2 * lax.axis_index("freq"), 2), :].astype(F32)
-    picks = edge_picks(points, lon)
-    slots = fields_ref.shape[0]
-    weights = [jnp.zeros((8, points), F32)] * slots
+    wait(5, 6)
 
     def ready(rows):
         return next_ref[rows, :], traj_ref[rows, :].astype(F32)
@@ -301,31 +340,13 @@
         high = (values[:, lon:points] * mask[1:2]).astype(BF16)
         low_ref[rows, :] = low
         high_ref[rows, :] = high
-        next_ref[rows, 0:lon] = low.astype(F32)
-        next_ref[rows, lon:points] = high.astype(F32)
-
-    own = two_substeps(m_scr, r_scr, turned_ref, factor_scr, coeff_ref[...], ready, write, True)
-    components = m_scr.shape[0]
-    edges = take_edges(next_ref[...].astype(BF16), picks)
-    west_ref[...] = edges[0:8].astype(BF16)
-    east_ref[...] = edges[8:16].astype(BF16)
-    chunk = components // 4
-    for at in range(0, components, chunk):
-        rows = slice(at, at + chunk)
-        value = next_ref[rows, :]
-        for slot in range(slots):
-            terms = fields_ref[slot, rows, :].astype(F32) * value
-            weights[slot] = weights[slot] + terms.reshape(chunk // 8, 8, points).sum(axis=0)
-    weights[0] = weights[0] + own
-    sums = jnp.zeros(sums_ref.shape[1:], F32)
-    group = lax.broadcasted_iota(jnp.int32, (sums.shape[1], points), 0).astype(F32)
-    for slot in range(slots):
-        hits = (group == near_ref[slot : slot + 1, :]).astype(F32)
-        sums = sums + lax.dot_general(
-            weights[slot], hits, (((1,), (1,)), ((), ())),
-            precision=lax.Precision.HIGHEST, preferred_element_type=F32,
-        )
-    sums_ref[...] = jnp.broadcast_to(sums[None], sums_ref.shape)
+
+    weights_ref[...] = two_substeps(
+        m_scr, r_scr, turned_ref, factor_scr, coeff_ref[...], ready, write, True
+    )
+    picks = edge_picks(points, lon)
+    edges = take_edges(low_ref[...], picks[:, 0:lon]) + take_edges(high_ref[...], picks[:, lon:points])
+    edge_ref[...] = edges.astype(BF16)
 
 
 def second_kernel(
@@ -396,28 +417,23 @@
     northward = [(i, i + 1) for i in range(peers - 1)]
     southward = [(j, i) for i, j in northward]
 
-    def swap(low, high, west, east):
+    def swap(low, high, edges):
         return (
             lax.ppermute(low, "freq", southward),
             lax.ppermute(high, "freq", northward),
-            lax.ppermute(east, "geo", eastward),
-            lax.ppermute(west, "geo", westward),
+            lax.ppermute(edges, "geo", eastward),
+            lax.ppermute(edges, "geo", westward),
         )
 
     field = adjoint_final.reshape(directions, lat, lon)
-    grouped, west, east, own_rates = call(
+    grouped, edges, own_rates = call(
         regroup_kernel,
-        [
-            shape((rows + 2 * PAD, lon), F32),
-            shape((8, rows), BF16),
-            shape((8, rows), BF16),
-            shape((2, height, lon), F32),
-        ],
+        [shape((rows + 2 * PAD, lon), F32), shape((16, rows), BF16), shape((2, height, lon), F32)],
         [field, sea_mask, courant_lon, courant_lat],
         late={0: None, 1: None, 2: None, 3: None},
     )
-    from_west = lax.ppermute(east, "geo", eastward)
-    from_east = lax.ppermute(west, "geo", westward)
+    from_west = lax.ppermute(edges, "geo", eastward)
+    from_east = lax.ppermute(edges, "geo", westward)
     part, rate = call(
         functools.partial(interior_kernel, directions=directions),
         [shape((peers, height, lon), F32), shape((height, lon), F32)],
@@ -426,63 +442,73 @@
     (sent,) = call(
         edges_kernel, [shape((peers, height, lon), BF16)], [part, rate, from_west, from_east]
     )
-    sent, trajectory, courant_lon, courant_lat = lax.optimization_barrier(
-        (sent, trajectory, courant_lon, courant_lat)
-    )
+    sent, trajectory = lax.optimization_barrier((sent, trajectory))
     moved = lax.all_to_all(sent, "freq", split_axis=0, concat_axis=0, tiled=True)
 
     product = 2 * components * components * points
     full, half_full = (components, points), (components, lon)
     tall = components + 16
-    turned, coeff, next1, next0, *pulls = call(
-        states_kernel,
+    coeff, next0, pull_low, pull_high, pull_edges = call(
+        pull_kernel,
         [
-            shape((components, components), BF16),
             shape((1, points), F32),
-            shape(full, F32),
             shape(full, F32),
             shape((tall, lon), BF16),
             shape((tall, lon), BF16),
-            shape((8, tall), BF16),
-            shape((8, tall), BF16),
+            shape((16, tall), BF16),
         ],
         [
-            trajectory, interaction, friction_factor, friction_coeff.reshape(1, groups),
-            sediment.reshape(1, points),
+            trajectory, pltpu.with_memory_space_constraint(interaction, pltpu.HBM),
+            friction_factor, friction_coeff.reshape(1, groups), sediment.reshape(1, points),
         ],
-        [pltpu.VMEM(full, F32), pltpu.VMEM(full, BF16), pltpu.VMEM((tall, points), BF16)],
-        flops=3 * product,
-        late={0: None, 1: None, 2: None, 3: None, 4: None},
-    )
-
+        [
+            pltpu.VMEM(full, F32), pltpu.VMEM(full, BF16), pltpu.VMEM((tall, points), BF16),
+            pltpu.VMEM((components, components), BF16), pltpu.SemaphoreType.DMA((4,)),
+        ],
+        flops=2 * product,
+        late={0: 0, 2: None, 3: None, 4: None},
+        outside=(1,),
+    )
+    pulls = swap(pull_low, pull_high, pull_edges)
+    turned, next1 = call(
+        states_kernel,
+        [shape((components, components), BF16), shape(full, F32)],
+        [trajectory, interaction, friction_factor, coeff],
+        [pltpu.VMEM(full, F32)],
+        flops=product,
+        late={0: 1, 1: None, 2: None, 3: None},
+    )
+    moved, *pulls = lax.optimization_barrier((moved, *pulls))
+    carried = [pltpu.VMEM(full, F32), pltpu.VMEM(full, BF16), pltpu.VMEM(full, F32)]
     spread = [pltpu.VMEM((128, 128), F32), pltpu.VMEM((2, *half_full), F32)]
-    fields, near = call(
-        fields_kernel,
-        [shape((5, *full), BF16), shape((8, points), F32)],
-        [pulls[0], pulls[1], *swap(*pulls), courant_lon, courant_lat],
-        spread,
-        late={6: None, 7: None},
-    )
-    carried = [pltpu.VMEM(full, F32), pltpu.VMEM(full, BF16), pltpu.VMEM(full, F32)]
-    low, high, west, east, sums = call(
+    low, high, edges, weights = call(
         first_kernel,
         [
             shape(half_full, BF16),
             shape(half_full, BF16),
-            shape((8, components), BF16),
-            shape((8, components), BF16),
-            shape((peers, 8, 128), F32),
+            shape((16, components), BF16),
+            shape((8, points), F32),
         ],
-        [moved, turned, friction_factor, coeff, sea_mask, near, next1, trajectory, fields],
+        [moved, turned, friction_factor, coeff, sea_mask, next1, trajectory],
         carried,
         flops=2 * product,
-        late={2: None, 3: None, 4: None, 5: None, 6: None, 7: 1, 8: None},
-    )
+        late={2: None, 3: None, 4: None, 5: None, 6: 1},
+    )
+    swapped = swap(low, high, edges)
+    (sums,) = call(
+        sums_kernel,
+        [shape((peers, 8, 128), F32)],
+        [low, high, pull_low, pull_high, *pulls, courant_lon, courant_lat, weights],
+        spread,
+        late={i: None for i in range(2, 10)},
+    )
+    above, below, from_west, from_east = swapped
+    sums, from_west, from_east = lax.optimization_barrier((sums, from_west, from_east))
     (result,) = call(
         second_kernel,
         [shape(full, BF16)],
         [
-            low, high, *swap(low, high, west, east),
+            low, high, above, below, from_west, from_east,
             turned, friction_factor, coeff, next0, trajectory, courant_lon, courant_lat,
         ],
         carried + spread,
@@ -490,6 +516,7 @@
         late={7: None, 8: None, 9: None, 10: 0, 11: None, 12: None},
     )
     sums = lax.all_to_all(sums, "freq", split_axis=0, concat_axis=0, tiled=True)
+    result, sums = lax.optimization_barrier((result, sums))
     (sums,) = call(add_kernel, [shape((regions, 8, 128), F32)], [sums])
     sums = lax.all_to_all(sums, "geo", split_axis=0, concat_axis=0, tiled=True)
     point_total = points * peers * regions

time: 102 us -> 99.4 us (0.975)
  starting transfers between devices: 63.1 us -> 47.9 us
  blocking collectives: 0 us -> 13.6 us
  local copies, waits for them, and re-layouts: 6.12 us -> 2.91 us
  Pallas kernels: 24.5 us -> 27.3 us
    all_to_all x0 -> x1, blocking collectives: none -> 13.6 us  [shards(): sums = lax.all_to_all(sums, 'geo', split_axis=0, concat_axis=0, tiled=True)]
    all_to_all x1 -> x0, starting transfers between devices: 12.7 us -> none  [shards(): sums = lax.all_to_all(sums, 'geo', split_axis=0, concat_axis=0, tiled=True)]
    ppermute x6, starting transfers between devices: 17.3 us -> 13.7 us  [the longest x1 6.89 us: shards(): from_east = lax.ppermute(edges, 'geo', westward)]
    unnamed x16, local copies, waits for them, and re-layouts: 6.12 us -> 2.91 us
    pallas_call x9 -> x10, Pallas kernels: 24.5 us -> 27.3 us  [call(): pl.pallas_call(body, out_shape=outs, in_specs=[OUTSIDE if i in late or i...]
    ppermute x6, waiting for transfers between devices: 1.02 us -> 3.18 us  [the longest x1 2.95 us: shards(): from_west = lax.ppermute(edges, 'geo', eastward)]
    all_to_all x1, waiting for transfers between devices: 4.38 us -> 3.11 us  [shards(): sums = lax.all_to_all(sums, 'freq', split_axis=0, concat_axis=0, tiled=True)]
    all_to_all x1 -> x0, waiting for transfers between devices: 1.16 us -> none  [shards(): sums = lax.all_to_all(sums, 'geo', split_axis=0, concat_axis=0, tiled=True)]
  transfers between devices with their start and end apart: 13 -> 12, of which waited for: 5 -> 3; matrix products, arithmetic and copies ran while one was open for 0% -> 0% of each run, Pallas kernels for 15% -> 20%
where the time goes in v3:
time: 99.4 us; the launch traced here: 98.8 us
  starting transfers between devices  47.9 us (48%)
  Pallas kernels  27.3 us (27%)
  blocking collectives  13.6 us (14%)
  waiting for transfers between devices  6.31 us (6%)
  local copies, waits for them, and re-layouts  2.91 us (3%)
    pallas_call x10, Pallas kernels, call(): pl.pallas_call(body, out_shape=outs, in_specs=[OUTSIDE if i in late or i...  27.3 us
    all_to_all x1, blocking collectives, shards(): sums = lax.all_to_all(sums, 'geo', split_axis=0, concat_axis=0, tiled=True)  13.6 us
    all_to_all x1, starting transfers between devices, shards(): sums = lax.all_to_all(sums, 'freq', split_axis=0, concat_axis=0, tiled=True)  12.5 us
    all_to_all x1, starting transfers between devices, shards(): lax.all_to_all(sent, 'freq', split_axis=0, concat_axis=0, tiled=True)  9.67 us
    ppermute x2, starting transfers between devices, swap(): lax.ppermute(high, 'freq', northward)  9.43 us
    ppermute x1, starting transfers between devices, shards(): from_east = lax.ppermute(edges, 'geo', westward)  6.89 us
    ppermute x2, starting transfers between devices, swap(): lax.ppermute(edges, 'geo', westward)  6.22 us
    all_to_all x1, waiting for transfers between devices, shards(): sums = lax.all_to_all(sums, 'freq', split_axis=0, concat_axis=0, tiled=True)  3.11 us
  transfers between devices with their start and end apart: 12, of which 3 were waited for; matrix products, arithmetic and copies ran while one was open for 0% of the time, Pallas kernels for 20%

profile of v3, /device:TPU:1, one launch (start us, length us, event | category | flops | bytes accessed | tf_op | source)
XLA Modules:
  0.0 98.8 jit_solution(14776262062838702218)
XLA Ops:
  0.6 1.5 %shard_map.104 = (f32[2384,128]{1,0:T(8,128)S(1)}, bf16[16,2304]{1,0:T(8,128)(2,1)S(1)}, f32[2,72,128]{2,1,0:T(8,128)S(1)}) custom-call(bf16[36,64,128]{2,1,0:T(8,128)(2,1)} %bitcast.4, s32[64,128]{1,0:T(8,128)} %refs_4_.1, f32[32,36]{1,0:T(8,128)} %refs_11_.1, f32[32,36]{1,0:T(8,128)} %refs_12_.1), custom_call_target="tpu_custom_call" | custom-call | bytes 1999872 | tf_op jit(solution)/shard_map/pallas_call | solution.py:50
  2.1 6.9 %collective-permute-start.1 = (bf16[16,2304]{1,0:T(8,128)(2,1)S(1)}, bf16[16,2304]{1,0:T(8,128)(2,1)S(1)}, u32[]{:S(2)}, u32[]{:S(2)}) collective-permute-start(bf16[16,2304]{1,0:T(8,128)(2,1)S(1)} %get-tuple-element.34), channel_id=1, source_target_pairs={{32,0},{64,32},{96,64},{128,96},{160,128},{192,160},{224,192},{256... | collective-permute-start | bytes 221192 | tf_op jit(solution)/shard_map/ppermute | solution.py:436
  9.0 0.0 collective-permute-start
  9.0 0.7 shard_map.105
  9.7 0.2 collective-permute-done.1.refs_3_
  9.9 3.0 %collective-permute-done.refs_2_ = bf16[16,2304]{1,0:T(8,128)(2,1)S(1)} collective-permute-done((bf16[16,2304]{1,0:T(8,128)(2,1)S(1)}, bf16[16,2304]{1,0:T(8,128)(2,1)S(1)}, u32[]{:S(2)}, u32[]{:S(2)}) %collective-permute-start) | collective-permute-done | bytes 73760 | tf_op jit(solution)/shard_map/ppermute | solution.py:435
  12.9 1.2 %shard_map.106 = bf16[32,72,128]{2,1,0:T(8,128)(2,1)} custom-call(f32[32,72,128]{2,1,0:T(8,128)S(1)} %get-tuple-element.32.refs_0_, f32[72,128]{1,0:T(8,128)S(1)} %get-tuple-element.33.refs_1_, bf16[16,2304]{1,0:T(8,128)(2,1)S(1)} %collective-permute-done.refs_2_, bf16[16,2304]{1,0:T(8,128)(2,1)S(1)} %collective-permute-done.1.refs_3_), custom_call_target="tpu_custom_call" | custom-call | bytes 1953792 | tf_op jit(solution)/shard_map/pallas_call | solution.py:50
  14.1 9.7 %all-to-all-start = ((bf16[32,72,128]{2,1,0:T(8,128)(2,1)}), bf16[32,72,128]{2,1,0:T(8,128)(2,1)S(1)}, u32[]{:S(2)}, u32[]{:S(2)}) async-start(bf16[32,72,128]{2,1,0:T(8,128)(2,1)} %shard_map.106), calls=%async_computation | async-start | bytes 1179648 | tf_op jit(solution)/shard_map/all_to_all | solution.py:446
  23.7 4.9 %shard_map.107 = (f32[1,256]{1,0:T(1,128)S(1)}, f32[1152,256]{1,0:T(8,128)S(1)}, bf16[1168,128]{1,0:T(8,128)(2,1)S(1)}, bf16[1168,128]{1,0:T(8,128)(2,1)S(1)}, bf16[16,1168]{1,0:T(8,128)(2,1)S(1)}) custom-call(bf16[2,1152,256]{2,1,0:T(8,128)(2,1)} %refs_10_, bf16[1152,1152]{1,0:T(8,128)(2,1)} %refs_1_.5, f32[32,256]{1,0:T(8,128)} %refs_7_.1, ...), custom_call_target="tpu_custom_call" | custom-call | flops 1358954496 | bytes 5683968 | tf_op jit(solution)/shard_map/pallas_call | solution.py:50
  28.7 0.0 copy-start.4
  28.7 0.6 copy-done.4
  29.2 0.0 copy-start
  29.3 0.0 copy-start.2
  29.3 0.0 copy-start.3
  29.3 1.3 %collective-permute-start.2 = (bf16[1168,128]{1,0:T(8,128)(2,1)S(1)}, bf16[1168,128]{1,0:T(8,128)(2,1)S(1)}, u32[]{:S(2)}, u32[]{:S(2)}) collective-permute-start(bf16[1168,128]{1,0:T(8,128)(2,1)S(1)} %get-tuple-element.37.refs_2_), channel_id=1, source_target_pairs={{1,0},{2,1},{3,2},{4,3},{5,4},{6,5},{7,6},{8,7},{9,8},{10,9},{11,1... | collective-permute-start | bytes 897032 | tf_op jit(solution)/shard_map/ppermute | solution.py:422
  30.5 4.7 %collective-permute-start.3 = (bf16[1168,128]{1,0:T(8,128)(2,1)S(1)}, bf16[1168,128]{1,0:T(8,128)(2,1)}, u32[]{:S(2)}, u32[]{:S(2)}) collective-permute-start(bf16[1168,128]{1,0:T(8,128)(2,1)S(1)} %get-tuple-element.38.refs_3_), channel_id=1, source_target_pairs={{0,1},{1,2},{2,3},{3,4},{4,5},{5,6},{6,7},{7,8},{8,9},{9,10},{10,1... | collective-permute-start | bytes 897032 | tf_op jit(solution)/shard_map/ppermute | solution.py:423
  35.3 5.1 %collective-permute-start.5 = (bf16[16,1168]{1,0:T(8,128)(2,1)S(1)}, bf16[16,1168]{1,0:T(8,128)(2,1)S(1)}, u32[]{:S(2)}, u32[]{:S(2)}) collective-permute-start(bf16[16,1168]{1,0:T(8,128)(2,1)S(1)} %get-tuple-element.39), channel_id=1, source_target_pairs={{32,0},{64,32},{96,64},{128,96},{160,128},{192,160},{224,192},{256... | collective-permute-start | bytes 112136 | tf_op jit(solution)/shard_map/ppermute | solution.py:425
  40.3 0.0 collective-permute-start.4
  40.3 3.0 %shard_map.108 = (bf16[1152,1152]{1,0:T(8,128)(2,1)S(1)}, f32[1152,256]{1,0:T(8,128)S(1)}) custom-call(bf16[2,1152,256]{2,1,0:T(8,128)(2,1)} %refs_10_, bf16[1152,1152]{1,0:T(8,128)(2,1)} %refs_1_.5, f32[32,256]{1,0:T(8,128)} %refs_7_.1, f32[1,256]{1,0:T(1,128)} %copy-done.4), custom_call_target="tpu_custom_call" | custom-call | flops 679477248 | bytes 7701504 | tf_op jit(solution)/shard_map/pallas_call | solution.py:50
  43.3 0.0 copy-done
  43.3 0.0 copy-done.2
  43.3 0.0 copy-done.3
  43.3 0.0 copy-start.1
  43.4 1.0 %copy-done.1 = f32[1152,256]{1,0:T(8,128)} copy-done((f32[1152,256]{1,0:T(8,128)}, f32[1152,256]{1,0:T(8,128)S(1)}, u32[]{:S(2)}) %copy-start.1) | copy-done | bytes 1179672
  44.4 0.0 collective-permute-done.5.refs_7_
  44.4 0.0 collective-permute-done.4.refs_6_
  44.4 0.0 copy-start.7
  44.4 0.0 collective-permute-done.2.refs_4_
  44.4 0.6 copy-done.6
  45.0 0.0 copy-done.7
  45.0 0.7 copy-done.5
  45.7 0.0 collective-permute-done.3.refs_5_
  45.7 0.0 all-to-all-done.refs_0_
  45.7 4.1 %shard_map.109 = (bf16[1152,128]{1,0:T(8,128)(2,1)S(1)}, bf16[1152,128]{1,0:T(8,128)(2,1)}, bf16[16,1152]{1,0:T(8,128)(2,1)S(1)}, f32[8,256]{1,0:T(8,128)S(1)}) custom-call(bf16[32,72,128]{2,1,0:T(8,128)(2,1)S(1)} %all-to-all-done.refs_0_, bf16[1152,1152]{1,0:T(8,128)(2,1)S(1)} %get-tuple-element.42.refs_1_.refs_6_, f32[32,256]{1,0:T(8,128)} %refs_7_.1, ...), custom_call_target="tpu_custom_call" | custom-call | flops 1358954496 | bytes 6304768 | tf_op jit(solution)/shard_map/pallas_call | solution.py:50
  49.8 1.3 %collective-permute-start.6 = (bf16[1152,128]{1,0:T(8,128)(2,1)S(1)}, bf16[1152,128]{1,0:T(8,128)(2,1)S(1)}, u32[]{:S(2)}, u32[]{:S(2)}) collective-permute-start(bf16[1152,128]{1,0:T(8,128)(2,1)S(1)} %get-tuple-element.44.refs_0_), channel_id=1, source_target_pairs={{1,0},{2,1},{3,2},{4,3},{5,4},{6,5},{7,6},{8,7},{9,8},{10,9},{11,1... | collective-permute-start | bytes 884744 | tf_op jit(solution)/shard_map/ppermute | solution.py:422
  51.1 4.7 %collective-permute-start.7 = (bf16[1152,128]{1,0:T(8,128)(2,1)}, bf16[1152,128]{1,0:T(8,128)(2,1)}, u32[]{:S(2)}, u32[]{:S(2)}) collective-permute-start(bf16[1152,128]{1,0:T(8,128)(2,1)} %get-tuple-element.45.refs_1_), channel_id=1, source_target_pairs={{0,1},{1,2},{2,3},{3,4},{4,5},{5,6},{6,7},{7,8},{8,9},{9,10},{10,1... | collective-permute-start | bytes 884744 | tf_op jit(solution)/shard_map/ppermute | solution.py:423
  55.8 1.1 %collective-permute-start.9 = (bf16[16,1152]{1,0:T(8,128)(2,1)S(1)}, bf16[16,1152]{1,0:T(8,128)(2,1)S(1)}, u32[]{:S(2)}, u32[]{:S(2)}) collective-permute-start(bf16[16,1152]{1,0:T(8,128)(2,1)S(1)} %get-tuple-element.51), channel_id=1, source_target_pairs={{32,0},{64,32},{96,64},{128,96},{160,128},{192,160},{224,192},{256... | collective-permute-start | bytes 110600 | tf_op jit(solution)/shard_map/ppermute | solution.py:425
  57.0 0.6 collective-permute-start.8
  57.6 5.4 %shard_map.110 = f32[32,8,128]{2,1,0:T(8,128)} custom-call(bf16[1152,128]{1,0:T(8,128)(2,1)S(1)} %get-tuple-element.44.refs_0_, bf16[1152,128]{1,0:T(8,128)(2,1)} %get-tuple-element.45.refs_1_, bf16[1168,128]{1,0:T(8,128)(2,1)} %copy-done.2, bf16[1168,128]{1,0:T(8,128)(2,1)} %copy-done.3, bf16[1168,128]{1,0:T(8,128)(2,1)} %copy-done.5, ...), custom_call_target="tpu_custom_call" | custom-call | bytes 2009088 | tf_op jit(solution)/shard_map/pallas_call | solution.py:50
  63.0 0.0 collective-permute-done.9.refs_5_
  63.0 0.0 collective-permute-done.8.refs_4_
  63.0 12.5 %all-to-all-start.1 = ((f32[32,8,128]{2,1,0:T(8,128)}), f32[32,8,128]{2,1,0:T(8,128)S(1)}, u32[]{:S(2)}, u32[]{:S(2)}) async-start(f32[32,8,128]{2,1,0:T(8,128)} %shard_map.110), calls=%async_computation.1 | async-start | bytes 262144 | tf_op jit(solution)/shard_map/all_to_all | solution.py:518
  75.5 0.0 collective-permute-done.6.refs_2_
  75.5 0.0 collective-permute-done.7.refs_3_
  75.5 6.0 %shard_map.111 = bf16[1152,256]{1,0:T(8,128)(2,1)} custom-call(bf16[1152,128]{1,0:T(8,128)(2,1)S(1)} %get-tuple-element.44.refs_0_, bf16[1152,128]{1,0:T(8,128)(2,1)} %get-tuple-element.45.refs_1_, bf16[1152,128]{1,0:T(8,128)(2,1)S(1)} %collective-permute-done.6.refs_2_, bf16[1152,128]{1,0:T(8,128)(2,1)} %collective-permute-done.7.refs_3_, ...), custom_call_target="tpu_custom_call" | custom-call | flops 1358954496 | bytes 6899712 | tf_op jit(solution)/shard_map/pallas_call | solution.py:50
  81.6 3.1 %all-to-all-done.1.refs_0_ = f32[32,8,128]{2,1,0:T(8,128)S(1)} async-done(((f32[32,8,128]{2,1,0:T(8,128)}), f32[32,8,128]{2,1,0:T(8,128)S(1)}, u32[]{:S(2)}, u32[]{:S(2)}) %all-to-all-start.1) | async-done | bytes 131104 | tf_op jit(solution)/shard_map/all_to_all | solution.py:518
  84.7 13.6 %all_to_all.15.refs_0_ = f32[16,8,128]{2,1,0:T(8,128)S(1)} all-to-all(f32[16,8,128]{2,1,0:T(8,128)S(1)} %shard_map.112), channel_id=1, replica_groups=mesh['geo'=16,'freq'=32] {'geo'}, dimensions={0} | all-to-all | bytes 131072 | tf_op jit(solution)/shard_map/all_to_all | solution.py:521
  98.3 0.5 shard_map.113
  (3 shorter events, 0.0 us)
Async XLA Ops:
  2.1 7.8 %collective-permute-start.1 = (bf16[16,2304]{1,0:T(8,128)(2,1)S(1)}, bf16[16,2304]{1,0:T(8,128)(2,1)S(1)}, u32[]{:S(2)}, u32[]{:S(2)}) collective-permute-start(bf16[16,2304]{1,0:T(8,128)(2,1)S(1)} %get-tuple-element.34), channel_id=1, source_target_pairs={{32,0},{64,32},{96,64},{128,96},{160,128},{192,160},{224,192},{256... | collective-permute-start | bytes 221192 | tf_op jit(solution)/shard_map/ppermute | solution.py:436
  9.0 3.9 %collective-permute-start = (bf16[16,2304]{1,0:T(8,128)(2,1)S(1)}, bf16[16,2304]{1,0:T(8,128)(2,1)S(1)}, u32[]{:S(2)}, u32[]{:S(2)}) collective-permute-start(bf16[16,2304]{1,0:T(8,128)(2,1)S(1)} %get-tuple-element.34), channel_id=1, source_target_pairs={{0,32},{32,64},{64,96},{96,128},{128,160},{160,192},{192,224},{224... | collective-permute-start | bytes 221192 | tf_op jit(solution)/shard_map/ppermute | solution.py:435
  14.1 31.7 %all-to-all-start = ((bf16[32,72,128]{2,1,0:T(8,128)(2,1)}), bf16[32,72,128]{2,1,0:T(8,128)(2,1)S(1)}, u32[]{:S(2)}, u32[]{:S(2)}) async-start(bf16[32,72,128]{2,1,0:T(8,128)(2,1)} %shard_map.106), calls=%async_computation | async-start | bytes 1179648 | tf_op jit(solution)/shard_map/all_to_all | solution.py:446
  28.7 0.6 copy-start.4
  29.2 14.1 %copy-start = (f32[1152,256]{1,0:T(8,128)}, f32[1152,256]{1,0:T(8,128)S(1)}, u32[]{:S(2)}) copy-start(f32[1152,256]{1,0:T(8,128)S(1)} %get-tuple-element.54.refs_9_) | copy-start | bytes 3538948
  29.3 14.1 %copy-start.2 = (bf16[1168,128]{1,0:T(8,128)(2,1)}, bf16[1168,128]{1,0:T(8,128)(2,1)S(1)}, u32[]{:S(2)}) copy-start(bf16[1168,128]{1,0:T(8,128)(2,1)S(1)} %get-tuple-element.37.refs_2_) | copy-start | bytes 897028
  29.3 14.1 %copy-start.3 = (bf16[1168,128]{1,0:T(8,128)(2,1)}, bf16[1168,128]{1,0:T(8,128)(2,1)S(1)}, u32[]{:S(2)}) copy-start(bf16[1168,128]{1,0:T(8,128)(2,1)S(1)} %get-tuple-element.38.refs_3_) | copy-start | bytes 897028
  29.3 15.1 %collective-permute-start.2 = (bf16[1168,128]{1,0:T(8,128)(2,1)S(1)}, bf16[1168,128]{1,0:T(8,128)(2,1)S(1)}, u32[]{:S(2)}, u32[]{:S(2)}) collective-permute-start(bf16[1168,128]{1,0:T(8,128)(2,1)S(1)} %get-tuple-element.37.refs_2_), channel_id=1, source_target_pairs={{1,0},{2,1},{3,2},{4,3},{5,4},{6,5},{7,6},{8,7},{9,8},{10,9},{11,1... | collective-permute-start | bytes 897032 | tf_op jit(solution)/shard_map/ppermute | solution.py:422
  30.5 15.2 %collective-permute-start.3 = (bf16[1168,128]{1,0:T(8,128)(2,1)S(1)}, bf16[1168,128]{1,0:T(8,128)(2,1)}, u32[]{:S(2)}, u32[]{:S(2)}) collective-permute-start(bf16[1168,128]{1,0:T(8,128)(2,1)S(1)} %get-tuple-element.38.refs_3_), channel_id=1, source_target_pairs={{0,1},{1,2},{2,3},{3,4},{4,5},{5,6},{6,7},{7,8},{8,9},{9,10},{10,1... | collective-permute-start | bytes 897032 | tf_op jit(solution)/shard_map/ppermute | solution.py:423
  35.3 9.1 %collective-permute-start.5 = (bf16[16,1168]{1,0:T(8,128)(2,1)S(1)}, bf16[16,1168]{1,0:T(8,128)(2,1)S(1)}, u32[]{:S(2)}, u32[]{:S(2)}) collective-permute-start(bf16[16,1168]{1,0:T(8,128)(2,1)S(1)} %get-tuple-element.39), channel_id=1, source_target_pairs={{32,0},{64,32},{96,64},{128,96},{160,128},{192,160},{224,192},{256... | collective-permute-start | bytes 112136 | tf_op jit(solution)/shard_map/ppermute | solution.py:425
  40.3 4.0 %collective-permute-start.4 = (bf16[16,1168]{1,0:T(8,128)(2,1)S(1)}, bf16[16,1168]{1,0:T(8,128)(2,1)S(1)}, u32[]{:S(2)}, u32[]{:S(2)}) collective-permute-start(bf16[16,1168]{1,0:T(8,128)(2,1)S(1)} %get-tuple-element.39), channel_id=1, source_target_pairs={{0,32},{32,64},{64,96},{96,128},{128,160},{160,192},{192,224},{224... | collective-permute-start | bytes 112136 | tf_op jit(solution)/shard_map/ppermute | solution.py:424
  43.3 1.0 %copy-start.1 = (f32[1152,256]{1,0:T(8,128)}, f32[1152,256]{1,0:T(8,128)S(1)}, u32[]{:S(2)}) copy-start(f32[1152,256]{1,0:T(8,128)S(1)} %get-tuple-element.43.refs_5_) | copy-start | bytes 3538948
  44.4 0.6 copy-start.6
  44.4 0.6 copy-start.7
  45.0 0.7 copy-start.5
  49.8 25.7 %collective-permute-start.6 = (bf16[1152,128]{1,0:T(8,128)(2,1)S(1)}, bf16[1152,128]{1,0:T(8,128)(2,1)S(1)}, u32[]{:S(2)}, u32[]{:S(2)}) collective-permute-start(bf16[1152,128]{1,0:T(8,128)(2,1)S(1)} %get-tuple-element.44.refs_0_), channel_id=1, source_target_pairs={{1,0},{2,1},{3,2},{4,3},{5,4},{6,5},{7,6},{8,7},{9,8},{10,9},{11,1... | collective-permute-start | bytes 884744 | tf_op jit(solution)/shard_map/ppermute | solution.py:422
  51.1 24.4 %collective-permute-start.7 = (bf16[1152,128]{1,0:T(8,128)(2,1)}, bf16[1152,128]{1,0:T(8,128)(2,1)}, u32[]{:S(2)}, u32[]{:S(2)}) collective-permute-start(bf16[1152,128]{1,0:T(8,128)(2,1)} %get-tuple-element.45.refs_1_), channel_id=1, source_target_pairs={{0,1},{1,2},{2,3},{3,4},{4,5},{5,6},{6,7},{7,8},{8,9},{9,10},{10,1... | collective-permute-start | bytes 884744 | tf_op jit(solution)/shard_map/ppermute | solution.py:423
  55.8 7.1 %collective-permute-start.9 = (bf16[16,1152]{1,0:T(8,128)(2,1)S(1)}, bf16[16,1152]{1,0:T(8,128)(2,1)S(1)}, u32[]{:S(2)}, u32[]{:S(2)}) collective-permute-start(bf16[16,1152]{1,0:T(8,128)(2,1)S(1)} %get-tuple-element.51), channel_id=1, source_target_pairs={{32,0},{64,32},{96,64},{128,96},{160,128},{192,160},{224,192},{256... | collective-permute-start | bytes 110600 | tf_op jit(solution)/shard_map/ppermute | solution.py:425
  57.0 6.0 %collective-permute-start.8 = (bf16[16,1152]{1,0:T(8,128)(2,1)S(1)}, bf16[16,1152]{1,0:T(8,128)(2,1)S(1)}, u32[]{:S(2)}, u32[]{:S(2)}) collective-permute-start(bf16[16,1152]{1,0:T(8,128)(2,1)S(1)} %get-tuple-element.51), channel_id=1, source_target_pairs={{0,32},{32,64},{64,96},{96,128},{128,160},{160,192},{192,224},{224... | collective-permute-start | bytes 110600 | tf_op jit(solution)/shard_map/ppermute | solution.py:424
  63.0 21.7 %all-to-all-start.1 = ((f32[32,8,128]{2,1,0:T(8,128)}), f32[32,8,128]{2,1,0:T(8,128)S(1)}, u32[]{:S(2)}, u32[]{:S(2)}) async-start(f32[32,8,128]{2,1,0:T(8,128)} %shard_map.110), calls=%async_computation.1 | async-start | bytes 262144 | tf_op jit(solution)/shard_map/all_to_all | solution.py:518

commit v4 on v3

--- a/solution.py
+++ b/solution.py
@@ -185,20 +185,13 @@
 
 
 def pull_kernel(
-    traj_ref, inter_any, kappa_ref, coeff_ref, sed_ref,
-    point_coeff_ref, next_ref, low_ref, high_ref, edge_ref,
-    factor_scr, product_scr, pull_scr, inter_ref, sems, wait,
-):
+    trajectory_ref, inter_ref, kappa_ref, coeff_ref, sed_ref,
+    point_coeff_ref, next_ref, pull_ref, factor_scr, product_scr, wait,
+):
+    traj_ref = trajectory_ref.at[0]
     components, points = traj_ref.shape
     groups = coeff_ref.shape[1]
-    lon = low_ref.shape[1]
     blocks = blocks_of(components, 4)
-    copies = [
-        pltpu.make_async_copy(inter_any.at[rows, :], inter_ref.at[rows, :], sems.at[i])
-        for i, rows in enumerate(blocks)
-    ]
-    for copy in copies:
-        copy.start()
     wait(2, 3, 4)
     sediment = sed_ref[...]
     hits = (lax.broadcasted_iota(jnp.int32, (groups, points), 0) == sediment).astype(F32)
@@ -208,9 +201,7 @@
     )[0:1]
     point_coeff_ref[...] = coeff
     spread_factor(kappa_ref, factor_scr)
-    wait(0)
-    for copy, rows in zip(copies, blocks):
-        copy.wait()
+    for rows in blocks:
         here, after = forward(traj_ref, inter_ref, factor_scr, coeff, rows)
         next_ref[rows, :] = after
         product_scr[rows, :] = (0.5 * factor_scr[rows, :] * here * after).astype(BF16)
@@ -219,73 +210,22 @@
         pushed = jnp.dot(inter_ref[rows, :], product, preferred_element_type=F32)
         factor, here = factor_scr[rows, :], traj_ref[rows, :].astype(F32)
         pull = factor * (next_ref[rows, :] + decay_of(factor, coeff) * here) + pushed
-        pull_scr[rows, :] = pull.astype(BF16)
-    extra = pull_scr.shape[0] - components
-    first_row = lax.broadcasted_iota(jnp.int32, (extra, points), 0) == 0
-    pull_scr[components:, :] = jnp.where(first_row, sediment.astype(F32), 0.0).astype(BF16)
-    low_ref[...] = pull_scr[:, 0:lon]
-    high_ref[...] = pull_scr[:, lon : 2 * lon]
-    edge_ref[...] = take_edges(pull_scr[...], edge_picks(2 * lon, lon)).astype(BF16)
+        pull_ref[rows, :] = pull.astype(BF16)
 
 
 def states_kernel(
-    traj_ref, inter_ref, kappa_ref, coeff_ref, turned_ref, next_ref, factor_scr, wait
-):
+    trajectory_ref, inter_ref, kappa_ref, coeff_ref, courant_lon_ref, courant_lat_ref,
+    turned_ref, next_ref, rates_ref, factor_scr, turn_scr, wait,
+):
+    traj_ref = trajectory_ref.at[1]
     components = traj_ref.shape[0]
-    wait(2, 3)
+    wait(2, 4, 5)
     spread_factor(kappa_ref, factor_scr)
-    wait(0, 1)
+    spread_rates((courant_lon_ref, courant_lat_ref), turn_scr, rates_ref)
     coeff = coeff_ref[...]
     turned_ref[...] = inter_ref[...].T
     for rows in blocks_of(components, 4):
         next_ref[rows, :] = forward(traj_ref, inter_ref, factor_scr, coeff, rows)[1]
-
-
-def sums_kernel(
-    low_ref, high_ref, pull_low_ref, pull_high_ref, above_ref, below_ref, west_ref, east_ref,
-    courant_lon_ref, courant_lat_ref, own_ref, sums_ref, turn_scr, rates_scr, wait,
-):
-    components, lon = low_ref.shape
-    total = components + 16
-    wait(8, 9)
-    spread_rates((courant_lon_ref, courant_lat_ref), turn_scr, rates_scr)
-    wait(6, 7)
-    cols = put_edges(west_ref[...], east_ref[...], 2 * lon, lon)
-    wait(2, 3, 4, 5)
-    weights = [[jnp.zeros((8, lon), F32)] * 5 for _ in range(2)]
-    weights[0][0], weights[1][0] = own_ref[:, 0:lon], own_ref[:, lon : 2 * lon]
-    near = [[None] * 5, [None] * 5]
-    for rows in [*blocks_of(components, components // 144), slice(components, total)]:
-        size = rows.stop - rows.start
-        lane = lax.broadcasted_iota(jnp.int32, (size, lon), 1)
-        low, high = pull_low_ref[rows, :].astype(F32), pull_high_ref[rows, :].astype(F32)
-        above, below = above_ref[rows, :].astype(F32), below_ref[rows, :].astype(F32)
-        if rows.start < components:
-            rates = split_rates(rates_scr[0, rows, :], rates_scr[1, rows, :])
-        for half, (here, up, down, field) in enumerate(
-            ((low, high, below, low_ref), (high, above, low, high_ref))
-        ):
-            edge = cols[rows, half * lon : (half + 1) * lon]
-            west = jnp.where(lane == 0, edge, pltpu.roll(here, 1, 1))
-            east = jnp.where(lane == lon - 1, edge, pltpu.roll(here, lon - 1, 1))
-            reached = (here, west, east, down, up)
-            if rows.start == components:
-                near[half] = [value[0:1] for value in reached]
-                continue
-            masked = field[rows, :].astype(F32)
-            for slot, value in enumerate(reached):
-                terms = (rates[slot] * value * masked).reshape(size // 8, 8, lon)
-                weights[half][slot] = weights[half][slot] + terms.sum(axis=0)
-    sums = jnp.zeros(sums_ref.shape[1:], F32)
-    group = lax.broadcasted_iota(jnp.int32, (sums.shape[1], lon), 0).astype(F32)
-    for half in range(2):
-        for slot in range(5):
-            hits = (group == near[half][slot]).astype(F32)
-            sums = sums + lax.dot_general(
-                weights[half][slot], hits, (((1,), (1,)), ((), ())),
-                precision=lax.Precision.HIGHEST, preferred_element_type=F32,
-            )
-    sums_ref[...] = jnp.broadcast_to(sums[None], sums_ref.shape)
 
 
 def two_substeps(m_scr, r_scr, turned_ref, factor_scr, coeff, ready, write, weigh):
@@ -349,24 +289,19 @@
     edge_ref[...] = edges.astype(BF16)
 
 
-def second_kernel(
-    low_ref, high_ref, north_ref, south_ref, west_ref, east_ref,
-    turned_ref, kappa_ref, coeff_ref, next_ref, traj_ref, courant_lon_ref, courant_lat_ref,
-    out_ref, m_scr, r_scr, factor_scr, turn_scr, rates_scr, wait,
+def halo_kernel(
+    low_ref, high_ref, north_ref, south_ref, west_ref, east_ref, rates_ref, pull_ref, own_ref, sed_ref,
+    moved_ref, sums_ref, wait,
 ):
     components, lon = low_ref.shape
-    wait(11, 12)
-    spread_rates((courant_lon_ref, courant_lat_ref), turn_scr, rates_scr)
-    wait(7)
-    spread_factor(kappa_ref, factor_scr)
     cols = put_edges(west_ref[...], east_ref[...], 2 * lon, lon)
-    chunk = components // 8
+    weights = [own_ref[:, 0:lon], own_ref[:, lon : 2 * lon]]
+    chunk = 144
     lane = lax.broadcasted_iota(jnp.int32, (chunk, lon), 1)
-    for at in range(0, components, chunk):
-        rows = slice(at, at + chunk)
+    for rows in blocks_of(components, components // chunk):
         low, high = low_ref[rows, :].astype(F32), high_ref[rows, :].astype(F32)
         above, below = north_ref[rows, :].astype(F32), south_ref[rows, :].astype(F32)
-        rates = split_rates(rates_scr[0, rows, :], rates_scr[1, rows, :])
+        rates = split_rates(rates_ref[0, rows, :], rates_ref[1, rows, :])
         for half, (here, up, down) in enumerate(((low, high, below), (high, above, low))):
             lanes = slice(half * lon, (half + 1) * lon)
             edge = cols[rows, lanes]
@@ -379,10 +314,28 @@
                 + rates[3] * up
                 + rates[4] * down
             ).astype(BF16)
-            r_scr[rows, lanes] = value
-            m_scr[rows, lanes] = value.astype(F32)
-
-    wait(8, 9, 10)
+            moved_ref[rows, lanes] = value
+            terms = value.astype(F32) * pull_ref[rows, lanes].astype(F32)
+            weights[half] = weights[half] + terms.reshape(chunk // 8, 8, lon).sum(axis=0)
+    wait(9)
+    groups, points = sums_ref.shape[2], 2 * lon
+    hits = (lax.broadcasted_iota(jnp.int32, (groups, points), 0) == sed_ref[...]).astype(F32)
+    sums = lax.dot_general(
+        jnp.concatenate(weights, axis=1), hits, (((1,), (1,)), ((), ())),
+        precision=lax.Precision.HIGHEST, preferred_element_type=F32,
+    )
+    sums_ref[...] = jnp.broadcast_to(sums.sum(axis=0, keepdims=True)[None], sums_ref.shape)
+
+
+def last_kernel(
+    moved_ref, turned_ref, kappa_ref, coeff_ref, next_ref, traj_ref, out_ref,
+    m_scr, r_scr, factor_scr, wait,
+):
+    r_scr[...] = moved_ref[...]
+    m_scr[...] = moved_ref[...].astype(F32)
+    wait(2, 3)
+    spread_factor(kappa_ref, factor_scr)
+    wait(4, 5)
 
     def ready(rows):
         return next_ref[rows, :], traj_ref[rows, :].astype(F32)
@@ -398,8 +351,7 @@
 
 
 def final_kernel(scale, parts_ref, out_ref):
-    total = parts_ref[...].sum(axis=0).sum(axis=0, keepdims=True)
-    out_ref[...] = total[:, 0 : out_ref.shape[1]] * scale
+    out_ref[...] = parts_ref[...].sum(axis=0)[:, 0 : out_ref.shape[1]] * scale
 
 
 def shards(
@@ -442,45 +394,35 @@
     (sent,) = call(
         edges_kernel, [shape((peers, height, lon), BF16)], [part, rate, from_west, from_east]
     )
-    sent, trajectory = lax.optimization_barrier((sent, trajectory))
+    sent, point_factor = lax.optimization_barrier((sent, friction_factor))
     moved = lax.all_to_all(sent, "freq", split_axis=0, concat_axis=0, tiled=True)
 
     product = 2 * components * components * points
     full, half_full = (components, points), (components, lon)
-    tall = components + 16
-    coeff, next0, pull_low, pull_high, pull_edges = call(
+    coeff, next0, pull = call(
         pull_kernel,
+        [shape((1, points), F32), shape(full, F32), shape(full, BF16)],
         [
-            shape((1, points), F32),
+            trajectory, interaction, point_factor, friction_coeff.reshape(1, groups),
+            sediment.reshape(1, points),
+        ],
+        [pltpu.VMEM(full, F32), pltpu.VMEM(full, BF16)],
+        flops=2 * product,
+        late={2: None, 3: None, 4: None},
+    )
+    turned, next1, rates = call(
+        states_kernel,
+        [
+            shape((components, components), BF16),
             shape(full, F32),
-            shape((tall, lon), BF16),
-            shape((tall, lon), BF16),
-            shape((16, tall), BF16),
+            shape((2, components, lon), F32),
         ],
-        [
-            trajectory, pltpu.with_memory_space_constraint(interaction, pltpu.HBM),
-            friction_factor, friction_coeff.reshape(1, groups), sediment.reshape(1, points),
-        ],
-        [
-            pltpu.VMEM(full, F32), pltpu.VMEM(full, BF16), pltpu.VMEM((tall, points), BF16),
-            pltpu.VMEM((components, components), BF16), pltpu.SemaphoreType.DMA((4,)),
-        ],
-        flops=2 * product,
-        late={0: 0, 2: None, 3: None, 4: None},
-        outside=(1,),
-    )
-    pulls = swap(pull_low, pull_high, pull_edges)
-    turned, next1 = call(
-        states_kernel,
-        [shape((components, components), BF16), shape(full, F32)],
-        [trajectory, interaction, friction_factor, coeff],
-        [pltpu.VMEM(full, F32)],
+        [trajectory, interaction, point_factor, coeff, courant_lon, courant_lat],
+        [pltpu.VMEM(full, F32), pltpu.VMEM((128, 128), F32)],
         flops=product,
-        late={0: 1, 1: None, 2: None, 3: None},
-    )
-    moved, *pulls = lax.optimization_barrier((moved, *pulls))
+        late={2: None, 4: None, 5: None},
+    )
     carried = [pltpu.VMEM(full, F32), pltpu.VMEM(full, BF16), pltpu.VMEM(full, F32)]
-    spread = [pltpu.VMEM((128, 128), F32), pltpu.VMEM((2, *half_full), F32)]
     low, high, edges, weights = call(
         first_kernel,
         [
@@ -494,30 +436,25 @@
         flops=2 * product,
         late={2: None, 3: None, 4: None, 5: None, 6: 1},
     )
-    swapped = swap(low, high, edges)
-    (sums,) = call(
-        sums_kernel,
-        [shape((peers, 8, 128), F32)],
-        [low, high, pull_low, pull_high, *pulls, courant_lon, courant_lat, weights],
-        spread,
-        late={i: None for i in range(2, 10)},
-    )
-    above, below, from_west, from_east = swapped
-    sums, from_west, from_east = lax.optimization_barrier((sums, from_west, from_east))
+    moved, sums = call(
+        halo_kernel,
+        [shape(full, BF16), shape((peers, 1, 128), F32)],
+        [
+            low, high, *swap(low, high, edges), rates, pull, weights, sediment.reshape(1, points),
+        ],
+        late={9: None},
+    )
+    sums = lax.all_to_all(sums, "freq", split_axis=0, concat_axis=0, tiled=True)
     (result,) = call(
-        second_kernel,
+        last_kernel,
         [shape(full, BF16)],
-        [
-            low, high, above, below, from_west, from_east,
-            turned, friction_factor, coeff, next0, trajectory, courant_lon, courant_lat,
-        ],
-        carried + spread,
+        [moved, turned, friction_factor, coeff, next0, trajectory],
+        carried,
         flops=2 * product,
-        late={7: None, 8: None, 9: None, 10: 0, 11: None, 12: None},
-    )
-    sums = lax.all_to_all(sums, "freq", split_axis=0, concat_axis=0, tiled=True)
+        late={2: None, 3: None, 4: None, 5: 0},
+    )
     result, sums = lax.optimization_barrier((result, sums))
-    (sums,) = call(add_kernel, [shape((regions, 8, 128), F32)], [sums])
+    (sums,) = call(add_kernel, [shape((regions, 1, 128), F32)], [sums])
     sums = lax.all_to_all(sums, "geo", split_axis=0, concat_axis=0, tiled=True)
     point_total = points * peers * regions
     scale = -step_weight * groups / (point_total * components)

time: 99.4 us -> 95 us (0.956)
  starting transfers between devices: 47.9 us -> 36.8 us
  Pallas kernels: 27.3 us -> 19 us
  waiting for transfers between devices: 6.31 us -> 13.2 us
  blocking collectives: 13.6 us -> 19 us
  local copies, waits for them, and re-layouts: 2.91 us -> 5.62 us
    pallas_call x10, Pallas kernels: 27.3 us -> 19 us  [call(): pl.pallas_call(body, out_shape=outs, in_specs=[OUTSIDE if i in late or i...]
    all_to_all x1, blocking collectives: 13.6 us -> 19 us  [shards(): sums = lax.all_to_all(sums, 'geo', split_axis=0, concat_axis=0, tiled=True)]
    ppermute x2 -> x1, starting transfers between devices: 9.43 us -> 4 us  [swap(): lax.ppermute(high, 'freq', northward)]
    all_to_all x1, starting transfers between devices: 12.5 us -> 7.53 us  [shards(): sums = lax.all_to_all(sums, 'freq', split_axis=0, concat_axis=0, tiled=True)]
    all_to_all x1, waiting for transfers between devices: 0.01 us -> 2.87 us  [shards(): lax.all_to_all(sent, 'freq', split_axis=0, concat_axis=0, tiled=True)]
    unnamed x16 -> x20, local copies, waits for them, and re-layouts: 2.91 us -> 5.62 us
    ppermute x2 -> x1, waiting for transfers between devices: 0.01 us -> 1.84 us  [swap(): lax.ppermute(edges, 'geo', eastward)]
    all_to_all x1, waiting for transfers between devices: 3.11 us -> 4.5 us  [shards(): sums = lax.all_to_all(sums, 'freq', split_axis=0, concat_axis=0, tiled=True)]
  transfers between devices with their start and end apart: 12 -> 8, of which waited for: 3 -> 6; matrix products, arithmetic and copies ran while one was open for 0% -> 0% of each run, Pallas kernels for 20% -> 10%
where the time goes in v4:
time: 95 us; the launch traced here: 94.5 us
  starting transfers between devices  36.8 us (39%)
  Pallas kernels  19 us (20%)
  blocking collectives  19 us (20%)
  waiting for transfers between devices  13.2 us (14%)
  local copies, waits for them, and re-layouts  5.62 us (6%)
    pallas_call x10, Pallas kernels, call(): pl.pallas_call(body, out_shape=outs, in_specs=[OUTSIDE if i in late or i...  19 us
    all_to_all x1, blocking collectives, shards(): sums = lax.all_to_all(sums, 'geo', split_axis=0, concat_axis=0, tiled=True)  19 us
    all_to_all x1, starting transfers between devices, shards(): lax.all_to_all(sent, 'freq', split_axis=0, concat_axis=0, tiled=True)  9.67 us
    all_to_all x1, starting transfers between devices, shards(): sums = lax.all_to_all(sums, 'freq', split_axis=0, concat_axis=0, tiled=True)  7.53 us
    ppermute x1, starting transfers between devices, swap(): lax.ppermute(edges, 'geo', westward)  7.39 us
    ppermute x1, starting transfers between devices, shards(): from_east = lax.ppermute(edges, 'geo', westward)  6.89 us
    unnamed x20, local copies, waits for them, and re-layouts  5.62 us
    all_to_all x1, waiting for transfers between devices, shards(): sums = lax.all_to_all(sums, 'freq', split_axis=0, concat_axis=0, tiled=True)  4.5 us
  transfers between devices with their start and end apart: 8, of which 6 were waited for; matrix products, arithmetic and copies ran while one was open for 0% of the time, Pallas kernels for 10%

profile of v4, /device:TPU:1, one launch (start us, length us, event | category | flops | bytes accessed | tf_op | source)
XLA Modules:
  0.0 94.5 jit_solution(9003043307184811733)
XLA Ops:
  0.6 1.5 %shard_map.104 = (f32[2384,128]{1,0:T(8,128)S(1)}, bf16[16,2304]{1,0:T(8,128)(2,1)S(1)}, f32[2,72,128]{2,1,0:T(8,128)S(1)}) custom-call(bf16[36,64,128]{2,1,0:T(8,128)(2,1)} %bitcast.4, s32[64,128]{1,0:T(8,128)} %refs_4_.3, f32[32,36]{1,0:T(8,128)} %refs_4_.2, f32[32,36]{1,0:T(8,128)} %refs_5_.2), custom_call_target="tpu_custom_call" | custom-call | bytes 1999872 | tf_op jit(solution)/shard_map/pallas_call | solution.py:50
  2.1 6.9 %collective-permute-start.1 = (bf16[16,2304]{1,0:T(8,128)(2,1)S(1)}, bf16[16,2304]{1,0:T(8,128)(2,1)S(1)}, u32[]{:S(2)}, u32[]{:S(2)}) collective-permute-start(bf16[16,2304]{1,0:T(8,128)(2,1)S(1)} %get-tuple-element.27), channel_id=1, source_target_pairs={{32,0},{64,32},{96,64},{128,96},{160,128},{192,160},{224,192},{256... | collective-permute-start | bytes 221192 | tf_op jit(solution)/shard_map/ppermute | solution.py:388
  9.0 0.0 collective-permute-start
  9.0 0.7 shard_map.105
  9.7 0.2 collective-permute-done.1.refs_3_
  9.9 3.0 %collective-permute-done.refs_2_ = bf16[16,2304]{1,0:T(8,128)(2,1)S(1)} collective-permute-done((bf16[16,2304]{1,0:T(8,128)(2,1)S(1)}, bf16[16,2304]{1,0:T(8,128)(2,1)S(1)}, u32[]{:S(2)}, u32[]{:S(2)}) %collective-permute-start) | collective-permute-done | bytes 73760 | tf_op jit(solution)/shard_map/ppermute | solution.py:387
  12.9 0.0 copy-start
  12.9 1.2 %shard_map.106 = bf16[32,72,128]{2,1,0:T(8,128)(2,1)} custom-call(f32[32,72,128]{2,1,0:T(8,128)S(1)} %get-tuple-element.25.refs_0_, f32[72,128]{1,0:T(8,128)S(1)} %get-tuple-element.26.refs_1_, bf16[16,2304]{1,0:T(8,128)(2,1)S(1)} %collective-permute-done.refs_2_, bf16[16,2304]{1,0:T(8,128)(2,1)S(1)} %collective-permute-done.1.refs_3_), custom_call_target="tpu_custom_call" | custom-call | bytes 1953792 | tf_op jit(solution)/shard_map/pallas_call | solution.py:50
  14.1 9.7 %all-to-all-start = ((bf16[32,72,128]{2,1,0:T(8,128)(2,1)}), bf16[32,72,128]{2,1,0:T(8,128)(2,1)S(1)}, u32[]{:S(2)}, u32[]{:S(2)}) async-start(bf16[32,72,128]{2,1,0:T(8,128)(2,1)} %shard_map.106), calls=%async_computation | async-start | bytes 1179648 | tf_op jit(solution)/shard_map/all_to_all | solution.py:398
  23.7 0.0 copy-done
  23.7 0.0 copy-start.2
  23.8 1.7 %copy-done.2 = bf16[1152,1152]{1,0:T(8,128)(2,1)S(1)} copy-done((bf16[1152,1152]{1,0:T(8,128)(2,1)S(1)}, bf16[1152,1152]{1,0:T(8,128)(2,1)}, u32[]{:S(2)}) %copy-start.2) | copy-done | bytes 2654232
  25.5 0.0 copy-start.1
  25.5 2.8 %shard_map.107 = (f32[1,256]{1,0:T(1,128)S(1)}, f32[1152,256]{1,0:T(8,128)S(1)}, bf16[1152,256]{1,0:T(8,128)(2,1)S(1)}) custom-call(bf16[2,1152,256]{2,1,0:T(8,128)(2,1)S(1)} %copy-done, bf16[1152,1152]{1,0:T(8,128)(2,1)S(1)} %copy-done.2, f32[32,256]{1,0:T(8,128)} %refs_2_.7, f32[1,64]{1,0:T(1,128)} %bitcast.8, s32[1,256]{1,0:T(1,128)} %bitcast.5), custom_call_target="tpu_custom_call" | custom-call | flops 1358954496 | bytes 5638400 | tf_op jit(solution)/shard_map/pallas_call | solution.py:50
  28.3 0.0 copy-start.3
  28.3 1.0 %copy-done.3 = f32[1152,256]{1,0:T(8,128)} copy-done((f32[1152,256]{1,0:T(8,128)}, f32[1152,256]{1,0:T(8,128)S(1)}, u32[]{:S(2)}) %copy-start.3) | copy-done | bytes 1179672
  29.3 0.0 copy-start.7
  29.3 0.8 copy-done.7
  30.1 0.0 copy-start.9
  30.1 0.0 copy-done.1
  30.1 2.1 %shard_map.108 = (bf16[1152,1152]{1,0:T(8,128)(2,1)S(1)}, f32[1152,256]{1,0:T(8,128)S(1)}, f32[2,1152,128]{2,1,0:T(8,128)S(1)}) custom-call(bf16[2,1152,256]{2,1,0:T(8,128)(2,1)S(1)} %copy-done.1, bf16[1152,1152]{1,0:T(8,128)(2,1)S(1)} %copy-done.2, f32[32,256]{1,0:T(8,128)} %refs_2_.7, f32[1,256]{1,0:T(1,128)S(1)} %get-tuple-element.30.refs_3_, ...), custom_call_target="tpu_custom_call" | custom-call | flops 679477248 | bytes 8890368 | tf_op jit(solution)/shard_map/pallas_call | solution.py:50
  32.2 0.0 copy-done.9
  32.3 0.0 copy-start.4
  32.3 1.0 %copy-done.4 = f32[2,1152,128]{2,1,0:T(8,128)} copy-done((f32[2,1152,128]{2,1,0:T(8,128)}, f32[2,1152,128]{2,1,0:T(8,128)S(1)}, u32[]{:S(2)}) %copy-start.4) | copy-done | bytes 1179672
  33.3 0.0 copy-start.6
  33.3 1.0 %copy-done.6 = f32[1152,256]{1,0:T(8,128)} copy-done((f32[1152,256]{1,0:T(8,128)}, f32[1152,256]{1,0:T(8,128)S(1)}, u32[]{:S(2)}) %copy-start.6) | copy-done | bytes 1179672
  34.3 2.9 %all-to-all-done.refs_0_ = bf16[32,72,128]{2,1,0:T(8,128)(2,1)S(1)} async-done(((bf16[32,72,128]{2,1,0:T(8,128)(2,1)}), bf16[32,72,128]{2,1,0:T(8,128)(2,1)S(1)}, u32[]{:S(2)}, u32[]{:S(2)}) %all-to-all-start) | async-done | bytes 589856 | tf_op jit(solution)/shard_map/all_to_all | solution.py:398
  37.2 0.0 copy-start.5
  37.2 0.0 copy-start.8
  37.2 3.7 %shard_map.109 = (bf16[1152,128]{1,0:T(8,128)(2,1)S(1)}, bf16[1152,128]{1,0:T(8,128)(2,1)S(1)}, bf16[16,1152]{1,0:T(8,128)(2,1)S(1)}, f32[8,256]{1,0:T(8,128)S(1)}) custom-call(bf16[32,72,128]{2,1,0:T(8,128)(2,1)S(1)} %all-to-all-done.refs_0_, bf16[1152,1152]{1,0:T(8,128)(2,1)S(1)} %get-tuple-element.31.refs_1_, f32[32,256]{1,0:T(8,128)} %refs_2_.7, ...), custom_call_target="tpu_custom_call" | custom-call | flops 1358954496 | bytes 6304768 | tf_op jit(solution)/shard_map/pallas_call | solution.py:50
  40.9 1.3 %collective-permute-start.2 = (bf16[1152,128]{1,0:T(8,128)(2,1)S(1)}, bf16[1152,128]{1,0:T(8,128)(2,1)S(1)}, u32[]{:S(2)}, u32[]{:S(2)}) collective-permute-start(bf16[1152,128]{1,0:T(8,128)(2,1)S(1)} %get-tuple-element.33.refs_0_), channel_id=1, source_target_pairs={{1,0},{2,1},{3,2},{4,3},{5,4},{6,5},{7,6},{8,7},{9,8},{10,9},{11,1... | collective-permute-start | bytes 884744 | tf_op jit(solution)/shard_map/ppermute | solution.py:374
  42.2 4.0 %collective-permute-start.3 = (bf16[1152,128]{1,0:T(8,128)(2,1)S(1)}, bf16[1152,128]{1,0:T(8,128)(2,1)S(1)}, u32[]{:S(2)}, u32[]{:S(2)}) collective-permute-start(bf16[1152,128]{1,0:T(8,128)(2,1)S(1)} %get-tuple-element.34.refs_1_), channel_id=1, source_target_pairs={{0,1},{1,2},{2,3},{3,4},{4,5},{5,6},{6,7},{7,8},{8,9},{9,10},{10,1... | collective-permute-start | bytes 884744 | tf_op jit(solution)/shard_map/ppermute | solution.py:375
  46.2 7.4 %collective-permute-start.5 = (bf16[16,1152]{1,0:T(8,128)(2,1)S(1)}, bf16[16,1152]{1,0:T(8,128)(2,1)S(1)}, u32[]{:S(2)}, u32[]{:S(2)}) collective-permute-start(bf16[16,1152]{1,0:T(8,128)(2,1)S(1)} %get-tuple-element.35), channel_id=1, source_target_pairs={{32,0},{64,32},{96,64},{128,96},{160,128},{192,160},{224,192},{256... | collective-permute-start | bytes 110600 | tf_op jit(solution)/shard_map/ppermute | solution.py:377
  53.6 0.0 collective-permute-start.4
  53.6 0.9 collective-permute-done.5.refs_5_
  54.5 1.8 %collective-permute-done.4.refs_4_ = bf16[16,1152]{1,0:T(8,128)(2,1)S(1)} collective-permute-done((bf16[16,1152]{1,0:T(8,128)(2,1)S(1)}, bf16[16,1152]{1,0:T(8,128)(2,1)S(1)}, u32[]{:S(2)}, u32[]{:S(2)}) %collective-permute-start.4) | collective-permute-done | bytes 36896 | tf_op jit(solution)/shard_map/ppermute | solution.py:376
  56.3 0.0 collective-permute-done.2.refs_2_
  56.3 0.0 collective-permute-done.3.refs_3_
  56.3 0.0 copy-done.5
  56.3 0.0 copy-done.8
  56.3 2.4 %shard_map.110 = (bf16[1152,256]{1,0:T(8,128)(2,1)S(1)}, f32[32,1,128]{2,1,0:T(1,128)}) custom-call(bf16[1152,128]{1,0:T(8,128)(2,1)S(1)} %get-tuple-element.33.refs_0_, bf16[1152,128]{1,0:T(8,128)(2,1)S(1)} %get-tuple-element.34.refs_1_, bf16[1152,128]{1,0:T(8,128)(2,1)S(1)} %collective-permute-done.2.refs_2_, ...), custom_call_target="tpu_custom_call" | custom-call | bytes 3638272 | tf_op jit(solution)/shard_map/pallas_call | solution.py:50
  58.8 7.5 %all-to-all-start.1 = ((f32[32,1,128]{2,1,0:T(1,128)}), f32[32,1,128]{2,1,0:T(1,128)S(1)}, u32[]{:S(2)}, u32[]{:S(2)}) async-start(f32[32,1,128]{2,1,0:T(1,128)} %get-tuple-element.41), calls=%async_computation.1 | async-start | bytes 32768 | tf_op jit(solution)/shard_map/all_to_all | solution.py:447
  66.3 4.1 %shard_map.111 = bf16[1152,256]{1,0:T(8,128)(2,1)} custom-call(bf16[1152,256]{1,0:T(8,128)(2,1)S(1)} %get-tuple-element.39.refs_0_, bf16[1152,1152]{1,0:T(8,128)(2,1)S(1)} %get-tuple-element.31.refs_1_, f32[32,256]{1,0:T(8,128)} %refs_2_.7, f32[1,256]{1,0:T(1,128)} %copy-done.9, f32[1152,256]{1,0:T(8,128)} %copy-done.3, bf16[2,1152,256]{2,1,0:T(8,128)(2,1)} %refs_5_.3), custom_call_target="tpu_custom_call" | custom-call | flops 1358954496 | bytes 6226944 | tf_op jit(solution)/shard_map/pallas_call | solution.py:50
  70.4 4.5 %all-to-all-done.1.refs_0_ = f32[32,1,128]{2,1,0:T(1,128)S(1)} async-done(((f32[32,1,128]{2,1,0:T(1,128)}), f32[32,1,128]{2,1,0:T(1,128)S(1)}, u32[]{:S(2)}, u32[]{:S(2)}) %all-to-all-start.1) | async-done | bytes 16416 | tf_op jit(solution)/shard_map/all_to_all | solution.py:447
  74.9 19.0 %all_to_all.15.refs_0_ = f32[16,1,128]{2,1,0:T(1,128)S(1)} all-to-all(f32[16,1,128]{2,1,0:T(1,128)S(1)} %shard_map.112), channel_id=1, replica_groups=mesh['geo'=16,'freq'=32] {'geo'}, dimensions={0} | all-to-all | bytes 16384 | tf_op jit(solution)/shard_map/all_to_all | solution.py:458
  94.0 0.5 shard_map.113
  (1 shorter events, 0.0 us)
Async XLA Ops:
  2.1 7.8 %collective-permute-start.1 = (bf16[16,2304]{1,0:T(8,128)(2,1)S(1)}, bf16[16,2304]{1,0:T(8,128)(2,1)S(1)}, u32[]{:S(2)}, u32[]{:S(2)}) collective-permute-start(bf16[16,2304]{1,0:T(8,128)(2,1)S(1)} %get-tuple-element.27), channel_id=1, source_target_pairs={{32,0},{64,32},{96,64},{128,96},{160,128},{192,160},{224,192},{256... | collective-permute-start | bytes 221192 | tf_op jit(solution)/shard_map/ppermute | solution.py:388
  9.0 3.9 %collective-permute-start = (bf16[16,2304]{1,0:T(8,128)(2,1)S(1)}, bf16[16,2304]{1,0:T(8,128)(2,1)S(1)}, u32[]{:S(2)}, u32[]{:S(2)}) collective-permute-start(bf16[16,2304]{1,0:T(8,128)(2,1)S(1)} %get-tuple-element.27), channel_id=1, source_target_pairs={{0,32},{32,64},{64,96},{96,128},{128,160},{160,192},{192,224},{224... | collective-permute-start | bytes 221192 | tf_op jit(solution)/shard_map/ppermute | solution.py:387
  12.9 10.9 %copy-start = (bf16[2,1152,256]{2,1,0:T(8,128)(2,1)S(1)}, bf16[2,1152,256]{2,1,0:T(8,128)(2,1)}, u32[]{:S(2)}) copy-start(bf16[2,1152,256]{2,1,0:T(8,128)(2,1)} %refs_5_.3) | copy-start | bytes 3538948
  14.1 23.1 %all-to-all-start = ((bf16[32,72,128]{2,1,0:T(8,128)(2,1)}), bf16[32,72,128]{2,1,0:T(8,128)(2,1)S(1)}, u32[]{:S(2)}, u32[]{:S(2)}) async-start(bf16[32,72,128]{2,1,0:T(8,128)(2,1)} %shard_map.106), calls=%async_computation | async-start | bytes 1179648 | tf_op jit(solution)/shard_map/all_to_all | solution.py:398
  23.7 1.8 %copy-start.2 = (bf16[1152,1152]{1,0:T(8,128)(2,1)S(1)}, bf16[1152,1152]{1,0:T(8,128)(2,1)}, u32[]{:S(2)}) copy-start(bf16[1152,1152]{1,0:T(8,128)(2,1)} %refs_1_.5) | copy-start | bytes 7962628
  25.5 4.6 %copy-start.1 = (bf16[2,1152,256]{2,1,0:T(8,128)(2,1)S(1)}, bf16[2,1152,256]{2,1,0:T(8,128)(2,1)}, u32[]{:S(2)}) copy-start(bf16[2,1152,256]{2,1,0:T(8,128)(2,1)} %refs_5_.3) | copy-start | bytes 3538948
  28.3 1.0 %copy-start.3 = (f32[1152,256]{1,0:T(8,128)}, f32[1152,256]{1,0:T(8,128)S(1)}, u32[]{:S(2)}) copy-start(f32[1152,256]{1,0:T(8,128)S(1)} %get-tuple-element.40.refs_4_) | copy-start | bytes 3538948
  29.3 0.8 copy-start.7
  30.1 2.1 %copy-start.9 = (f32[1,256]{1,0:T(1,128)}, f32[1,256]{1,0:T(1,128)S(1)}, u32[]{:S(2)}) copy-start(f32[1,256]{1,0:T(1,128)S(1)} %get-tuple-element.30.refs_3_) | copy-start | bytes 3076
  32.3 1.0 %copy-start.4 = (f32[2,1152,128]{2,1,0:T(8,128)}, f32[2,1152,128]{2,1,0:T(8,128)S(1)}, u32[]{:S(2)}) copy-start(f32[2,1152,128]{2,1,0:T(8,128)S(1)} %get-tuple-element.36.refs_6_) | copy-start | bytes 3538948
  33.3 1.0 %copy-start.6 = (f32[1152,256]{1,0:T(8,128)}, f32[1152,256]{1,0:T(8,128)S(1)}, u32[]{:S(2)}) copy-start(f32[1152,256]{1,0:T(8,128)S(1)} %get-tuple-element.32.refs_5_) | copy-start | bytes 3538948
  37.2 19.2 %copy-start.5 = (f32[2,1152,128]{2,1,0:T(8,128)S(1)}, f32[2,1152,128]{2,1,0:T(8,128)}, u32[]{:S(2)}) copy-start(f32[2,1152,128]{2,1,0:T(8,128)} %copy-done.4) | copy-start | bytes 3538948
  37.2 19.2 %copy-start.8 = (bf16[1152,256]{1,0:T(8,128)(2,1)S(1)}, bf16[1152,256]{1,0:T(8,128)(2,1)}, u32[]{:S(2)}) copy-start(bf16[1152,256]{1,0:T(8,128)(2,1)} %copy-done.7) | copy-start | bytes 1769476
  40.9 15.4 %collective-permute-start.2 = (bf16[1152,128]{1,0:T(8,128)(2,1)S(1)}, bf16[1152,128]{1,0:T(8,128)(2,1)S(1)}, u32[]{:S(2)}, u32[]{:S(2)}) collective-permute-start(bf16[1152,128]{1,0:T(8,128)(2,1)S(1)} %get-tuple-element.33.refs_0_), channel_id=1, source_target_pairs={{1,0},{2,1},{3,2},{4,3},{5,4},{6,5},{7,6},{8,7},{9,8},{10,9},{11,1... | collective-permute-start | bytes 884744 | tf_op jit(solution)/shard_map/ppermute | solution.py:374
  42.2 14.1 %collective-permute-start.3 = (bf16[1152,128]{1,0:T(8,128)(2,1)S(1)}, bf16[1152,128]{1,0:T(8,128)(2,1)S(1)}, u32[]{:S(2)}, u32[]{:S(2)}) collective-permute-start(bf16[1152,128]{1,0:T(8,128)(2,1)S(1)} %get-tuple-element.34.refs_1_), channel_id=1, source_target_pairs={{0,1},{1,2},{2,3},{3,4},{4,5},{5,6},{6,7},{7,8},{8,9},{9,10},{10,1... | collective-permute-start | bytes 884744 | tf_op jit(solution)/shard_map/ppermute | solution.py:375
  46.2 8.3 %collective-permute-start.5 = (bf16[16,1152]{1,0:T(8,128)(2,1)S(1)}, bf16[16,1152]{1,0:T(8,128)(2,1)S(1)}, u32[]{:S(2)}, u32[]{:S(2)}) collective-permute-start(bf16[16,1152]{1,0:T(8,128)(2,1)S(1)} %get-tuple-element.35), channel_id=1, source_target_pairs={{32,0},{64,32},{96,64},{128,96},{160,128},{192,160},{224,192},{256... | collective-permute-start | bytes 110600 | tf_op jit(solution)/shard_map/ppermute | solution.py:377
  53.6 2.7 %collective-permute-start.4 = (bf16[16,1152]{1,0:T(8,128)(2,1)S(1)}, bf16[16,1152]{1,0:T(8,128)(2,1)S(1)}, u32[]{:S(2)}, u32[]{:S(2)}) collective-permute-start(bf16[16,1152]{1,0:T(8,128)(2,1)S(1)} %get-tuple-element.35), channel_id=1, source_target_pairs={{0,32},{32,64},{64,96},{96,128},{128,160},{160,192},{192,224},{224... | collective-permute-start | bytes 110600 | tf_op jit(solution)/shard_map/ppermute | solution.py:376
  58.8 16.1 %all-to-all-start.1 = ((f32[32,1,128]{2,1,0:T(1,128)}), f32[32,1,128]{2,1,0:T(1,128)S(1)}, u32[]{:S(2)}, u32[]{:S(2)}) async-start(f32[32,1,128]{2,1,0:T(1,128)} %get-tuple-element.41), calls=%async_computation.1 | async-start | bytes 32768 | tf_op jit(solution)/shard_map/all_to_all | solution.py:447

commit v5 on v4

--- a/solution.py
+++ b/solution.py
@@ -17,7 +17,7 @@
 OUTSIDE = pl.BlockSpec(memory_space=pl.ANY)
 
 
-def call(kernel, outs, args, scratch=(), flops=0, late=None, outside=(), limit=32):
+def call(kernel, outs, args, scratch=(), flops=0, late=None, outside_outs=(), limit=32):
     late = {} if late is None else late
     places = sorted(late)
     size = sum(a.size * a.dtype.itemsize for a in (*args, *outs))
@@ -50,8 +50,8 @@
     return pl.pallas_call(
         body,
         out_shape=outs,
-        in_specs=[OUTSIDE if i in late or i in outside else WHOLE for i in range(len(args))],
-        out_specs=[WHOLE] * len(outs),
+        in_specs=[OUTSIDE if i in late else WHOLE for i in range(len(args))],
+        out_specs=[OUTSIDE if i in outside_outs else WHOLE for i in range(len(outs))],
         scratch_shapes=[*scratch, *buffers],
         compiler_params=pltpu.CompilerParams(vmem_limit_bytes=limit * MIB),
         cost_estimate=pl.CostEstimate(flops=flops, bytes_accessed=size, transcendentals=0),
@@ -77,10 +77,9 @@
 
 
 def put_edges(from_west, from_east, width, lon):
-    both = jnp.concatenate([from_west.astype(F32)[8:16], from_east.astype(F32)[0:8]], axis=0)
+    both = jnp.concatenate([from_west.astype(F32), from_east.astype(F32)], axis=0).astype(BF16)
     return lax.dot_general(
-        both.astype(BF16), edge_picks(width, lon), (((0,), (0,)), ((), ())),
-        preferred_element_type=F32,
+        both, edge_picks(width, lon), (((0,), (0,)), ((), ())), preferred_element_type=F32
     )
 
 
@@ -92,7 +91,7 @@
 
 
 def regroup_kernel(
-    field_ref, mask_ref, lon_ref, lat_ref, rows_ref, edge_ref, rates_ref, wait
+    field_ref, mask_ref, lon_ref, lat_ref, rows_ref, west_ref, east_ref, rates_ref, wait
 ):
     directions, lat, lon = field_ref.shape
     freqs = lon_ref.shape[0]
@@ -114,7 +113,8 @@
     for d in range(directions):
         rows_ref[pl.ds(PAD + d, lat, stride=directions), :] = field_ref[d].astype(F32) * mask
     edges = take_edges(rows_ref[PAD : PAD + rows, :].astype(BF16), edge_picks(lon, lon))
-    edge_ref[...] = edges.astype(BF16)
+    west_ref[...] = edges[0:8].astype(BF16)
+    east_ref[...] = edges[8:16].astype(BF16)
 
 
 def interior_kernel(rows_ref, rates_ref, part_ref, rate_ref, *, directions):
@@ -136,12 +136,19 @@
         )
 
 
-def edges_kernel(part_ref, rate_ref, west_ref, east_ref, out_ref):
+def edges_kernel(part_ref, rate_ref, west_ref, east_ref, out_any, out_ref, sems):
     peers, height, lon = part_ref.shape
+    groups = blocks_of(peers, 4)
+    copies = []
     cols = put_edges(west_ref[...], east_ref[...], lon, lon)
     rate = rate_ref[...]
-    for r in range(peers):
-        out_ref[r] = (part_ref[r] + rate * cols[r * height : (r + 1) * height]).astype(BF16)
+    for i, group in enumerate(groups):
+        for r in range(group.start, group.stop):
+            out_ref[r] = (part_ref[r] + rate * cols[r * height : (r + 1) * height]).astype(BF16)
+        copies.append(pltpu.make_async_copy(out_ref.at[group], out_any.at[group], sems.at[i]))
+        copies[-1].start()
+    for copy in copies:
+        copy.wait()
 
 
 def spread_rates(courant_refs, turn_scr, rates_scr):
@@ -228,25 +235,27 @@
         next_ref[rows, :] = forward(traj_ref, inter_ref, factor_scr, coeff, rows)[1]
 
 
-def two_substeps(m_scr, r_scr, turned_ref, factor_scr, coeff, ready, write, weigh):
+def two_substeps(carried, turned_ref, kappa_ref, prepare, ready, write, weigh):
+    m_scr, r_scr, factor_scr, product_scr = carried
     components, points = m_scr.shape
-    chunk = components // 4
+    blocks = blocks_of(components, 4)
     weights = jnp.zeros((8, points), F32)
     moved = r_scr[...]
-    for at in range(0, components, chunk):
-        rows = slice(at, at + chunk)
-        pulled = jnp.dot(turned_ref[rows, :], moved, preferred_element_type=F32)
+    for rows in blocks:
+        product_scr[rows, :] = jnp.dot(turned_ref[rows, :], moved, preferred_element_type=F32)
+    coeff = prepare()
+    spread_factor(kappa_ref, factor_scr)
+    for rows in blocks:
         after, state = ready(rows)
         factor, old = factor_scr[rows, :], m_scr[rows, :]
-        new = decay_of(factor, coeff) * old + 0.5 * (after * pulled)
+        new = decay_of(factor, coeff) * old + 0.5 * (after * product_scr[rows, :])
         if weigh:
             terms = factor * (old * after + new * state)
-            weights = weights + terms.reshape(chunk // 8, 8, points).sum(axis=0)
+            weights = weights + terms.reshape(-1, 8, points).sum(axis=0)
         m_scr[rows, :] = new
         r_scr[rows, :] = new.astype(BF16)
     moved = r_scr[...]
-    for at in range(0, components, chunk):
-        rows = slice(at, at + chunk)
+    for rows in blocks:
         pulled = jnp.dot(turned_ref[rows, :], moved, preferred_element_type=F32)
         state = ready(rows)[1]
         new = decay_of(factor_scr[rows, :], coeff) * m_scr[rows, :] + 0.5 * (state * pulled)
@@ -256,68 +265,90 @@
 
 def first_kernel(
     moved_ref, turned_ref, kappa_ref, coeff_ref, mask_ref, next_ref, traj_ref,
-    low_ref, high_ref, edge_ref, weights_ref, m_scr, r_scr, factor_scr, wait,
+    low_ref, high_ref, west_ref, east_ref, weights_ref, *carried, wait,
 ):
     freqs, height, lon = moved_ref.shape
     points = 2 * lon
     directions = height // 2
+    m_scr, r_scr = carried[:2]
     for f in range(freqs):
         block = moved_ref[f].astype(F32)
         rows = slice(f * directions, (f + 1) * directions)
         m_scr[rows, 0:lon] = block[0:directions]
         m_scr[rows, lon:points] = block[directions:height]
     r_scr[...] = m_scr[...].astype(BF16)
-    wait(2, 3, 4)
-    spread_factor(kappa_ref, factor_scr)
-    mask = mask_ref[pl.ds(2 * lax.axis_index("freq"), 2), :].astype(F32)
-    wait(5, 6)
+
+    def prepare():
+        wait(2, 3, 5, 6)
+        return coeff_ref[...]
+
+    def masks():
+        return mask_ref[pl.ds(2 * lax.axis_index("freq"), 2), :].astype(F32)
 
     def ready(rows):
         return next_ref[rows, :], traj_ref[rows, :].astype(F32)
 
     def write(rows, values):
+        if rows.start == 0:
+            wait(4)
+        mask = masks()
         low = (values[:, 0:lon] * mask[0:1]).astype(BF16)
         high = (values[:, lon:points] * mask[1:2]).astype(BF16)
         low_ref[rows, :] = low
         high_ref[rows, :] = high
 
     weights_ref[...] = two_substeps(
-        m_scr, r_scr, turned_ref, factor_scr, coeff_ref[...], ready, write, True
+        carried, turned_ref, kappa_ref, prepare, ready, write, True
     )
     picks = edge_picks(points, lon)
     edges = take_edges(low_ref[...], picks[:, 0:lon]) + take_edges(high_ref[...], picks[:, lon:points])
-    edge_ref[...] = edges.astype(BF16)
-
-
-def halo_kernel(
-    low_ref, high_ref, north_ref, south_ref, west_ref, east_ref, rates_ref, pull_ref, own_ref, sed_ref,
-    moved_ref, sums_ref, wait,
+    west_ref[...] = edges[0:8].astype(BF16)
+    east_ref[...] = edges[8:16].astype(BF16)
+
+
+def inner_kernel(
+    low_ref, high_ref, courant_ref, part_ref, edge_rate_ref, north_rate_ref, south_rate_ref
 ):
     components, lon = low_ref.shape
-    cols = put_edges(west_ref[...], east_ref[...], 2 * lon, lon)
-    weights = [own_ref[:, 0:lon], own_ref[:, lon : 2 * lon]]
     chunk = 144
     lane = lax.broadcasted_iota(jnp.int32, (chunk, lon), 1)
     for rows in blocks_of(components, components // chunk):
         low, high = low_ref[rows, :].astype(F32), high_ref[rows, :].astype(F32)
-        above, below = north_ref[rows, :].astype(F32), south_ref[rows, :].astype(F32)
-        rates = split_rates(rates_ref[0, rows, :], rates_ref[1, rows, :])
-        for half, (here, up, down) in enumerate(((low, high, below), (high, above, low))):
+        center, east, west, north, south = split_rates(
+            courant_ref[0, rows, :], courant_ref[1, rows, :]
+        )
+        edge_rate_ref[rows, :] = jnp.where(lane == 0, west, east)
+        north_rate_ref[rows, :] = north
+        south_rate_ref[rows, :] = south
+        east = jnp.where(lane == lon - 1, 0.0, east)
+        west = jnp.where(lane == 0, 0.0, west)
+        for half, (here, rate, other) in enumerate(((low, north, high), (high, south, low))):
+            part_ref[rows, half * lon : (half + 1) * lon] = (
+                center * here
+                + east * pltpu.roll(here, lon - 1, 1)
+                + west * pltpu.roll(here, 1, 1)
+                + rate * other
+            )
+
+
+def halo_kernel(
+    part_ref, edge_rate_ref, north_rate_ref, south_rate_ref, north_ref, south_ref, west_ref, east_ref,
+    pull_ref, own_ref, sed_ref, moved_ref, sums_ref, wait,
+):
+    components, lon = north_ref.shape
+    cols = put_edges(west_ref[...], east_ref[...], 2 * lon, lon)
+    weights = [own_ref[:, 0:lon], own_ref[:, lon : 2 * lon]]
+    for rows in blocks_of(components, components // 144):
+        edge_rate = edge_rate_ref[rows, :]
+        below = south_rate_ref[rows, :] * south_ref[rows, :].astype(F32)
+        above = north_rate_ref[rows, :] * north_ref[rows, :].astype(F32)
+        for half, outer in enumerate((below, above)):
             lanes = slice(half * lon, (half + 1) * lon)
-            edge = cols[rows, lanes]
-            east = jnp.where(lane == lon - 1, edge, pltpu.roll(here, lon - 1, 1))
-            west = jnp.where(lane == 0, edge, pltpu.roll(here, 1, 1))
-            value = (
-                rates[0] * here
-                + rates[1] * east
-                + rates[2] * west
-                + rates[3] * up
-                + rates[4] * down
-            ).astype(BF16)
+            value = (part_ref[rows, lanes] + outer + edge_rate * cols[rows, lanes]).astype(BF16)
             moved_ref[rows, lanes] = value
             terms = value.astype(F32) * pull_ref[rows, lanes].astype(F32)
-            weights[half] = weights[half] + terms.reshape(chunk // 8, 8, lon).sum(axis=0)
-    wait(9)
+            weights[half] = weights[half] + terms.reshape(-1, 8, lon).sum(axis=0)
+    wait(10)
     groups, points = sums_ref.shape[2], 2 * lon
     hits = (lax.broadcasted_iota(jnp.int32, (groups, points), 0) == sed_ref[...]).astype(F32)
     sums = lax.dot_general(
@@ -328,22 +359,31 @@
 
 
 def last_kernel(
-    moved_ref, turned_ref, kappa_ref, coeff_ref, next_ref, traj_ref, out_ref,
-    m_scr, r_scr, factor_scr, wait,
-):
+    moved_ref, turned_ref, kappa_ref, coeff_ref, next_ref, traj_ref, out_any, *carried, wait
+):
+    *carried, out_ref, sems = carried
+    copies = []
+    m_scr, r_scr = carried[:2]
     r_scr[...] = moved_ref[...]
     m_scr[...] = moved_ref[...].astype(F32)
-    wait(2, 3)
-    spread_factor(kappa_ref, factor_scr)
-    wait(4, 5)
+
+    def prepare():
+        wait(2, 3, 4, 5)
+        return coeff_ref[...]
 
     def ready(rows):
         return next_ref[rows, :], traj_ref[rows, :].astype(F32)
 
     def write(rows, values):
         out_ref[rows, :] = values.astype(BF16)
-
-    two_substeps(m_scr, r_scr, turned_ref, factor_scr, coeff_ref[...], ready, write, False)
+        copies.append(
+            pltpu.make_async_copy(out_ref.at[rows, :], out_any.at[rows, :], sems.at[len(copies)])
+        )
+        copies[-1].start()
+
+    two_substeps(carried, turned_ref, kappa_ref, prepare, ready, write, False)
+    for copy in copies:
+        copy.wait()
 
 
 def add_kernel(parts_ref, out_ref):
@@ -369,30 +409,39 @@
     northward = [(i, i + 1) for i in range(peers - 1)]
     southward = [(j, i) for i, j in northward]
 
-    def swap(low, high, edges):
+    def swap(low, high, west, east):
         return (
             lax.ppermute(low, "freq", southward),
             lax.ppermute(high, "freq", northward),
-            lax.ppermute(edges, "geo", eastward),
-            lax.ppermute(edges, "geo", westward),
+            lax.ppermute(east, "geo", eastward),
+            lax.ppermute(west, "geo", westward),
         )
 
     field = adjoint_final.reshape(directions, lat, lon)
-    grouped, edges, own_rates = call(
+    grouped, west, east, own_rates = call(
         regroup_kernel,
-        [shape((rows + 2 * PAD, lon), F32), shape((16, rows), BF16), shape((2, height, lon), F32)],
+        [
+            shape((rows + 2 * PAD, lon), F32),
+            shape((8, rows), BF16),
+            shape((8, rows), BF16),
+            shape((2, height, lon), F32),
+        ],
         [field, sea_mask, courant_lon, courant_lat],
         late={0: None, 1: None, 2: None, 3: None},
     )
-    from_west = lax.ppermute(edges, "geo", eastward)
-    from_east = lax.ppermute(edges, "geo", westward)
+    from_west = lax.ppermute(east, "geo", eastward)
+    from_east = lax.ppermute(west, "geo", westward)
     part, rate = call(
         functools.partial(interior_kernel, directions=directions),
         [shape((peers, height, lon), F32), shape((height, lon), F32)],
         [grouped, own_rates],
     )
     (sent,) = call(
-        edges_kernel, [shape((peers, height, lon), BF16)], [part, rate, from_west, from_east]
+        edges_kernel,
+        [shape((peers, height, lon), BF16)],
+        [part, rate, from_west, from_east],
+        [pltpu.VMEM((peers, height, lon), BF16), pltpu.SemaphoreType.DMA((4,))],
+        outside_outs=(0,),
     )
     sent, point_factor = lax.optimization_barrier((sent, friction_factor))
     moved = lax.all_to_all(sent, "freq", split_axis=0, concat_axis=0, tiled=True)
@@ -422,13 +471,14 @@
         flops=product,
         late={2: None, 4: None, 5: None},
     )
-    carried = [pltpu.VMEM(full, F32), pltpu.VMEM(full, BF16), pltpu.VMEM(full, F32)]
-    low, high, edges, weights = call(
+    carried = [pltpu.VMEM(full, kind) for kind in (F32, BF16, F32, F32)]
+    low, high, west, east, weights = call(
         first_kernel,
         [
             shape(half_full, BF16),
             shape(half_full, BF16),
-            shape((16, components), BF16),
+            shape((8, components), BF16),
+            shape((8, components), BF16),
             shape((8, points), F32),
         ],
         [moved, turned, friction_factor, coeff, sea_mask, next1, trajectory],
@@ -436,22 +486,27 @@
         flops=2 * product,
         late={2: None, 3: None, 4: None, 5: None, 6: 1},
     )
+    swapped = swap(low, high, west, east)
+    inner = call(
+        inner_kernel,
+        [shape(full, F32), shape(half_full, F32), shape(half_full, F32), shape(half_full, F32)],
+        [low, high, rates],
+    )
     moved, sums = call(
         halo_kernel,
         [shape(full, BF16), shape((peers, 1, 128), F32)],
-        [
-            low, high, *swap(low, high, edges), rates, pull, weights, sediment.reshape(1, points),
-        ],
-        late={9: None},
+        [*inner, *swapped, pull, weights, sediment.reshape(1, points)],
+        late={10: None},
     )
     sums = lax.all_to_all(sums, "freq", split_axis=0, concat_axis=0, tiled=True)
     (result,) = call(
         last_kernel,
         [shape(full, BF16)],
         [moved, turned, friction_factor, coeff, next0, trajectory],
-        carried,
+        [*carried, pltpu.VMEM(full, BF16), pltpu.SemaphoreType.DMA((4,))],
         flops=2 * product,
         late={2: None, 3: None, 4: None, 5: 0},
+        outside_outs=(0,),
     )
     result, sums = lax.optimization_barrier((result, sums))
     (sums,) = call(add_kernel, [shape((regions, 1, 128), F32)], [sums])

time: 95 us -> 94.4 us (level)
  blocking collectives: 19 us -> 23.4 us
  waiting for transfers between devices: 13.2 us -> 9.01 us
    ppermute x4, waiting for transfers between devices: 5.87 us -> 1.28 us  [the longest x1 1.11 us: swap(): lax.ppermute(west, 'geo', westward)]
    all_to_all x1, blocking collectives: 19 us -> 23.4 us  [shards(): sums = lax.all_to_all(sums, 'geo', split_axis=0, concat_axis=0, tiled=True)]
    pallas_call x10 -> x11, Pallas kernels: 19 us -> 18.9 us  [call(): pl.pallas_call(body, out_shape=outs, in_specs=[OUTSIDE if i in late else...]
  transfers between devices with their start and end apart: 8 -> 8, of which waited for: 6 -> 4; matrix products, arithmetic and copies ran while one was open for 0% -> 0% of each run, Pallas kernels for 10% -> 11%
where the time goes in v5:
time: 94.4 us; the launch traced here: 93.9 us
  starting transfers between devices  36.2 us (38%)
  blocking collectives  23.4 us (25%)
  Pallas kernels  18.9 us (20%)
  waiting for transfers between devices  9.01 us (10%)
  local copies, waits for them, and re-layouts  5.66 us (6%)
    all_to_all x1, blocking collectives, shards(): sums = lax.all_to_all(sums, 'geo', split_axis=0, concat_axis=0, tiled=True)  23.4 us
    pallas_call x11, Pallas kernels, call(): pl.pallas_call(body, out_shape=outs, in_specs=[OUTSIDE if i in late else...  18.9 us
    all_to_all x1, starting transfers between devices, shards(): lax.all_to_all(sent, 'freq', split_axis=0, concat_axis=0, tiled=True)  8.78 us
    all_to_all x1, starting transfers between devices, shards(): sums = lax.all_to_all(sums, 'freq', split_axis=0, concat_axis=0, tiled=True)  7.29 us
    ppermute x1, starting transfers between devices, swap(): lax.ppermute(east, 'geo', eastward)  6.1 us
    unnamed x20, local copies, waits for them, and re-layouts  5.66 us
    all_to_all x1, waiting for transfers between devices, shards(): sums = lax.all_to_all(sums, 'freq', split_axis=0, concat_axis=0, tiled=True)  4.84 us
    ppermute x1, starting transfers between devices, swap(): lax.ppermute(high, 'freq', northward)  4 us
  transfers between devices with their start and end apart: 8, of which 4 were waited for; matrix products, arithmetic and copies ran while one was open for 0% of the time, Pallas kernels for 11%

profile of v5, /device:TPU:1, one launch (start us, length us, event | category | flops | bytes accessed | tf_op | source)
XLA Modules:
  0.0 93.9 jit_solution(8972902124200691986)
XLA Ops:
  0.6 1.5 %shard_map.104 = (f32[2384,128]{1,0:T(8,128)S(1)}, bf16[8,2304]{1,0:T(8,128)(2,1)S(1)}, bf16[8,2304]{1,0:T(8,128)(2,1)S(1)}, f32[2,72,128]{2,1,0:T(8,128)S(1)}) custom-call(bf16[36,64,128]{2,1,0:T(8,128)(2,1)} %bitcast.4, s32[64,128]{1,0:T(8,128)} %refs_4_.3, f32[32,36]{1,0:T(8,128)} %refs_4_.2, f32[32,36]{1,0:T(8,128)} %refs_5_.2), custom_call_target="tpu_custom_call" | custom-call | bytes 1999872 | tf_op jit(solution)/shard_map/pallas_call | solution.py:50
  2.1 3.5 %collective-permute-start = (bf16[8,2304]{1,0:T(8,128)(2,1)S(1)}, bf16[8,2304]{1,0:T(8,128)(2,1)S(1)}, u32[]{:S(2)}, u32[]{:S(2)}) collective-permute-start(bf16[8,2304]{1,0:T(8,128)(2,1)S(1)} %get-tuple-element.33), channel_id=1, source_target_pairs={{0,32},{32,64},{64,96},{96,128},{128,160},{160,192},{192,224},{224... | collective-permute-start | bytes 110600 | tf_op jit(solution)/shard_map/ppermute | solution.py:432
  5.6 3.4 %collective-permute-start.1 = (bf16[8,2304]{1,0:T(8,128)(2,1)S(1)}, bf16[8,2304]{1,0:T(8,128)(2,1)S(1)}, u32[]{:S(2)}, u32[]{:S(2)}) collective-permute-start(bf16[8,2304]{1,0:T(8,128)(2,1)S(1)} %get-tuple-element.34), channel_id=1, source_target_pairs={{32,0},{64,32},{96,64},{128,96},{160,128},{192,160},{224,192},{256... | collective-permute-start | bytes 110600 | tf_op jit(solution)/shard_map/ppermute | solution.py:433
  9.0 0.7 shard_map.105
  9.7 0.0 collective-permute-done.refs_2_
  9.7 0.2 collective-permute-done.1.refs_3_
  9.9 0.0 copy-start
  9.9 1.1 %shard_map.106 = bf16[32,72,128]{2,1,0:T(8,128)(2,1)} custom-call(f32[32,72,128]{2,1,0:T(8,128)S(1)} %get-tuple-element.31.refs_0_, f32[72,128]{1,0:T(8,128)S(1)} %get-tuple-element.32.refs_1_, bf16[8,2304]{1,0:T(8,128)(2,1)S(1)} %collective-permute-done.refs_2_, bf16[8,2304]{1,0:T(8,128)(2,1)S(1)} %collective-permute-done.1.refs_3_), custom_call_target="tpu_custom_call" | custom-call | bytes 1880064 | tf_op jit(solution)/shard_map/pallas_call | solution.py:50
  11.1 8.8 %all-to-all-start = ((bf16[32,72,128]{2,1,0:T(8,128)(2,1)}), bf16[32,72,128]{2,1,0:T(8,128)(2,1)S(1)}, u32[]{:S(2)}, u32[]{:S(2)}) async-start(bf16[32,72,128]{2,1,0:T(8,128)(2,1)} %shard_map.106), calls=%async_computation | async-start | bytes 1179648 | tf_op jit(solution)/shard_map/all_to_all | solution.py:447
  19.8 0.0 copy-done
  19.8 0.0 copy-start.2
  19.9 1.7 %copy-done.2 = bf16[1152,1152]{1,0:T(8,128)(2,1)S(1)} copy-done((bf16[1152,1152]{1,0:T(8,128)(2,1)S(1)}, bf16[1152,1152]{1,0:T(8,128)(2,1)}, u32[]{:S(2)}) %copy-start.2) | copy-done | bytes 2654232
  21.6 0.0 copy-start.1
  21.6 2.8 %shard_map.107 = (f32[1,256]{1,0:T(1,128)S(1)}, f32[1152,256]{1,0:T(8,128)S(1)}, bf16[1152,256]{1,0:T(8,128)(2,1)S(1)}) custom-call(bf16[2,1152,256]{2,1,0:T(8,128)(2,1)S(1)} %copy-done, bf16[1152,1152]{1,0:T(8,128)(2,1)S(1)} %copy-done.2, f32[32,256]{1,0:T(8,128)} %refs_2_.7, f32[1,64]{1,0:T(1,128)} %bitcast.8, s32[1,256]{1,0:T(1,128)} %bitcast.5), custom_call_target="tpu_custom_call" | custom-call | flops 1358954496 | bytes 5638400 | tf_op jit(solution)/shard_map/pallas_call | solution.py:50
  24.4 0.0 copy-start.3
  24.4 1.0 %copy-done.3 = f32[1152,256]{1,0:T(8,128)} copy-done((f32[1152,256]{1,0:T(8,128)}, f32[1152,256]{1,0:T(8,128)S(1)}, u32[]{:S(2)}) %copy-start.3) | copy-done | bytes 1179672
  25.4 0.0 copy-start.7
  25.4 0.8 copy-done.7
  26.3 0.0 copy-start.9
  26.3 0.0 copy-done.1
  26.3 2.1 %shard_map.108 = (bf16[1152,1152]{1,0:T(8,128)(2,1)S(1)}, f32[1152,256]{1,0:T(8,128)S(1)}, f32[2,1152,128]{2,1,0:T(8,128)S(1)}) custom-call(bf16[2,1152,256]{2,1,0:T(8,128)(2,1)S(1)} %copy-done.1, bf16[1152,1152]{1,0:T(8,128)(2,1)S(1)} %copy-done.2, f32[32,256]{1,0:T(8,128)} %refs_2_.7, f32[1,256]{1,0:T(1,128)S(1)} %get-tuple-element.37.refs_3_, ...), custom_call_target="tpu_custom_call" | custom-call | flops 679477248 | bytes 8890368 | tf_op jit(solution)/shard_map/pallas_call | solution.py:50
  28.4 0.0 copy-done.9
  28.4 0.0 copy-start.4
  28.4 1.0 %copy-done.4 = f32[2,1152,128]{2,1,0:T(8,128)} copy-done((f32[2,1152,128]{2,1,0:T(8,128)}, f32[2,1152,128]{2,1,0:T(8,128)S(1)}, u32[]{:S(2)}) %copy-start.4) | copy-done | bytes 1179672
  29.4 0.0 copy-start.6
  29.4 1.0 %copy-done.6 = f32[1152,256]{1,0:T(8,128)} copy-done((f32[1152,256]{1,0:T(8,128)}, f32[1152,256]{1,0:T(8,128)S(1)}, u32[]{:S(2)}) %copy-start.6) | copy-done | bytes 1179672
  30.4 2.9 %all-to-all-done.refs_0_ = bf16[32,72,128]{2,1,0:T(8,128)(2,1)S(1)} async-done(((bf16[32,72,128]{2,1,0:T(8,128)(2,1)}), bf16[32,72,128]{2,1,0:T(8,128)(2,1)S(1)}, u32[]{:S(2)}, u32[]{:S(2)}) %all-to-all-start) | async-done | bytes 589856 | tf_op jit(solution)/shard_map/all_to_all | solution.py:447
  33.3 0.0 copy-start.5
  33.3 4.1 %shard_map.109 = (bf16[1152,128]{1,0:T(8,128)(2,1)S(1)}, bf16[1152,128]{1,0:T(8,128)(2,1)S(1)}, bf16[8,1152]{1,0:T(8,128)(2,1)S(1)}, bf16[8,1152]{1,0:T(8,128)(2,1)S(1)}, f32[8,256]{1,0:T(8,128)S(1)}) custom-call(bf16[32,72,128]{2,1,0:T(8,128)(2,1)S(1)} %all-to-all-done.refs_0_, bf16[1152,1152]{1,0:T(8,128)(2,1)S(1)} %get-tuple-element.38.refs_1_, ...), custom_call_target="tpu_custom_call" | custom-call | flops 1358954496 | bytes 6304768 | tf_op jit(solution)/shard_map/pallas_call | solution.py:50
  37.4 0.0 copy-start.8
  37.4 1.4 %collective-permute-start.2 = (bf16[1152,128]{1,0:T(8,128)(2,1)S(1)}, bf16[1152,128]{1,0:T(8,128)(2,1)S(1)}, u32[]{:S(2)}, u32[]{:S(2)}) collective-permute-start(bf16[1152,128]{1,0:T(8,128)(2,1)S(1)} %get-tuple-element.40.refs_0_), channel_id=1, source_target_pairs={{1,0},{2,1},{3,2},{4,3},{5,4},{6,5},{7,6},{8,7},{9,8},{10,9},{11,1... | collective-permute-start | bytes 884744 | tf_op jit(solution)/shard_map/ppermute | solution.py:414
  38.8 4.0 %collective-permute-start.3 = (bf16[1152,128]{1,0:T(8,128)(2,1)S(1)}, bf16[1152,128]{1,0:T(8,128)(2,1)S(1)}, u32[]{:S(2)}, u32[]{:S(2)}) collective-permute-start(bf16[1152,128]{1,0:T(8,128)(2,1)S(1)} %get-tuple-element.41.refs_1_), channel_id=1, source_target_pairs={{0,1},{1,2},{2,3},{3,4},{4,5},{5,6},{6,7},{7,8},{8,9},{9,10},{10,1... | collective-permute-start | bytes 884744 | tf_op jit(solution)/shard_map/ppermute | solution.py:415
  42.8 6.1 %collective-permute-start.4 = (bf16[8,1152]{1,0:T(8,128)(2,1)S(1)}, bf16[8,1152]{1,0:T(8,128)(2,1)S(1)}, u32[]{:S(2)}, u32[]{:S(2)}) collective-permute-start(bf16[8,1152]{1,0:T(8,128)(2,1)S(1)} %get-tuple-element.47), channel_id=1, source_target_pairs={{0,32},{32,64},{64,96},{96,128},{128,160},{160,192},{192,224},{224... | collective-permute-start | bytes 55304 | tf_op jit(solution)/shard_map/ppermute | solution.py:416
  48.9 1.7 %collective-permute-start.5 = (bf16[8,1152]{1,0:T(8,128)(2,1)S(1)}, bf16[8,1152]{1,0:T(8,128)(2,1)S(1)}, u32[]{:S(2)}, u32[]{:S(2)}) collective-permute-start(bf16[8,1152]{1,0:T(8,128)(2,1)S(1)} %get-tuple-element.48), channel_id=1, source_target_pairs={{32,0},{64,32},{96,64},{128,96},{160,128},{192,160},{224,192},{256... | collective-permute-start | bytes 55304 | tf_op jit(solution)/shard_map/ppermute | solution.py:417
  50.6 0.0 copy-done.5
  50.6 0.7 shard_map.110
  51.3 0.0 collective-permute-done.4.refs_6_
  51.3 1.1 %collective-permute-done.5.refs_7_ = bf16[8,1152]{1,0:T(8,128)(2,1)S(1)} collective-permute-done((bf16[8,1152]{1,0:T(8,128)(2,1)S(1)}, bf16[8,1152]{1,0:T(8,128)(2,1)S(1)}, u32[]{:S(2)}, u32[]{:S(2)}) %collective-permute-start.5) | collective-permute-done | bytes 18464 | tf_op jit(solution)/shard_map/ppermute | solution.py:417
  52.4 0.0 collective-permute-done.2.refs_4_
  52.4 0.0 collective-permute-done.3.refs_5_
  52.4 0.0 copy-done.8
  52.4 1.6 %shard_map.111 = (bf16[1152,256]{1,0:T(8,128)(2,1)S(1)}, f32[32,1,128]{2,1,0:T(1,128)}) custom-call(f32[1152,256]{1,0:T(8,128)S(1)} %get-tuple-element.43.refs_0_, f32[1152,128]{1,0:T(8,128)S(1)} %get-tuple-element.44.refs_1_, f32[1152,128]{1,0:T(8,128)S(1)} %get-tuple-element.45.refs_2_, f32[1152,128]{1,0:T(8,128)S(1)} %get-tuple-element.46.refs_3_, ...), custom_call_target="tpu_custom_call" | custom-call | bytes 4781056 | tf_op jit(solution)/shard_map/pallas_call | solution.py:50
  54.1 7.3 %all-to-all-start.1 = ((f32[32,1,128]{2,1,0:T(1,128)}), f32[32,1,128]{2,1,0:T(1,128)S(1)}, u32[]{:S(2)}, u32[]{:S(2)}) async-start(f32[32,1,128]{2,1,0:T(1,128)} %get-tuple-element.53), calls=%async_computation.1 | async-start | bytes 32768 | tf_op jit(solution)/shard_map/all_to_all | solution.py:501
  61.4 3.7 %shard_map.112 = bf16[1152,256]{1,0:T(8,128)(2,1)} custom-call(bf16[1152,256]{1,0:T(8,128)(2,1)S(1)} %get-tuple-element.51.refs_0_, bf16[1152,1152]{1,0:T(8,128)(2,1)S(1)} %get-tuple-element.38.refs_1_, f32[32,256]{1,0:T(8,128)} %refs_2_.7, f32[1,256]{1,0:T(1,128)} %copy-done.9, f32[1152,256]{1,0:T(8,128)} %copy-done.3, bf16[2,1152,256]{2,1,0:T(8,128)(2,1)} %refs_5_.3), custom_call_target="tpu_custom_call" | custom-call | flops 1358954496 | bytes 6226944 | tf_op jit(solution)/shard_map/pallas_call | solution.py:50
  65.1 4.8 %all-to-all-done.1.refs_0_ = f32[32,1,128]{2,1,0:T(1,128)S(1)} async-done(((f32[32,1,128]{2,1,0:T(1,128)}), f32[32,1,128]{2,1,0:T(1,128)S(1)}, u32[]{:S(2)}, u32[]{:S(2)}) %all-to-all-start.1) | async-done | bytes 16416 | tf_op jit(solution)/shard_map/all_to_all | solution.py:501
  70.0 23.4 %all_to_all.15.refs_0_ = f32[16,1,128]{2,1,0:T(1,128)S(1)} all-to-all(f32[16,1,128]{2,1,0:T(1,128)S(1)} %shard_map.113), channel_id=1, replica_groups=mesh['geo'=16,'freq'=32] {'geo'}, dimensions={0} | all-to-all | bytes 16384 | tf_op jit(solution)/shard_map/all_to_all | solution.py:513
  93.4 0.5 shard_map.114
  (1 shorter events, 0.0 us)
Async XLA Ops:
  2.1 7.6 %collective-permute-start = (bf16[8,2304]{1,0:T(8,128)(2,1)S(1)}, bf16[8,2304]{1,0:T(8,128)(2,1)S(1)}, u32[]{:S(2)}, u32[]{:S(2)}) collective-permute-start(bf16[8,2304]{1,0:T(8,128)(2,1)S(1)} %get-tuple-element.33), channel_id=1, source_target_pairs={{0,32},{32,64},{64,96},{96,128},{128,160},{160,192},{192,224},{224... | collective-permute-start | bytes 110600 | tf_op jit(solution)/shard_map/ppermute | solution.py:432
  5.6 4.3 %collective-permute-start.1 = (bf16[8,2304]{1,0:T(8,128)(2,1)S(1)}, bf16[8,2304]{1,0:T(8,128)(2,1)S(1)}, u32[]{:S(2)}, u32[]{:S(2)}) collective-permute-start(bf16[8,2304]{1,0:T(8,128)(2,1)S(1)} %get-tuple-element.34), channel_id=1, source_target_pairs={{32,0},{64,32},{96,64},{128,96},{160,128},{192,160},{224,192},{256... | collective-permute-start | bytes 110600 | tf_op jit(solution)/shard_map/ppermute | solution.py:433
  9.9 9.9 %copy-start = (bf16[2,1152,256]{2,1,0:T(8,128)(2,1)S(1)}, bf16[2,1152,256]{2,1,0:T(8,128)(2,1)}, u32[]{:S(2)}) copy-start(bf16[2,1152,256]{2,1,0:T(8,128)(2,1)} %refs_5_.3) | copy-start | bytes 3538948
  11.1 22.3 %all-to-all-start = ((bf16[32,72,128]{2,1,0:T(8,128)(2,1)}), bf16[32,72,128]{2,1,0:T(8,128)(2,1)S(1)}, u32[]{:S(2)}, u32[]{:S(2)}) async-start(bf16[32,72,128]{2,1,0:T(8,128)(2,1)} %shard_map.106), calls=%async_computation | async-start | bytes 1179648 | tf_op jit(solution)/shard_map/all_to_all | solution.py:447
  19.8 1.8 %copy-start.2 = (bf16[1152,1152]{1,0:T(8,128)(2,1)S(1)}, bf16[1152,1152]{1,0:T(8,128)(2,1)}, u32[]{:S(2)}) copy-start(bf16[1152,1152]{1,0:T(8,128)(2,1)} %refs_1_.5) | copy-start | bytes 7962628
  21.6 4.7 %copy-start.1 = (bf16[2,1152,256]{2,1,0:T(8,128)(2,1)S(1)}, bf16[2,1152,256]{2,1,0:T(8,128)(2,1)}, u32[]{:S(2)}) copy-start(bf16[2,1152,256]{2,1,0:T(8,128)(2,1)} %refs_5_.3) | copy-start | bytes 3538948
  24.4 1.1 %copy-start.3 = (f32[1152,256]{1,0:T(8,128)}, f32[1152,256]{1,0:T(8,128)S(1)}, u32[]{:S(2)}) copy-start(f32[1152,256]{1,0:T(8,128)S(1)} %get-tuple-element.52.refs_4_) | copy-start | bytes 3538948
  25.4 0.8 copy-start.7
  26.3 2.1 %copy-start.9 = (f32[1,256]{1,0:T(1,128)}, f32[1,256]{1,0:T(1,128)S(1)}, u32[]{:S(2)}) copy-start(f32[1,256]{1,0:T(1,128)S(1)} %get-tuple-element.37.refs_3_) | copy-start | bytes 3076
  28.4 1.0 %copy-start.4 = (f32[2,1152,128]{2,1,0:T(8,128)}, f32[2,1152,128]{2,1,0:T(8,128)S(1)}, u32[]{:S(2)}) copy-start(f32[2,1152,128]{2,1,0:T(8,128)S(1)} %get-tuple-element.42.refs_2_) | copy-start | bytes 3538948
  29.4 1.0 %copy-start.6 = (f32[1152,256]{1,0:T(8,128)}, f32[1152,256]{1,0:T(8,128)S(1)}, u32[]{:S(2)}) copy-start(f32[1152,256]{1,0:T(8,128)S(1)} %get-tuple-element.39.refs_5_) | copy-start | bytes 3538948
  33.3 17.3 %copy-start.5 = (f32[2,1152,128]{2,1,0:T(8,128)S(1)}, f32[2,1152,128]{2,1,0:T(8,128)}, u32[]{:S(2)}) copy-start(f32[2,1152,128]{2,1,0:T(8,128)} %copy-done.4) | copy-start | bytes 3538948
  37.4 15.0 %copy-start.8 = (bf16[1152,256]{1,0:T(8,128)(2,1)S(1)}, bf16[1152,256]{1,0:T(8,128)(2,1)}, u32[]{:S(2)}) copy-start(bf16[1152,256]{1,0:T(8,128)(2,1)} %copy-done.7) | copy-start | bytes 1769476
  37.4 15.0 %collective-permute-start.2 = (bf16[1152,128]{1,0:T(8,128)(2,1)S(1)}, bf16[1152,128]{1,0:T(8,128)(2,1)S(1)}, u32[]{:S(2)}, u32[]{:S(2)}) collective-permute-start(bf16[1152,128]{1,0:T(8,128)(2,1)S(1)} %get-tuple-element.40.refs_0_), channel_id=1, source_target_pairs={{1,0},{2,1},{3,2},{4,3},{5,4},{6,5},{7,6},{8,7},{9,8},{10,9},{11,1... | collective-permute-start | bytes 884744 | tf_op jit(solution)/shard_map/ppermute | solution.py:414
  38.8 13.6 %collective-permute-start.3 = (bf16[1152,128]{1,0:T(8,128)(2,1)S(1)}, bf16[1152,128]{1,0:T(8,128)(2,1)S(1)}, u32[]{:S(2)}, u32[]{:S(2)}) collective-permute-start(bf16[1152,128]{1,0:T(8,128)(2,1)S(1)} %get-tuple-element.41.refs_1_), channel_id=1, source_target_pairs={{0,1},{1,2},{2,3},{3,4},{4,5},{5,6},{6,7},{7,8},{8,9},{9,10},{10,1... | collective-permute-start | bytes 884744 | tf_op jit(solution)/shard_map/ppermute | solution.py:415
  42.8 8.5 %collective-permute-start.4 = (bf16[8,1152]{1,0:T(8,128)(2,1)S(1)}, bf16[8,1152]{1,0:T(8,128)(2,1)S(1)}, u32[]{:S(2)}, u32[]{:S(2)}) collective-permute-start(bf16[8,1152]{1,0:T(8,128)(2,1)S(1)} %get-tuple-element.47), channel_id=1, source_target_pairs={{0,32},{32,64},{64,96},{96,128},{128,160},{160,192},{192,224},{224... | collective-permute-start | bytes 55304 | tf_op jit(solution)/shard_map/ppermute | solution.py:416
  48.9 3.5 %collective-permute-start.5 = (bf16[8,1152]{1,0:T(8,128)(2,1)S(1)}, bf16[8,1152]{1,0:T(8,128)(2,1)S(1)}, u32[]{:S(2)}, u32[]{:S(2)}) collective-permute-start(bf16[8,1152]{1,0:T(8,128)(2,1)S(1)} %get-tuple-element.48), channel_id=1, source_target_pairs={{32,0},{64,32},{96,64},{128,96},{160,128},{192,160},{224,192},{256... | collective-permute-start | bytes 55304 | tf_op jit(solution)/shard_map/ppermute | solution.py:417
  54.1 15.9 %all-to-all-start.1 = ((f32[32,1,128]{2,1,0:T(1,128)}), f32[32,1,128]{2,1,0:T(1,128)S(1)}, u32[]{:S(2)}, u32[]{:S(2)}) async-start(f32[32,1,128]{2,1,0:T(1,128)} %get-tuple-element.53), calls=%async_computation.1 | async-start | bytes 32768 | tf_op jit(solution)/shard_map/all_to_all | solution.py:501

commit v6 on v5

--- a/solution.py
+++ b/solution.py
@@ -13,11 +13,12 @@
 step_weight = 0.25
 PAD = 40
 MIB = 1 << 20
+PARTS = 4
 WHOLE = pl.BlockSpec(memory_space=pltpu.VMEM)
 OUTSIDE = pl.BlockSpec(memory_space=pl.ANY)
 
 
-def call(kernel, outs, args, scratch=(), flops=0, late=None, outside_outs=(), limit=32):
+def call(kernel, outs, args, scratch=(), flops=0, late=None, parted=(), outside_outs=(), limit=32):
     late = {} if late is None else late
     places = sorted(late)
     size = sum(a.size * a.dtype.itemsize for a in (*args, *outs))
@@ -29,13 +30,25 @@
 
     def body(*refs):
         given, kept, buffers = list(refs[: len(args)]), refs[len(args) : n], refs[n:]
-        copies = {}
-        for k, i in enumerate(places):
+        copies, sources = {}, {}
+        order = sorted(range(len(places)), key=lambda k: math.prod(buffers[k].shape))
+        for k in order:
+            i = places[k]
             source = given[i] if late[i] is None else given[i].at[late[i]]
-            copies[i] = pltpu.make_async_copy(source, buffers[k], buffers[-1].at[k])
-            given[i] = buffers[k]
-        for i in sorted(places, key=lambda i: math.prod(given[i].shape)):
-            copies[i].start()
+            sources[i], given[i] = source, buffers[k]
+            if i not in parted:
+                copies[i] = pltpu.make_async_copy(source, buffers[k], buffers[-1].at[k, 0])
+                copies[i].start()
+        for part in range(PARTS):
+            for k in order:
+                i = places[k]
+                if i in parted:
+                    source = sources[i]
+                    rows = blocks_of(source.shape[0], PARTS)[part]
+                    copies[i, part] = pltpu.make_async_copy(
+                        source.at[rows, :], buffers[k].at[rows, :], buffers[-1].at[k, part]
+                    )
+                    copies[i, part].start()
         if places:
             kernel(*given, *kept, wait=lambda *which: [copies[i].wait() for i in which])
         else:
@@ -46,7 +59,7 @@
         for i in places
     ]
     if places:
-        buffers.append(pltpu.SemaphoreType.DMA((len(places),)))
+        buffers.append(pltpu.SemaphoreType.DMA((len(places), PARTS)))
     return pl.pallas_call(
         body,
         out_shape=outs,
@@ -238,7 +251,7 @@
 def two_substeps(carried, turned_ref, kappa_ref, prepare, ready, write, weigh):
     m_scr, r_scr, factor_scr, product_scr = carried
     components, points = m_scr.shape
-    blocks = blocks_of(components, 4)
+    blocks = blocks_of(components, PARTS)
     weights = jnp.zeros((8, points), F32)
     moved = r_scr[...]
     for rows in blocks:
@@ -265,7 +278,7 @@
 
 def first_kernel(
     moved_ref, turned_ref, kappa_ref, coeff_ref, mask_ref, next_ref, traj_ref,
-    low_ref, high_ref, west_ref, east_ref, weights_ref, *carried, wait,
+    low_ref, high_ref, edge_ref, weights_ref, *carried, wait,
 ):
     freqs, height, lon = moved_ref.shape
     points = 2 * lon
@@ -279,13 +292,18 @@
     r_scr[...] = m_scr[...].astype(BF16)
 
     def prepare():
-        wait(2, 3, 5, 6)
+        wait(2, 3)
         return coeff_ref[...]
 
     def masks():
         return mask_ref[pl.ds(2 * lax.axis_index("freq"), 2), :].astype(F32)
 
+    unread = list(range(PARTS))
+
     def ready(rows):
+        if unread:
+            part = unread.pop(0)
+            wait((5, part), (6, part))
         return next_ref[rows, :], traj_ref[rows, :].astype(F32)
 
     def write(rows, values):
@@ -302,8 +320,7 @@
     )
     picks = edge_picks(points, lon)
     edges = take_edges(low_ref[...], picks[:, 0:lon]) + take_edges(high_ref[...], picks[:, lon:points])
-    west_ref[...] = edges[0:8].astype(BF16)
-    east_ref[...] = edges[8:16].astype(BF16)
+    edge_ref[...] = edges.astype(BF16)
 
 
 def inner_kernel(
@@ -336,7 +353,7 @@
     pull_ref, own_ref, sed_ref, moved_ref, sums_ref, wait,
 ):
     components, lon = north_ref.shape
-    cols = put_edges(west_ref[...], east_ref[...], 2 * lon, lon)
+    cols = put_edges(west_ref[...].astype(F32)[8:16], east_ref[...].astype(F32)[0:8], 2 * lon, lon)
     weights = [own_ref[:, 0:lon], own_ref[:, lon : 2 * lon]]
     for rows in blocks_of(components, components // 144):
         edge_rate = edge_rate_ref[rows, :]
@@ -409,14 +426,6 @@
     northward = [(i, i + 1) for i in range(peers - 1)]
     southward = [(j, i) for i, j in northward]
 
-    def swap(low, high, west, east):
-        return (
-            lax.ppermute(low, "freq", southward),
-            lax.ppermute(high, "freq", northward),
-            lax.ppermute(east, "geo", eastward),
-            lax.ppermute(west, "geo", westward),
-        )
-
     field = adjoint_final.reshape(directions, lat, lon)
     grouped, west, east, own_rates = call(
         regroup_kernel,
@@ -472,21 +481,24 @@
         late={2: None, 4: None, 5: None},
     )
     carried = [pltpu.VMEM(full, kind) for kind in (F32, BF16, F32, F32)]
-    low, high, west, east, weights = call(
+    low, high, edges, weights = call(
         first_kernel,
         [
             shape(half_full, BF16),
             shape(half_full, BF16),
-            shape((8, components), BF16),
-            shape((8, components), BF16),
+            shape((16, components), BF16),
             shape((8, points), F32),
         ],
         [moved, turned, friction_factor, coeff, sea_mask, next1, trajectory],
         carried,
         flops=2 * product,
         late={2: None, 3: None, 4: None, 5: None, 6: 1},
-    )
-    swapped = swap(low, high, west, east)
+        parted=(5, 6),
+    )
+    above = lax.ppermute(low, "freq", southward)
+    below = lax.ppermute(high, "freq", northward)
+    from_west = lax.ppermute(edges, "geo", eastward)
+    from_east = lax.ppermute(edges, "geo", westward)
     inner = call(
         inner_kernel,
         [shape(full, F32), shape(half_full, F32), shape(half_full, F32), shape(half_full, F32)],
@@ -495,10 +507,11 @@
     moved, sums = call(
         halo_kernel,
         [shape(full, BF16), shape((peers, 1, 128), F32)],
-        [*inner, *swapped, pull, weights, sediment.reshape(1, points)],
+        [*inner, above, below, from_west, from_east, pull, weights, sediment.reshape(1, points)],
         late={10: None},
     )
     sums = lax.all_to_all(sums, "freq", split_axis=0, concat_axis=0, tiled=True)
+    sums, moved = lax.optimization_barrier((sums, moved))
     (result,) = call(
         last_kernel,
         [shape(full, BF16)],
@@ -508,7 +521,6 @@
         late={2: None, 3: None, 4: None, 5: 0},
         outside_outs=(0,),
     )
-    result, sums = lax.optimization_barrier((result, sums))
     (sums,) = call(add_kernel, [shape((regions, 1, 128), F32)], [sums])
     sums = lax.all_to_all(sums, "geo", split_axis=0, concat_axis=0, tiled=True)
     point_total = points * peers * regions

time: 94.4 us -> 94.4 us (level)
  starting transfers between devices: 36.2 us -> 45.4 us
  blocking collectives: 23.4 us -> 15.6 us
  waiting for transfers between devices: 9.01 us -> 7.39 us
    all_to_all x1, starting transfers between devices: 7.29 us -> 16.5 us  [shards(): sums = lax.all_to_all(sums, 'geo', split_axis=0, concat_axis=0, tiled=True)]
    all_to_all x1, blocking collectives: 23.4 us -> 15.6 us  [shards(): sums = lax.all_to_all(sums, 'freq', split_axis=0, concat_axis=0, tiled=True)]
    all_to_all x1, waiting for transfers between devices: 4.84 us -> 3.18 us  [shards(): sums = lax.all_to_all(sums, 'geo', split_axis=0, concat_axis=0, tiled=True)]
where the time goes in v6:
time: 94.4 us; the launch traced here: 93.8 us
  starting transfers between devices  45.4 us (48%)
  Pallas kernels  18.9 us (20%)
  blocking collectives  15.6 us (17%)
  waiting for transfers between devices  7.39 us (8%)
  local copies, waits for them, and re-layouts  5.66 us (6%)
    pallas_call x11, Pallas kernels, call(): pl.pallas_call(body, out_shape=outs, in_specs=[OUTSIDE if i in late else...  18.9 us
    all_to_all x1, starting transfers between devices, shards(): sums = lax.all_to_all(sums, 'geo', split_axis=0, concat_axis=0, tiled=True)  16.5 us
    all_to_all x1, blocking collectives, shards(): sums = lax.all_to_all(sums, 'freq', split_axis=0, concat_axis=0, tiled=True)  15.6 us
    all_to_all x1, starting transfers between devices, shards(): lax.all_to_all(sent, 'freq', split_axis=0, concat_axis=0, tiled=True)  8.78 us
    ppermute x1, starting transfers between devices, shards(): from_west = lax.ppermute(edges, 'geo', eastward)  6.11 us
    unnamed x20, local copies, waits for them, and re-layouts  5.66 us
    ppermute x1, starting transfers between devices, shards(): below = lax.ppermute(high, 'freq', northward)  4 us
    ppermute x1, starting transfers between devices, shards(): from_west = lax.ppermute(east, 'geo', eastward)  3.49 us
  transfers between devices with their start and end apart: 8, of which 4 were waited for; matrix products, arithmetic and copies ran while one was open for 0% of the time, Pallas kernels for 11%

profile of v6, /device:TPU:1, one launch (start us, length us, event | category | flops | bytes accessed | tf_op | source)
XLA Modules:
  0.0 93.8 jit_solution(7366105706778188645)
XLA Ops:
  0.6 1.6 %shard_map.104 = (f32[2384,128]{1,0:T(8,128)S(1)}, bf16[8,2304]{1,0:T(8,128)(2,1)S(1)}, bf16[8,2304]{1,0:T(8,128)(2,1)S(1)}, f32[2,72,128]{2,1,0:T(8,128)S(1)}) custom-call(bf16[36,64,128]{2,1,0:T(8,128)(2,1)} %bitcast.4, s32[64,128]{1,0:T(8,128)} %refs_4_.3, f32[32,36]{1,0:T(8,128)} %refs_4_.2, f32[32,36]{1,0:T(8,128)} %refs_5_.2), custom_call_target="tpu_custom_call" | custom-call | bytes 1999872 | tf_op jit(solution)/shard_map/pallas_call | solution.py:63
  2.2 3.5 %collective-permute-start = (bf16[8,2304]{1,0:T(8,128)(2,1)S(1)}, bf16[8,2304]{1,0:T(8,128)(2,1)S(1)}, u32[]{:S(2)}, u32[]{:S(2)}) collective-permute-start(bf16[8,2304]{1,0:T(8,128)(2,1)S(1)} %get-tuple-element.32), channel_id=1, source_target_pairs={{0,32},{32,64},{64,96},{96,128},{128,160},{160,192},{192,224},{224... | collective-permute-start | bytes 110600 | tf_op jit(solution)/shard_map/ppermute | solution.py:441
  5.7 3.4 %collective-permute-start.1 = (bf16[8,2304]{1,0:T(8,128)(2,1)S(1)}, bf16[8,2304]{1,0:T(8,128)(2,1)S(1)}, u32[]{:S(2)}, u32[]{:S(2)}) collective-permute-start(bf16[8,2304]{1,0:T(8,128)(2,1)S(1)} %get-tuple-element.33), channel_id=1, source_target_pairs={{32,0},{64,32},{96,64},{128,96},{160,128},{192,160},{224,192},{256... | collective-permute-start | bytes 110600 | tf_op jit(solution)/shard_map/ppermute | solution.py:442
  9.2 0.7 shard_map.105
  9.8 0.0 collective-permute-done.refs_2_
  9.8 0.2 collective-permute-done.1.refs_3_
  10.0 0.0 copy-start
  10.0 1.1 %shard_map.106 = bf16[32,72,128]{2,1,0:T(8,128)(2,1)} custom-call(f32[32,72,128]{2,1,0:T(8,128)S(1)} %get-tuple-element.30.refs_0_, f32[72,128]{1,0:T(8,128)S(1)} %get-tuple-element.31.refs_1_, bf16[8,2304]{1,0:T(8,128)(2,1)S(1)} %collective-permute-done.refs_2_, bf16[8,2304]{1,0:T(8,128)(2,1)S(1)} %collective-permute-done.1.refs_3_), custom_call_target="tpu_custom_call" | custom-call | bytes 1880064 | tf_op jit(solution)/shard_map/pallas_call | solution.py:63
  11.2 8.8 %all-to-all-start = ((bf16[32,72,128]{2,1,0:T(8,128)(2,1)}), bf16[32,72,128]{2,1,0:T(8,128)(2,1)S(1)}, u32[]{:S(2)}, u32[]{:S(2)}) async-start(bf16[32,72,128]{2,1,0:T(8,128)(2,1)} %shard_map.106), calls=%async_computation | async-start | bytes 1179648 | tf_op jit(solution)/shard_map/all_to_all | solution.py:456
  19.9 0.0 copy-done
  20.0 0.0 copy-start.2
  20.0 1.7 %copy-done.2 = bf16[1152,1152]{1,0:T(8,128)(2,1)S(1)} copy-done((bf16[1152,1152]{1,0:T(8,128)(2,1)S(1)}, bf16[1152,1152]{1,0:T(8,128)(2,1)}, u32[]{:S(2)}) %copy-start.2) | copy-done | bytes 2654232
  21.7 0.0 copy-start.1
  21.7 2.8 %shard_map.107 = (f32[1,256]{1,0:T(1,128)S(1)}, f32[1152,256]{1,0:T(8,128)S(1)}, bf16[1152,256]{1,0:T(8,128)(2,1)S(1)}) custom-call(bf16[2,1152,256]{2,1,0:T(8,128)(2,1)S(1)} %copy-done, bf16[1152,1152]{1,0:T(8,128)(2,1)S(1)} %copy-done.2, f32[32,256]{1,0:T(8,128)} %refs_2_.7, f32[1,64]{1,0:T(1,128)} %bitcast.8, s32[1,256]{1,0:T(1,128)} %bitcast.5), custom_call_target="tpu_custom_call" | custom-call | flops 1358954496 | bytes 5638400 | tf_op jit(solution)/shard_map/pallas_call | solution.py:63
  24.6 0.0 copy-start.3
  24.6 1.0 %copy-done.3 = f32[1152,256]{1,0:T(8,128)} copy-done((f32[1152,256]{1,0:T(8,128)}, f32[1152,256]{1,0:T(8,128)S(1)}, u32[]{:S(2)}) %copy-start.3) | copy-done | bytes 1179672
  25.6 0.0 copy-start.7
  25.6 0.8 copy-done.7
  26.4 0.0 copy-start.9
  26.4 0.0 copy-done.1
  26.4 2.2 %shard_map.108 = (bf16[1152,1152]{1,0:T(8,128)(2,1)S(1)}, f32[1152,256]{1,0:T(8,128)S(1)}, f32[2,1152,128]{2,1,0:T(8,128)S(1)}) custom-call(bf16[2,1152,256]{2,1,0:T(8,128)(2,1)S(1)} %copy-done.1, bf16[1152,1152]{1,0:T(8,128)(2,1)S(1)} %copy-done.2, f32[32,256]{1,0:T(8,128)} %refs_2_.7, f32[1,256]{1,0:T(1,128)S(1)} %get-tuple-element.36.refs_3_, ...), custom_call_target="tpu_custom_call" | custom-call | flops 679477248 | bytes 8890368 | tf_op jit(solution)/shard_map/pallas_call | solution.py:63
  28.7 0.0 copy-done.9
  28.7 0.0 copy-start.4
  28.7 1.0 %copy-done.4 = f32[2,1152,128]{2,1,0:T(8,128)} copy-done((f32[2,1152,128]{2,1,0:T(8,128)}, f32[2,1152,128]{2,1,0:T(8,128)S(1)}, u32[]{:S(2)}) %copy-start.4) | copy-done | bytes 1179672
  29.7 0.0 copy-start.6
  29.7 1.0 %copy-done.6 = f32[1152,256]{1,0:T(8,128)} copy-done((f32[1152,256]{1,0:T(8,128)}, f32[1152,256]{1,0:T(8,128)S(1)}, u32[]{:S(2)}) %copy-start.6) | copy-done | bytes 1179672
  30.7 2.7 %all-to-all-done.refs_0_ = bf16[32,72,128]{2,1,0:T(8,128)(2,1)S(1)} async-done(((bf16[32,72,128]{2,1,0:T(8,128)(2,1)}), bf16[32,72,128]{2,1,0:T(8,128)(2,1)S(1)}, u32[]{:S(2)}, u32[]{:S(2)}) %all-to-all-start) | async-done | bytes 589856 | tf_op jit(solution)/shard_map/all_to_all | solution.py:456
  33.4 0.0 copy-start.5
  33.4 3.7 %shard_map.109 = (bf16[1152,128]{1,0:T(8,128)(2,1)S(1)}, bf16[1152,128]{1,0:T(8,128)(2,1)S(1)}, bf16[16,1152]{1,0:T(8,128)(2,1)S(1)}, f32[8,256]{1,0:T(8,128)S(1)}) custom-call(bf16[32,72,128]{2,1,0:T(8,128)(2,1)S(1)} %all-to-all-done.refs_0_, bf16[1152,1152]{1,0:T(8,128)(2,1)S(1)} %get-tuple-element.37.refs_1_, f32[32,256]{1,0:T(8,128)} %refs_2_.7, ...), custom_call_target="tpu_custom_call" | custom-call | flops 1358954496 | bytes 6304768 | tf_op jit(solution)/shard_map/pallas_call | solution.py:63
  37.1 0.0 copy-start.8
  37.2 1.4 %collective-permute-start.2 = (bf16[1152,128]{1,0:T(8,128)(2,1)S(1)}, bf16[1152,128]{1,0:T(8,128)(2,1)S(1)}, u32[]{:S(2)}, u32[]{:S(2)}) collective-permute-start(bf16[1152,128]{1,0:T(8,128)(2,1)S(1)} %get-tuple-element.39.refs_0_), channel_id=1, source_target_pairs={{1,0},{2,1},{3,2},{4,3},{5,4},{6,5},{7,6},{8,7},{9,8},{10,9},{11,1... | collective-permute-start | bytes 884744 | tf_op jit(solution)/shard_map/ppermute | solution.py:498
  38.6 4.0 %collective-permute-start.3 = (bf16[1152,128]{1,0:T(8,128)(2,1)S(1)}, bf16[1152,128]{1,0:T(8,128)(2,1)S(1)}, u32[]{:S(2)}, u32[]{:S(2)}) collective-permute-start(bf16[1152,128]{1,0:T(8,128)(2,1)S(1)} %get-tuple-element.40.refs_1_), channel_id=1, source_target_pairs={{0,1},{1,2},{2,3},{3,4},{4,5},{5,6},{6,7},{7,8},{8,9},{9,10},{10,1... | collective-permute-start | bytes 884744 | tf_op jit(solution)/shard_map/ppermute | solution.py:499
  42.6 6.1 %collective-permute-start.4 = (bf16[16,1152]{1,0:T(8,128)(2,1)S(1)}, bf16[16,1152]{1,0:T(8,128)(2,1)S(1)}, u32[]{:S(2)}, u32[]{:S(2)}) collective-permute-start(bf16[16,1152]{1,0:T(8,128)(2,1)S(1)} %get-tuple-element.46), channel_id=1, source_target_pairs={{0,32},{32,64},{64,96},{96,128},{128,160},{160,192},{192,224},{224... | collective-permute-start | bytes 110600 | tf_op jit(solution)/shard_map/ppermute | solution.py:500
  48.7 1.6 %collective-permute-start.5 = (bf16[16,1152]{1,0:T(8,128)(2,1)S(1)}, bf16[16,1152]{1,0:T(8,128)(2,1)S(1)}, u32[]{:S(2)}, u32[]{:S(2)}) collective-permute-start(bf16[16,1152]{1,0:T(8,128)(2,1)S(1)} %get-tuple-element.46), channel_id=1, source_target_pairs={{32,0},{64,32},{96,64},{128,96},{160,128},{192,160},{224,192},{256... | collective-permute-start | bytes 110600 | tf_op jit(solution)/shard_map/ppermute | solution.py:501
  50.4 0.0 copy-done.5
  50.4 0.7 shard_map.110
  51.1 0.0 collective-permute-done.4.refs_6_
  51.1 1.3 %collective-permute-done.5.refs_7_ = bf16[16,1152]{1,0:T(8,128)(2,1)S(1)} collective-permute-done((bf16[16,1152]{1,0:T(8,128)(2,1)S(1)}, bf16[16,1152]{1,0:T(8,128)(2,1)S(1)}, u32[]{:S(2)}, u32[]{:S(2)}) %collective-permute-start.5) | collective-permute-done | bytes 36896 | tf_op jit(solution)/shard_map/ppermute | solution.py:501
  52.4 0.0 collective-permute-done.2.refs_4_
  52.4 0.0 collective-permute-done.3.refs_5_
  52.4 0.0 copy-done.8
  52.4 1.1 %shard_map.111 = (bf16[1152,256]{1,0:T(8,128)(2,1)S(1)}, f32[32,1,128]{2,1,0:T(1,128)S(1)}) custom-call(f32[1152,256]{1,0:T(8,128)S(1)} %get-tuple-element.42.refs_0_, f32[1152,128]{1,0:T(8,128)S(1)} %get-tuple-element.43.refs_1_, f32[1152,128]{1,0:T(8,128)S(1)} %get-tuple-element.44.refs_2_, f32[1152,128]{1,0:T(8,128)S(1)} %get-tuple-element.45.refs_3_, ...), custom_call_target="tpu_custom_call" | custom-call | bytes 4817920 | tf_op jit(solution)/shard_map/pallas_call | solution.py:63
  53.5 15.6 %all_to_all.15.refs_0_ = f32[32,1,128]{2,1,0:T(1,128)S(1)} all-to-all(f32[32,1,128]{2,1,0:T(1,128)S(1)} %get-tuple-element.49), channel_id=1, replica_groups=mesh['geo'=16,'freq'=32] {'freq'}, dimensions={0} | all-to-all | bytes 32768 | tf_op jit(solution)/shard_map/all_to_all | solution.py:513
  69.1 0.6 shard_map.113
  69.7 16.5 %all-to-all-start.2 = ((f32[16,1,128]{2,1,0:T(1,128)}), f32[16,1,128]{2,1,0:T(1,128)S(1)}, u32[]{:S(2)}, u32[]{:S(2)}) async-start(f32[16,1,128]{2,1,0:T(1,128)} %shard_map.113), calls=%async_computation.2 | async-start | bytes 16384 | tf_op jit(solution)/shard_map/all_to_all | solution.py:525
  86.3 3.8 %shard_map.112 = bf16[1152,256]{1,0:T(8,128)(2,1)} custom-call(bf16[1152,256]{1,0:T(8,128)(2,1)S(1)} %get-tuple-element.51.refs_0_, bf16[1152,1152]{1,0:T(8,128)(2,1)S(1)} %get-tuple-element.37.refs_1_, f32[32,256]{1,0:T(8,128)} %refs_2_.7, f32[1,256]{1,0:T(1,128)} %copy-done.9, f32[1152,256]{1,0:T(8,128)} %copy-done.3, bf16[2,1152,256]{2,1,0:T(8,128)(2,1)} %refs_5_.3), custom_call_target="tpu_custom_call" | custom-call | flops 1358954496 | bytes 6226944 | tf_op jit(solution)/shard_map/pallas_call | solution.py:63
  90.1 3.2 %all-to-all-done.2.refs_0_ = f32[16,1,128]{2,1,0:T(1,128)S(1)} async-done(((f32[16,1,128]{2,1,0:T(1,128)}), f32[16,1,128]{2,1,0:T(1,128)S(1)}, u32[]{:S(2)}, u32[]{:S(2)}) %all-to-all-start.2) | async-done | bytes 8224 | tf_op jit(solution)/shard_map/all_to_all | solution.py:525
  93.3 0.5 shard_map.114
Async XLA Ops:
  2.2 7.6 %collective-permute-start = (bf16[8,2304]{1,0:T(8,128)(2,1)S(1)}, bf16[8,2304]{1,0:T(8,128)(2,1)S(1)}, u32[]{:S(2)}, u32[]{:S(2)}) collective-permute-start(bf16[8,2304]{1,0:T(8,128)(2,1)S(1)} %get-tuple-element.32), channel_id=1, source_target_pairs={{0,32},{32,64},{64,96},{96,128},{128,160},{160,192},{192,224},{224... | collective-permute-start | bytes 110600 | tf_op jit(solution)/shard_map/ppermute | solution.py:441
  5.7 4.3 %collective-permute-start.1 = (bf16[8,2304]{1,0:T(8,128)(2,1)S(1)}, bf16[8,2304]{1,0:T(8,128)(2,1)S(1)}, u32[]{:S(2)}, u32[]{:S(2)}) collective-permute-start(bf16[8,2304]{1,0:T(8,128)(2,1)S(1)} %get-tuple-element.33), channel_id=1, source_target_pairs={{32,0},{64,32},{96,64},{128,96},{160,128},{192,160},{224,192},{256... | collective-permute-start | bytes 110600 | tf_op jit(solution)/shard_map/ppermute | solution.py:442
  10.0 9.9 %copy-start = (bf16[2,1152,256]{2,1,0:T(8,128)(2,1)S(1)}, bf16[2,1152,256]{2,1,0:T(8,128)(2,1)}, u32[]{:S(2)}) copy-start(bf16[2,1152,256]{2,1,0:T(8,128)(2,1)} %refs_5_.3) | copy-start | bytes 3538948
  11.2 22.3 %all-to-all-start = ((bf16[32,72,128]{2,1,0:T(8,128)(2,1)}), bf16[32,72,128]{2,1,0:T(8,128)(2,1)S(1)}, u32[]{:S(2)}, u32[]{:S(2)}) async-start(bf16[32,72,128]{2,1,0:T(8,128)(2,1)} %shard_map.106), calls=%async_computation | async-start | bytes 1179648 | tf_op jit(solution)/shard_map/all_to_all | solution.py:456
  20.0 1.8 %copy-start.2 = (bf16[1152,1152]{1,0:T(8,128)(2,1)S(1)}, bf16[1152,1152]{1,0:T(8,128)(2,1)}, u32[]{:S(2)}) copy-start(bf16[1152,1152]{1,0:T(8,128)(2,1)} %refs_1_.5) | copy-start | bytes 7962628
  21.7 4.7 %copy-start.1 = (bf16[2,1152,256]{2,1,0:T(8,128)(2,1)S(1)}, bf16[2,1152,256]{2,1,0:T(8,128)(2,1)}, u32[]{:S(2)}) copy-start(bf16[2,1152,256]{2,1,0:T(8,128)(2,1)} %refs_5_.3) | copy-start | bytes 3538948
  24.6 1.1 %copy-start.3 = (f32[1152,256]{1,0:T(8,128)}, f32[1152,256]{1,0:T(8,128)S(1)}, u32[]{:S(2)}) copy-start(f32[1152,256]{1,0:T(8,128)S(1)} %get-tuple-element.52.refs_4_) | copy-start | bytes 3538948
  25.6 0.8 copy-start.7
  26.4 2.2 %copy-start.9 = (f32[1,256]{1,0:T(1,128)}, f32[1,256]{1,0:T(1,128)S(1)}, u32[]{:S(2)}) copy-start(f32[1,256]{1,0:T(1,128)S(1)} %get-tuple-element.36.refs_3_) | copy-start | bytes 3076
  28.7 1.0 %copy-start.4 = (f32[2,1152,128]{2,1,0:T(8,128)}, f32[2,1152,128]{2,1,0:T(8,128)S(1)}, u32[]{:S(2)}) copy-start(f32[2,1152,128]{2,1,0:T(8,128)S(1)} %get-tuple-element.41.refs_2_) | copy-start | bytes 3538948
  29.7 1.0 %copy-start.6 = (f32[1152,256]{1,0:T(8,128)}, f32[1152,256]{1,0:T(8,128)S(1)}, u32[]{:S(2)}) copy-start(f32[1152,256]{1,0:T(8,128)S(1)} %get-tuple-element.38.refs_5_) | copy-start | bytes 3538948
  33.4 16.9 %copy-start.5 = (f32[2,1152,128]{2,1,0:T(8,128)S(1)}, f32[2,1152,128]{2,1,0:T(8,128)}, u32[]{:S(2)}) copy-start(f32[2,1152,128]{2,1,0:T(8,128)} %copy-done.4) | copy-start | bytes 3538948
  37.1 15.3 %copy-start.8 = (bf16[1152,256]{1,0:T(8,128)(2,1)S(1)}, bf16[1152,256]{1,0:T(8,128)(2,1)}, u32[]{:S(2)}) copy-start(bf16[1152,256]{1,0:T(8,128)(2,1)} %copy-done.7) | copy-start | bytes 1769476
  37.2 15.2 %collective-permute-start.2 = (bf16[1152,128]{1,0:T(8,128)(2,1)S(1)}, bf16[1152,128]{1,0:T(8,128)(2,1)S(1)}, u32[]{:S(2)}, u32[]{:S(2)}) collective-permute-start(bf16[1152,128]{1,0:T(8,128)(2,1)S(1)} %get-tuple-element.39.refs_0_), channel_id=1, source_target_pairs={{1,0},{2,1},{3,2},{4,3},{5,4},{6,5},{7,6},{8,7},{9,8},{10,9},{11,1... | collective-permute-start | bytes 884744 | tf_op jit(solution)/shard_map/ppermute | solution.py:498
  38.6 13.8 %collective-permute-start.3 = (bf16[1152,128]{1,0:T(8,128)(2,1)S(1)}, bf16[1152,128]{1,0:T(8,128)(2,1)S(1)}, u32[]{:S(2)}, u32[]{:S(2)}) collective-permute-start(bf16[1152,128]{1,0:T(8,128)(2,1)S(1)} %get-tuple-element.40.refs_1_), channel_id=1, source_target_pairs={{0,1},{1,2},{2,3},{3,4},{4,5},{5,6},{6,7},{7,8},{8,9},{9,10},{10,1... | collective-permute-start | bytes 884744 | tf_op jit(solution)/shard_map/ppermute | solution.py:499
  42.6 8.5 %collective-permute-start.4 = (bf16[16,1152]{1,0:T(8,128)(2,1)S(1)}, bf16[16,1152]{1,0:T(8,128)(2,1)S(1)}, u32[]{:S(2)}, u32[]{:S(2)}) collective-permute-start(bf16[16,1152]{1,0:T(8,128)(2,1)S(1)} %get-tuple-element.46), channel_id=1, source_target_pairs={{0,32},{32,64},{64,96},{96,128},{128,160},{160,192},{192,224},{224... | collective-permute-start | bytes 110600 | tf_op jit(solution)/shard_map/ppermute | solution.py:500
  48.7 3.7 %collective-permute-start.5 = (bf16[16,1152]{1,0:T(8,128)(2,1)S(1)}, bf16[16,1152]{1,0:T(8,128)(2,1)S(1)}, u32[]{:S(2)}, u32[]{:S(2)}) collective-permute-start(bf16[16,1152]{1,0:T(8,128)(2,1)S(1)} %get-tuple-element.46), channel_id=1, source_target_pairs={{32,0},{64,32},{96,64},{128,96},{160,128},{192,160},{224,192},{256... | collective-permute-start | bytes 110600 | tf_op jit(solution)/shard_map/ppermute | solution.py:501
  69.7 23.6 %all-to-all-start.2 = ((f32[16,1,128]{2,1,0:T(1,128)}), f32[16,1,128]{2,1,0:T(1,128)S(1)}, u32[]{:S(2)}, u32[]{:S(2)}) async-start(f32[16,1,128]{2,1,0:T(1,128)} %shard_map.113), calls=%async_computation.2 | async-start | bytes 16384 | tf_op jit(solution)/shard_map/all_to_all | solution.py:525

commit v7 on v6

--- a/solution.py
+++ b/solution.py
@@ -385,10 +385,15 @@
     m_scr[...] = moved_ref[...].astype(F32)
 
     def prepare():
-        wait(2, 3, 4, 5)
+        wait(2, 3)
         return coeff_ref[...]
 
+    unread = list(range(PARTS))
+
     def ready(rows):
+        if unread:
+            part = unread.pop(0)
+            wait((4, part), (5, part))
         return next_ref[rows, :], traj_ref[rows, :].astype(F32)
 
     def write(rows, values):
@@ -519,6 +524,7 @@
         [*carried, pltpu.VMEM(full, BF16), pltpu.SemaphoreType.DMA((4,))],
         flops=2 * product,
         late={2: None, 3: None, 4: None, 5: 0},
+        parted=(4, 5),
         outside_outs=(0,),
     )
     (sums,) = call(add_kernel, [shape((regions, 1, 128), F32)], [sums])

time: 94.4 us -> 94.4 us (level)
  no operation moved by 1% of the time
where the time goes in v7:
time: 94.4 us; the launch traced here: 93.8 us
  starting transfers between devices  45.4 us (48%)
  Pallas kernels  19 us (20%)
  blocking collectives  15.6 us (17%)
  waiting for transfers between devices  7.27 us (8%)
  local copies, waits for them, and re-layouts  5.66 us (6%)
    pallas_call x11, Pallas kernels, call(): pl.pallas_call(body, out_shape=outs, in_specs=[OUTSIDE if i in late else...  19 us
    all_to_all x1, starting transfers between devices, shards(): sums = lax.all_to_all(sums, 'geo', split_axis=0, concat_axis=0, tiled=True)  16.5 us
    all_to_all x1, blocking collectives, shards(): sums = lax.all_to_all(sums, 'freq', split_axis=0, concat_axis=0, tiled=True)  15.6 us
    all_to_all x1, starting transfers between devices, shards(): lax.all_to_all(sent, 'freq', split_axis=0, concat_axis=0, tiled=True)  8.78 us
    ppermute x1, starting transfers between devices, shards(): from_west = lax.ppermute(edges, 'geo', eastward)  6.11 us
    unnamed x20, local copies, waits for them, and re-layouts  5.66 us
    ppermute x1, starting transfers between devices, shards(): below = lax.ppermute(high, 'freq', northward)  4 us
    ppermute x1, starting transfers between devices, shards(): from_west = lax.ppermute(east, 'geo', eastward)  3.49 us
  transfers between devices with their start and end apart: 8, of which 4 were waited for; matrix products, arithmetic and copies ran while one was open for 0% of the time, Pallas kernels for 11%

profile of v7, /device:TPU:1, one launch (start us, length us, event | category | flops | bytes accessed | tf_op | source)
XLA Modules:
  0.0 93.8 jit_solution(11781165953791782147)
XLA Ops:
  0.6 1.6 %shard_map.104 = (f32[2384,128]{1,0:T(8,128)S(1)}, bf16[8,2304]{1,0:T(8,128)(2,1)S(1)}, bf16[8,2304]{1,0:T(8,128)(2,1)S(1)}, f32[2,72,128]{2,1,0:T(8,128)S(1)}) custom-call(bf16[36,64,128]{2,1,0:T(8,128)(2,1)} %bitcast.4, s32[64,128]{1,0:T(8,128)} %refs_4_.3, f32[32,36]{1,0:T(8,128)} %refs_4_.2, f32[32,36]{1,0:T(8,128)} %refs_5_.2), custom_call_target="tpu_custom_call" | custom-call | bytes 1999872 | tf_op jit(solution)/shard_map/pallas_call | solution.py:63
  2.2 3.5 %collective-permute-start = (bf16[8,2304]{1,0:T(8,128)(2,1)S(1)}, bf16[8,2304]{1,0:T(8,128)(2,1)S(1)}, u32[]{:S(2)}, u32[]{:S(2)}) collective-permute-start(bf16[8,2304]{1,0:T(8,128)(2,1)S(1)} %get-tuple-element.32), channel_id=1, source_target_pairs={{0,32},{32,64},{64,96},{96,128},{128,160},{160,192},{192,224},{224... | collective-permute-start | bytes 110600 | tf_op jit(solution)/shard_map/ppermute | solution.py:446
  5.7 3.4 %collective-permute-start.1 = (bf16[8,2304]{1,0:T(8,128)(2,1)S(1)}, bf16[8,2304]{1,0:T(8,128)(2,1)S(1)}, u32[]{:S(2)}, u32[]{:S(2)}) collective-permute-start(bf16[8,2304]{1,0:T(8,128)(2,1)S(1)} %get-tuple-element.33), channel_id=1, source_target_pairs={{32,0},{64,32},{96,64},{128,96},{160,128},{192,160},{224,192},{256... | collective-permute-start | bytes 110600 | tf_op jit(solution)/shard_map/ppermute | solution.py:447
  9.2 0.7 shard_map.105
  9.8 0.0 collective-permute-done.refs_2_
  9.8 0.2 collective-permute-done.1.refs_3_
  10.0 0.0 copy-start
  10.0 1.1 %shard_map.106 = bf16[32,72,128]{2,1,0:T(8,128)(2,1)} custom-call(f32[32,72,128]{2,1,0:T(8,128)S(1)} %get-tuple-element.30.refs_0_, f32[72,128]{1,0:T(8,128)S(1)} %get-tuple-element.31.refs_1_, bf16[8,2304]{1,0:T(8,128)(2,1)S(1)} %collective-permute-done.refs_2_, bf16[8,2304]{1,0:T(8,128)(2,1)S(1)} %collective-permute-done.1.refs_3_), custom_call_target="tpu_custom_call" | custom-call | bytes 1880064 | tf_op jit(solution)/shard_map/pallas_call | solution.py:63
  11.2 8.8 %all-to-all-start = ((bf16[32,72,128]{2,1,0:T(8,128)(2,1)}), bf16[32,72,128]{2,1,0:T(8,128)(2,1)S(1)}, u32[]{:S(2)}, u32[]{:S(2)}) async-start(bf16[32,72,128]{2,1,0:T(8,128)(2,1)} %shard_map.106), calls=%async_computation | async-start | bytes 1179648 | tf_op jit(solution)/shard_map/all_to_all | solution.py:461
  19.9 0.0 copy-done
  20.0 0.0 copy-start.2
  20.0 1.7 %copy-done.2 = bf16[1152,1152]{1,0:T(8,128)(2,1)S(1)} copy-done((bf16[1152,1152]{1,0:T(8,128)(2,1)S(1)}, bf16[1152,1152]{1,0:T(8,128)(2,1)}, u32[]{:S(2)}) %copy-start.2) | copy-done | bytes 2654232
  21.7 0.0 copy-start.1
  21.7 2.8 %shard_map.107 = (f32[1,256]{1,0:T(1,128)S(1)}, f32[1152,256]{1,0:T(8,128)S(1)}, bf16[1152,256]{1,0:T(8,128)(2,1)S(1)}) custom-call(bf16[2,1152,256]{2,1,0:T(8,128)(2,1)S(1)} %copy-done, bf16[1152,1152]{1,0:T(8,128)(2,1)S(1)} %copy-done.2, f32[32,256]{1,0:T(8,128)} %refs_2_.7, f32[1,64]{1,0:T(1,128)} %bitcast.8, s32[1,256]{1,0:T(1,128)} %bitcast.5), custom_call_target="tpu_custom_call" | custom-call | flops 1358954496 | bytes 5638400 | tf_op jit(solution)/shard_map/pallas_call | solution.py:63
  24.6 0.0 copy-start.3
  24.6 1.0 %copy-done.3 = f32[1152,256]{1,0:T(8,128)} copy-done((f32[1152,256]{1,0:T(8,128)}, f32[1152,256]{1,0:T(8,128)S(1)}, u32[]{:S(2)}) %copy-start.3) | copy-done | bytes 1179672
  25.6 0.0 copy-start.7
  25.6 0.8 copy-done.7
  26.4 0.0 copy-start.9
  26.4 0.0 copy-done.1
  26.4 2.2 %shard_map.108 = (bf16[1152,1152]{1,0:T(8,128)(2,1)S(1)}, f32[1152,256]{1,0:T(8,128)S(1)}, f32[2,1152,128]{2,1,0:T(8,128)S(1)}) custom-call(bf16[2,1152,256]{2,1,0:T(8,128)(2,1)S(1)} %copy-done.1, bf16[1152,1152]{1,0:T(8,128)(2,1)S(1)} %copy-done.2, f32[32,256]{1,0:T(8,128)} %refs_2_.7, f32[1,256]{1,0:T(1,128)S(1)} %get-tuple-element.36.refs_3_, ...), custom_call_target="tpu_custom_call" | custom-call | flops 679477248 | bytes 8890368 | tf_op jit(solution)/shard_map/pallas_call | solution.py:63
  28.7 0.0 copy-done.9
  28.7 0.0 copy-start.4
  28.7 1.0 %copy-done.4 = f32[2,1152,128]{2,1,0:T(8,128)} copy-done((f32[2,1152,128]{2,1,0:T(8,128)}, f32[2,1152,128]{2,1,0:T(8,128)S(1)}, u32[]{:S(2)}) %copy-start.4) | copy-done | bytes 1179672
  29.7 0.0 copy-start.6
  29.7 1.0 %copy-done.6 = f32[1152,256]{1,0:T(8,128)} copy-done((f32[1152,256]{1,0:T(8,128)}, f32[1152,256]{1,0:T(8,128)S(1)}, u32[]{:S(2)}) %copy-start.6) | copy-done | bytes 1179672
  30.7 2.7 %all-to-all-done.refs_0_ = bf16[32,72,128]{2,1,0:T(8,128)(2,1)S(1)} async-done(((bf16[32,72,128]{2,1,0:T(8,128)(2,1)}), bf16[32,72,128]{2,1,0:T(8,128)(2,1)S(1)}, u32[]{:S(2)}, u32[]{:S(2)}) %all-to-all-start) | async-done | bytes 589856 | tf_op jit(solution)/shard_map/all_to_all | solution.py:461
  33.4 0.0 copy-start.5
  33.4 3.7 %shard_map.109 = (bf16[1152,128]{1,0:T(8,128)(2,1)S(1)}, bf16[1152,128]{1,0:T(8,128)(2,1)S(1)}, bf16[16,1152]{1,0:T(8,128)(2,1)S(1)}, f32[8,256]{1,0:T(8,128)S(1)}) custom-call(bf16[32,72,128]{2,1,0:T(8,128)(2,1)S(1)} %all-to-all-done.refs_0_, bf16[1152,1152]{1,0:T(8,128)(2,1)S(1)} %get-tuple-element.37.refs_1_, f32[32,256]{1,0:T(8,128)} %refs_2_.7, ...), custom_call_target="tpu_custom_call" | custom-call | flops 1358954496 | bytes 6304768 | tf_op jit(solution)/shard_map/pallas_call | solution.py:63
  37.1 0.0 copy-start.8
  37.2 1.4 %collective-permute-start.2 = (bf16[1152,128]{1,0:T(8,128)(2,1)S(1)}, bf16[1152,128]{1,0:T(8,128)(2,1)S(1)}, u32[]{:S(2)}, u32[]{:S(2)}) collective-permute-start(bf16[1152,128]{1,0:T(8,128)(2,1)S(1)} %get-tuple-element.39.refs_0_), channel_id=1, source_target_pairs={{1,0},{2,1},{3,2},{4,3},{5,4},{6,5},{7,6},{8,7},{9,8},{10,9},{11,1... | collective-permute-start | bytes 884744 | tf_op jit(solution)/shard_map/ppermute | solution.py:503
  38.6 4.0 %collective-permute-start.3 = (bf16[1152,128]{1,0:T(8,128)(2,1)S(1)}, bf16[1152,128]{1,0:T(8,128)(2,1)S(1)}, u32[]{:S(2)}, u32[]{:S(2)}) collective-permute-start(bf16[1152,128]{1,0:T(8,128)(2,1)S(1)} %get-tuple-element.40.refs_1_), channel_id=1, source_target_pairs={{0,1},{1,2},{2,3},{3,4},{4,5},{5,6},{6,7},{7,8},{8,9},{9,10},{10,1... | collective-permute-start | bytes 884744 | tf_op jit(solution)/shard_map/ppermute | solution.py:504
  42.6 6.1 %collective-permute-start.4 = (bf16[16,1152]{1,0:T(8,128)(2,1)S(1)}, bf16[16,1152]{1,0:T(8,128)(2,1)S(1)}, u32[]{:S(2)}, u32[]{:S(2)}) collective-permute-start(bf16[16,1152]{1,0:T(8,128)(2,1)S(1)} %get-tuple-element.46), channel_id=1, source_target_pairs={{0,32},{32,64},{64,96},{96,128},{128,160},{160,192},{192,224},{224... | collective-permute-start | bytes 110600 | tf_op jit(solution)/shard_map/ppermute | solution.py:505
  48.7 1.6 %collective-permute-start.5 = (bf16[16,1152]{1,0:T(8,128)(2,1)S(1)}, bf16[16,1152]{1,0:T(8,128)(2,1)S(1)}, u32[]{:S(2)}, u32[]{:S(2)}) collective-permute-start(bf16[16,1152]{1,0:T(8,128)(2,1)S(1)} %get-tuple-element.46), channel_id=1, source_target_pairs={{32,0},{64,32},{96,64},{128,96},{160,128},{192,160},{224,192},{256... | collective-permute-start | bytes 110600 | tf_op jit(solution)/shard_map/ppermute | solution.py:506
  50.4 0.0 copy-done.5
  50.4 0.7 shard_map.110
  51.1 0.0 collective-permute-done.4.refs_6_
  51.1 1.3 %collective-permute-done.5.refs_7_ = bf16[16,1152]{1,0:T(8,128)(2,1)S(1)} collective-permute-done((bf16[16,1152]{1,0:T(8,128)(2,1)S(1)}, bf16[16,1152]{1,0:T(8,128)(2,1)S(1)}, u32[]{:S(2)}, u32[]{:S(2)}) %collective-permute-start.5) | collective-permute-done | bytes 36896 | tf_op jit(solution)/shard_map/ppermute | solution.py:506
  52.4 0.0 collective-permute-done.2.refs_4_
  52.4 0.0 collective-permute-done.3.refs_5_
  52.4 0.0 copy-done.8
  52.4 1.1 %shard_map.111 = (bf16[1152,256]{1,0:T(8,128)(2,1)S(1)}, f32[32,1,128]{2,1,0:T(1,128)S(1)}) custom-call(f32[1152,256]{1,0:T(8,128)S(1)} %get-tuple-element.42.refs_0_, f32[1152,128]{1,0:T(8,128)S(1)} %get-tuple-element.43.refs_1_, f32[1152,128]{1,0:T(8,128)S(1)} %get-tuple-element.44.refs_2_, f32[1152,128]{1,0:T(8,128)S(1)} %get-tuple-element.45.refs_3_, ...), custom_call_target="tpu_custom_call" | custom-call | bytes 4817920 | tf_op jit(solution)/shard_map/pallas_call | solution.py:63
  53.5 15.6 %all_to_all.15.refs_0_ = f32[32,1,128]{2,1,0:T(1,128)S(1)} all-to-all(f32[32,1,128]{2,1,0:T(1,128)S(1)} %get-tuple-element.49), channel_id=1, replica_groups=mesh['geo'=16,'freq'=32] {'freq'}, dimensions={0} | all-to-all | bytes 32768 | tf_op jit(solution)/shard_map/all_to_all | solution.py:518
  69.1 0.6 shard_map.113
  69.7 16.5 %all-to-all-start.2 = ((f32[16,1,128]{2,1,0:T(1,128)}), f32[16,1,128]{2,1,0:T(1,128)S(1)}, u32[]{:S(2)}, u32[]{:S(2)}) async-start(f32[16,1,128]{2,1,0:T(1,128)} %shard_map.113), calls=%async_computation.2 | async-start | bytes 16384 | tf_op jit(solution)/shard_map/all_to_all | solution.py:531
  86.3 4.0 %shard_map.112 = bf16[1152,256]{1,0:T(8,128)(2,1)} custom-call(bf16[1152,256]{1,0:T(8,128)(2,1)S(1)} %get-tuple-element.51.refs_0_, bf16[1152,1152]{1,0:T(8,128)(2,1)S(1)} %get-tuple-element.37.refs_1_, f32[32,256]{1,0:T(8,128)} %refs_2_.7, f32[1,256]{1,0:T(1,128)} %copy-done.9, f32[1152,256]{1,0:T(8,128)} %copy-done.3, bf16[2,1152,256]{2,1,0:T(8,128)(2,1)} %refs_5_.3), custom_call_target="tpu_custom_call" | custom-call | flops 1358954496 | bytes 6226944 | tf_op jit(solution)/shard_map/pallas_call | solution.py:63
  90.3 3.1 %all-to-all-done.2.refs_0_ = f32[16,1,128]{2,1,0:T(1,128)S(1)} async-done(((f32[16,1,128]{2,1,0:T(1,128)}), f32[16,1,128]{2,1,0:T(1,128)S(1)}, u32[]{:S(2)}, u32[]{:S(2)}) %all-to-all-start.2) | async-done | bytes 8224 | tf_op jit(solution)/shard_map/all_to_all | solution.py:531
  93.3 0.5 shard_map.114
Async XLA Ops:
  2.2 7.6 %collective-permute-start = (bf16[8,2304]{1,0:T(8,128)(2,1)S(1)}, bf16[8,2304]{1,0:T(8,128)(2,1)S(1)}, u32[]{:S(2)}, u32[]{:S(2)}) collective-permute-start(bf16[8,2304]{1,0:T(8,128)(2,1)S(1)} %get-tuple-element.32), channel_id=1, source_target_pairs={{0,32},{32,64},{64,96},{96,128},{128,160},{160,192},{192,224},{224... | collective-permute-start | bytes 110600 | tf_op jit(solution)/shard_map/ppermute | solution.py:446
  5.7 4.3 %collective-permute-start.1 = (bf16[8,2304]{1,0:T(8,128)(2,1)S(1)}, bf16[8,2304]{1,0:T(8,128)(2,1)S(1)}, u32[]{:S(2)}, u32[]{:S(2)}) collective-permute-start(bf16[8,2304]{1,0:T(8,128)(2,1)S(1)} %get-tuple-element.33), channel_id=1, source_target_pairs={{32,0},{64,32},{96,64},{128,96},{160,128},{192,160},{224,192},{256... | collective-permute-start | bytes 110600 | tf_op jit(solution)/shard_map/ppermute | solution.py:447
  10.0 9.9 %copy-start = (bf16[2,1152,256]{2,1,0:T(8,128)(2,1)S(1)}, bf16[2,1152,256]{2,1,0:T(8,128)(2,1)}, u32[]{:S(2)}) copy-start(bf16[2,1152,256]{2,1,0:T(8,128)(2,1)} %refs_5_.3) | copy-start | bytes 3538948
  11.2 22.3 %all-to-all-start = ((bf16[32,72,128]{2,1,0:T(8,128)(2,1)}), bf16[32,72,128]{2,1,0:T(8,128)(2,1)S(1)}, u32[]{:S(2)}, u32[]{:S(2)}) async-start(bf16[32,72,128]{2,1,0:T(8,128)(2,1)} %shard_map.106), calls=%async_computation | async-start | bytes 1179648 | tf_op jit(solution)/shard_map/all_to_all | solution.py:461
  20.0 1.8 %copy-start.2 = (bf16[1152,1152]{1,0:T(8,128)(2,1)S(1)}, bf16[1152,1152]{1,0:T(8,128)(2,1)}, u32[]{:S(2)}) copy-start(bf16[1152,1152]{1,0:T(8,128)(2,1)} %refs_1_.5) | copy-start | bytes 7962628
  21.7 4.7 %copy-start.1 = (bf16[2,1152,256]{2,1,0:T(8,128)(2,1)S(1)}, bf16[2,1152,256]{2,1,0:T(8,128)(2,1)}, u32[]{:S(2)}) copy-start(bf16[2,1152,256]{2,1,0:T(8,128)(2,1)} %refs_5_.3) | copy-start | bytes 3538948
  24.6 1.1 %copy-start.3 = (f32[1152,256]{1,0:T(8,128)}, f32[1152,256]{1,0:T(8,128)S(1)}, u32[]{:S(2)}) copy-start(f32[1152,256]{1,0:T(8,128)S(1)} %get-tuple-element.52.refs_4_) | copy-start | bytes 3538948
  25.6 0.8 copy-start.7
  26.4 2.2 %copy-start.9 = (f32[1,256]{1,0:T(1,128)}, f32[1,256]{1,0:T(1,128)S(1)}, u32[]{:S(2)}) copy-start(f32[1,256]{1,0:T(1,128)S(1)} %get-tuple-element.36.refs_3_) | copy-start | bytes 3076
  28.7 1.0 %copy-start.4 = (f32[2,1152,128]{2,1,0:T(8,128)}, f32[2,1152,128]{2,1,0:T(8,128)S(1)}, u32[]{:S(2)}) copy-start(f32[2,1152,128]{2,1,0:T(8,128)S(1)} %get-tuple-element.41.refs_2_) | copy-start | bytes 3538948
  29.7 1.0 %copy-start.6 = (f32[1152,256]{1,0:T(8,128)}, f32[1152,256]{1,0:T(8,128)S(1)}, u32[]{:S(2)}) copy-start(f32[1152,256]{1,0:T(8,128)S(1)} %get-tuple-element.38.refs_5_) | copy-start | bytes 3538948
  33.4 16.9 %copy-start.5 = (f32[2,1152,128]{2,1,0:T(8,128)S(1)}, f32[2,1152,128]{2,1,0:T(8,128)}, u32[]{:S(2)}) copy-start(f32[2,1152,128]{2,1,0:T(8,128)} %copy-done.4) | copy-start | bytes 3538948
  37.1 15.3 %copy-start.8 = (bf16[1152,256]{1,0:T(8,128)(2,1)S(1)}, bf16[1152,256]{1,0:T(8,128)(2,1)}, u32[]{:S(2)}) copy-start(bf16[1152,256]{1,0:T(8,128)(2,1)} %copy-done.7) | copy-start | bytes 1769476
  37.2 15.2 %collective-permute-start.2 = (bf16[1152,128]{1,0:T(8,128)(2,1)S(1)}, bf16[1152,128]{1,0:T(8,128)(2,1)S(1)}, u32[]{:S(2)}, u32[]{:S(2)}) collective-permute-start(bf16[1152,128]{1,0:T(8,128)(2,1)S(1)} %get-tuple-element.39.refs_0_), channel_id=1, source_target_pairs={{1,0},{2,1},{3,2},{4,3},{5,4},{6,5},{7,6},{8,7},{9,8},{10,9},{11,1... | collective-permute-start | bytes 884744 | tf_op jit(solution)/shard_map/ppermute | solution.py:503
  38.6 13.8 %collective-permute-start.3 = (bf16[1152,128]{1,0:T(8,128)(2,1)S(1)}, bf16[1152,128]{1,0:T(8,128)(2,1)S(1)}, u32[]{:S(2)}, u32[]{:S(2)}) collective-permute-start(bf16[1152,128]{1,0:T(8,128)(2,1)S(1)} %get-tuple-element.40.refs_1_), channel_id=1, source_target_pairs={{0,1},{1,2},{2,3},{3,4},{4,5},{5,6},{6,7},{7,8},{8,9},{9,10},{10,1... | collective-permute-start | bytes 884744 | tf_op jit(solution)/shard_map/ppermute | solution.py:504
  42.6 8.5 %collective-permute-start.4 = (bf16[16,1152]{1,0:T(8,128)(2,1)S(1)}, bf16[16,1152]{1,0:T(8,128)(2,1)S(1)}, u32[]{:S(2)}, u32[]{:S(2)}) collective-permute-start(bf16[16,1152]{1,0:T(8,128)(2,1)S(1)} %get-tuple-element.46), channel_id=1, source_target_pairs={{0,32},{32,64},{64,96},{96,128},{128,160},{160,192},{192,224},{224... | collective-permute-start | bytes 110600 | tf_op jit(solution)/shard_map/ppermute | solution.py:505
  48.7 3.7 %collective-permute-start.5 = (bf16[16,1152]{1,0:T(8,128)(2,1)S(1)}, bf16[16,1152]{1,0:T(8,128)(2,1)S(1)}, u32[]{:S(2)}, u32[]{:S(2)}) collective-permute-start(bf16[16,1152]{1,0:T(8,128)(2,1)S(1)} %get-tuple-element.46), channel_id=1, source_target_pairs={{32,0},{64,32},{96,64},{128,96},{160,128},{192,160},{224,192},{256... | collective-permute-start | bytes 110600 | tf_op jit(solution)/shard_map/ppermute | solution.py:506
  69.7 23.6 %all-to-all-start.2 = ((f32[16,1,128]{2,1,0:T(1,128)}), f32[16,1,128]{2,1,0:T(1,128)S(1)}, u32[]{:S(2)}, u32[]{:S(2)}) async-start(f32[16,1,128]{2,1,0:T(1,128)} %shard_map.113), calls=%async_computation.2 | async-start | bytes 16384 | tf_op jit(solution)/shard_map/all_to_all | solution.py:531
